TPU v7x, 128 devices: a whole 4x4x4 slice. The times are simulated.
128 devices in a mesh: dp: 16 (over y, z), tensor: 8 (over x, core).
Axes of the slice: x: 4, y: 4, z: 4, core: 2. Of those that a mesh axis runs over, the one named last changes fastest.
Arguments:
- hidden_in: bfloat16 [16384, 2560], P('dp'), may hold values from -6 to 6
- ln_gain: float32 [2560], replicated, may hold values from 0.5 to 1.5
- attn_probs: bfloat16 [32, 24, 512, 512], P('dp', 'tensor'), may hold values from 9.727478e-05 to 0.009765625
- w_value: bfloat16 [2560, 3072], P(None, 'tensor'), may hold values from -0.5 to 0.5
- w_out: bfloat16 [3072, 2560], P('tensor'), may hold values from -0.109375 to 0.109375
- out_grad: bfloat16 [16384, 2560], P('dp'), may hold values from -6 to 6
- err_out: float32 [16, 3072, 2560], P('dp', 'tensor'), may hold values from -6 to 6
- err_value: float32 [16, 3072, 2560], P('dp', 'tensor'), may hold values from -6 to 6
- factor_codes: int32 [2], replicated, may hold values from 0 to 999999
Outputs:
- in_grad: bfloat16 [16384, 2560], P(('dp', 'tensor'))
- gain_grad: float32 [2560], replicated
- new_err_out: float32 [16, 3072, 2560], P('dp', 'tensor')
- new_err_value: float32 [16, 3072, 2560], P('dp', 'tensor')
- left_out: float32 [3072, 32], P('tensor')
- left_value: float32 [3072, 32], P('tensor')
- right_out: float32 [2560, 32], P('tensor')
- right_value: float32 [2560, 32], P('tensor')
All inputs are finite; a program needn't handle non-finite values.
Results may differ from a plain program's by a relative error of at most 0.022.
Values may be sent and summed in bfloat16 or wider, within the bound.
No kernel may reach another device: no remote copies, remote signals or barrier semaphores. Data moves between devices by JAX's collectives and lax.ppermute only.
A program may use at most 192 MiB of HBM per device.

v0:
```python
import math

import jax
import jax.numpy as jnp
from jax import lax
from jax.sharding import PartitionSpec as P

D = 2560
HEADS = 24
HEAD_DIM = 128
RANK = 32


def layer_stats(hidden, gain):
    widened = hidden.astype(jnp.float32)
    row_mean = jnp.mean(widened, axis=-1, keepdims=True)
    centred = widened - row_mean
    inv_std = lax.rsqrt(jnp.mean(centred * centred, axis=-1, keepdims=True) + 1e-05)
    standard = centred * inv_std
    return (standard, inv_std, (standard * gain).astype(jnp.bfloat16))


def norm_back(branch_grad, standard, inv_std, gain):
    scaled = branch_grad * gain
    first_mean = jnp.mean(scaled, axis=-1, keepdims=True)
    second_mean = jnp.mean(scaled * standard, axis=-1, keepdims=True)
    result = inv_std * (scaled - first_mean - standard * second_mean)
    return (result.astype(jnp.bfloat16), jnp.sum(branch_grad * standard, axis=0))


def make_start(code):
    row_ids = lax.broadcasted_iota(jnp.int32, (D, RANK), 0)
    col_ids = lax.broadcasted_iota(jnp.int32, (D, RANK), 1)
    hashed = row_ids * 40503 + col_ids * 1531 + code * 7919
    hashed = jnp.bitwise_xor(hashed, jnp.right_shift(hashed, 15)) * 668265261
    hashed = jnp.bitwise_xor(hashed, jnp.right_shift(hashed, 15)) * 374761393
    hashed = jnp.bitwise_xor(hashed, jnp.right_shift(hashed, 13))
    level = jnp.bitwise_and(hashed, 8388607).astype(jnp.float32)
    return ((level + 0.5) / 8388608.0 - 0.5) * math.sqrt(12.0)


def precise_dot(left_side, right_side):
    return jnp.dot(left_side, right_side, precision=lax.Precision.HIGHEST)


def orthonormal(left, gram):
    factor = jnp.linalg.cholesky(gram)
    return lax.linalg.triangular_solve(factor, left, left_side=False, lower=True, transpose_a=True)


def finish(matrix, ortho, right):
    fresh = (matrix - precise_dot(ortho, right.T))[None]
    share_rows = right.shape[0] // lax.axis_size("tensor")
    right_share = lax.dynamic_slice_in_dim(
        right, lax.axis_index("tensor") * share_rows, share_rows, 0
    )
    return (fresh, ortho * math.sqrt(HEADS * HEAD_DIM), right_share)


def compress_apart(matrix, start, worker_count):
    left = (
        lax.psum(precise_dot(matrix, start).astype(jnp.bfloat16), "dp").astype(jnp.float32)
        / worker_count
    )
    gram = lax.psum(precise_dot(left.T, left), "tensor")
    ortho = orthonormal(left, gram)
    right = lax.psum(precise_dot(matrix.T, ortho), ("dp", "tensor")) / worker_count
    return finish(matrix, ortho, right)


def local(
    hidden_in, ln_gain, attn_probs, w_value, w_out, out_grad, err_out, err_value, factor_codes
):
    tok_rows = hidden_in.shape[0]
    seq_count = attn_probs.shape[0]
    head_count = attn_probs.shape[1]
    length = attn_probs.shape[2]
    standard, inv_std, normed = layer_stats(hidden_in, ln_gain)
    values = jnp.dot(normed, w_value, preferred_element_type=jnp.float32).astype(jnp.bfloat16)
    shaped = values.reshape(seq_count, length, head_count, -1)
    mixed = jnp.einsum("shqk,skhd->sqhd", attn_probs, shaped, preferred_element_type=jnp.float32)
    mixed = mixed.astype(jnp.bfloat16).reshape(tok_rows, -1)
    grad_out = lax.dot_general(
        mixed, out_grad, (((0,), (0,)), ((), ())), preferred_element_type=jnp.float32
    )
    d_mixed = lax.dot_general(
        out_grad, w_out, (((1,), (1,)), ((), ())), preferred_element_type=jnp.float32
    )
    d_mixed = d_mixed.astype(jnp.bfloat16).reshape(seq_count, length, head_count, -1)
    d_values = jnp.einsum(
        "shqk,sqhd->skhd", attn_probs, d_mixed, preferred_element_type=jnp.float32
    )
    d_values = d_values.astype(jnp.bfloat16).reshape(tok_rows, -1)
    grad_value = lax.dot_general(
        d_values, normed, (((0,), (0,)), ((), ())), preferred_element_type=jnp.float32
    )
    partial_grad = lax.dot_general(
        d_values, w_value, (((1,), (1,)), ((), ())), preferred_element_type=jnp.float32
    )
    shard_rows = tok_rows // lax.axis_size("tensor")
    first_row = lax.axis_index("tensor") * shard_rows
    total = lax.psum(partial_grad.astype(jnp.bfloat16), "tensor").astype(jnp.float32)
    whole_grad, gain_part = norm_back(total, standard, inv_std, ln_gain)
    in_grad = lax.dynamic_slice_in_dim(whole_grad, first_row, shard_rows, 0)
    gain_grad = lax.psum(gain_part, "dp")
    matrix_out = grad_out + err_out[0]
    matrix_value = grad_value + err_value[0]
    start_out = make_start(factor_codes[0])
    start_value = make_start(factor_codes[1])
    worker_count = lax.axis_size("dp")
    result_out = compress_apart(matrix_out, start_out, worker_count)
    result_value = compress_apart(matrix_value, start_value, worker_count)
    return (
        in_grad,
        gain_grad,
        result_out[0],
        result_value[0],
        result_out[1],
        result_value[1],
        result_out[2],
        result_value[2],
    )


def solution(mesh):
    in_specs = (
        P("dp", None),
        P(),
        P("dp", "tensor", None, None),
        P(None, "tensor"),
        P("tensor", None),
        P("dp", None),
        P("dp", "tensor", None),
        P("dp", "tensor", None),
        P(),
    )
    out_specs = (
        P(("dp", "tensor"), None),
        P(),
        P("dp", "tensor", None),
        P("dp", "tensor", None),
        P("tensor", None),
        P("tensor", None),
        P("tensor", None),
        P("tensor", None),
    )
    return jax.shard_map(local, mesh=mesh, in_specs=in_specs, out_specs=out_specs, check_vma=False)
```

profile of v0, /device:TPU:0, one launch (start us, length us, event | category | flops | bytes accessed | tf_op | source)
XLA Modules:
  0.0 498.0 jit_solution(16147864590115914208)
XLA Ops:
  7.3 7.0 %convolution_convert_fusion.3 = bf16[1024,384]{1,0:T(8,128)(2,1)} fusion(bf16[1024,2560]{1,0:T(8,128)(2,1)} %param.17, bf16[384,2560]{1,0:T(8,128)(2,1)} %param.16), kind=kOutput, calls=%fused_computation.22 | convolution fusion | flops 2013659136 | bytes 7995392 | tf_op jit(solution)/shard_map/dot_general | solution.py:86
  14.3 3.2 reshape.74
  21.2 3.8 convert_reduce_fusion
  25.0 4.1 fusion.2
  29.2 3.9 fusion.8
  33.1 3.7 reshape.75
  42.6 4.9 convolution_add_fusion.1
  47.5 2.7 convolution_add_fusion
  50.2 3.8 convolution_convert_fusion.5
  54.1 3.8 convolution_convert_fusion.4
  57.8 76.4 %all-reduce.2 = (bf16[384,32]{0,1:T(8,128)(2,1)S(1)}, bf16[384,32]{0,1:T(8,128)(2,1)S(1)}) all-reduce(bf16[384,32]{0,1:T(8,128)(2,1)S(1)} %convolution_convert_fusion.5, bf16[384,32]{0,1:T(8,128)(2,1)S(1)} %convolution_convert_fusion.4), channel_id=1, replica_groups=mesh['dp'=16,'tensor'=8] {'dp'}, use_global_device_ids=true, to_apply=%region_7.0 | all-reduce | flops 24576 | bytes 98304 | tf_op jit(solution)/shard_map/psum | solution.py:62
  134.6 23.6 %all-reduce.1 = (f32[32,32]{0,1:T(8,128)S(1)}, f32[32,32]{0,1:T(8,128)S(1)}) all-reduce(f32[32,32]{0,1:T(8,128)S(1)} %fusion.59, f32[32,32]{0,1:T(8,128)S(1)} %fusion.58), channel_id=1, replica_groups=mesh['dp'=16,'tensor'=8] {'tensor'}, use_global_device_ids=true, to_apply=%region_8.0 | all-reduce | flops 2048 | bytes 16384 | tf_op jit(solution)/shard_map/psum | solution.py:65
  158.4 2.9 cholesky.44
  166.0 5.4 %fusion.95 = f32[2560,32]{0,1:T(8,128)} fusion(f32[384,2560]{1,0:T(8,128)} %copy-done.4, f32[384,32]{0,1:T(8,128)S(1)} %get-tuple-element.24), kind=kOutput, calls=%fused_computation.143 | convolution fusion | flops 377487360 | bytes 4308992 | tf_op jit(solution)/shard_map/dot_general | solution.py:43
  171.4 2.9 cholesky.55
  179.0 5.2 %fusion.96 = f32[2560,32]{0,1:T(8,128)} fusion(f32[384,2560]{1,0:T(8,128)} %copy-done.2, f32[384,32]{0,1:T(8,128)S(1)} %get-tuple-element.26), kind=kOutput, calls=%fused_computation.144 | convolution fusion | flops 377487360 | bytes 4308992 | tf_op jit(solution)/shard_map/dot_general | solution.py:43
  184.3 4.9 convolution_convert_fusion
  189.3 133.6 %all-reduce.8.cloned.1.call-done = (f32[2560,32]{0,1:T(8,128)}, f32[2560,32]{0,1:T(8,128)}) async-done(((f32[2560,32]{0,1:T(8,128)}, f32[2560,32]{0,1:T(8,128)}), (f32[2560,32]{0,1:T(8,128)}, f32[2560,32]{0,1:T(8,128)})) %all-reduce.8.cloned.1.call-update) | async-done | bytes 655376 | tf_op jit(solution)/shard_map/psum | solution.py:67
  326.3 7.6 %fusion.4 = f32[1,384,2560]{2,1,0:T(8,128)} fusion(f32[384,2560]{1,0:T(8,128)} %copy-done.4, f32[384,32]{0,1:T(8,128)S(1)} %get-tuple-element.24, f32[2560,32]{0,1:T(8,128)} %get-tuple-element.13), kind=kOutput, calls=%fused_computation.13 | convolution fusion | flops 378552320 | bytes 8241152 | tf_op jit(solution)/shard_map/dot_general | solution.py:43
  333.9 5.3 %fusion.5 = f32[1,384,2560]{2,1,0:T(8,128)} fusion(f32[384,2560]{1,0:T(8,128)S(1)} %copy-done.3, f32[384,32]{0,1:T(8,128)S(1)} %get-tuple-element.26, f32[2560,32]{0,1:T(8,128)S(1)} %copy-done.5), kind=kOutput, calls=%fused_computation.14 | convolution fusion | flops 378552320 | bytes 8241152 | tf_op jit(solution)/shard_map/dot_general | solution.py:43
  339.1 61.3 %all-reduce.6.cloned.1.call-done = bf16[1024,2560]{1,0:T(8,128)(2,1)} async-done(((bf16[1024,2560]{1,0:T(8,128)(2,1)}), bf16[1024,2560]{1,0:T(8,128)(2,1)}) %all-reduce.6.cloned.1.call-update) | async-done | bytes 5242896 | tf_op jit(solution)/shard_map/psum | solution.py:102
  400.5 13.0 %fusion.3 = (f32[2560]{0:T(1024)S(1)}, f32[1024]{0:T(1024)S(1)}, f32[1024]{0:T(1024)S(1)}, f32[1024,2560]{1,0:T(8,128)}, f32[1024,2560]{1,0:T(8,128)}) fusion(bf16[1024,2560]{1,0:T(8,128)(2,1)} %all-reduce.6.cloned.1.call-done, f32[1024]{0:T(1024)S(1)} %add_rsqrt_fusion, f32[1024]{0:T(1024)S(1)} %broadcast_multiply_fusion.6, bf16[1024,2560]{1,0:T(8,128)(2,1)} %param.12, ...), kind=kLoop, calls=%fused_computation.7 | loop fusion | flops 26209792 | bytes 31494144 | tf_op jit(solution)/shard_map/reduce_sum | solution.py:28
  413.6 74.5 %psum.57 = f32[2560]{0:T(1024)} all-reduce(f32[2560]{0:T(1024)S(1)} %get-tuple-element.10), channel_id=1, replica_groups=mesh['dp'=16,'tensor'=8] {'dp'}, use_global_device_ids=true, to_apply=%region_6.0 | all-reduce | flops 2560 | bytes 20480 | tf_op jit(solution)/shard_map/psum | solution.py:105
  488.1 2.9 fusion.11
  (74 shorter events, 21.5 us)
Async XLA Ops:
  7.2 10.3 %copy-start = (bf16[2,3,512,512]{3,2,1,0:T(8,128)(2,1)S(1)}, bf16[2,3,512,512]{3,2,1,0:T(8,128)(2,1)}, u32[]{:S(2)}) copy-start(bf16[2,3,512,512]{3,2,1,0:T(8,128)(2,1)} %param.14) | copy-start | bytes 9437188
  7.2 315.7 %all-reduce.8.cloned.1.call-start = ((), (), s32[]{:S(2)}) async-start(), calls=%async_computation.1 | async-start | bytes 1310720 | tf_op jit(solution)/shard_map/psum | solution.py:67
  20.2 9.0 %slice-start = ((s8[5242880]{0:T(1024)(128)(4,1)}), s8[4194304]{0:T(1024)(128)(4,1)S(1)}, s32[]{:S(2)}) async-start(s8[5242880]{0:T(1024)(128)(4,1)} %bitcast.68), calls=%async_computation.2 | async-start | bytes 8388608
  21.2 7.9 %slice-start.1 = ((s8[5242880]{0:T(1024)(128)(4,1)}), s8[1048576]{0:T(1024)(128)(4,1)S(1)}, s32[]{:S(2)}) async-start(s8[5242880]{0:T(1024)(128)(4,1)} %bitcast.68), calls=%async_computation.3 | async-start | bytes 2097152
  25.0 4.2 copy-start.7
  25.0 4.2 copy-start.11
  36.8 3.5 copy-start.8
  36.8 5.8 %copy-start.9 = (f32[1,384,2560]{2,1,0:T(8,128)S(1)}, f32[1,384,2560]{2,1,0:T(8,128)}, u32[]{:S(2)}) copy-start(f32[1,384,2560]{2,1,0:T(8,128)} %param.18) | copy-start | bytes 11796484
  40.2 7.3 %slice-start.2 = ((s8[5242880]{0:T(1024)(128)(4,1)}), s8[4194304]{0:T(1024)(128)(4,1)S(1)}, s32[]{:S(2)}) async-start(s8[5242880]{0:T(1024)(128)(4,1)} %bitcast.70), calls=%async_computation.4 | async-start | bytes 8388608
  42.6 4.9 slice-start.3
  42.6 4.9 copy-start.6
  42.6 4.9 copy-start.10
  47.5 2.8 copy-start.4
  50.2 3.8 copy-start.2
  166.0 18.2 %copy-start.12 = (bf16[2560,384]{1,0:T(8,128)(2,1)S(1)}, bf16[2560,384]{1,0:T(8,128)(2,1)}, u32[]{:S(2)}) copy-start(bf16[2560,384]{1,0:T(8,128)(2,1)} %param.15) | copy-start | bytes 5898244
  184.2 216.3 %all-reduce.6.cloned.1.call-start = ((), (), s32[]{:S(2)}) async-start(), calls=%async_computation | async-start | bytes 10485760 | tf_op jit(solution)/shard_map/psum | solution.py:102
  326.3 7.6 %copy-start.3 = (f32[384,2560]{1,0:T(8,128)S(1)}, f32[384,2560]{1,0:T(8,128)}, u32[]{:S(2)}) copy-start(f32[384,2560]{1,0:T(8,128)} %copy-done.2) | copy-start | bytes 11796484
  326.3 7.6 %copy-start.5 = (f32[2560,32]{0,1:T(8,128)S(1)}, f32[2560,32]{0,1:T(8,128)}, u32[]{:S(2)}) copy-start(f32[2560,32]{0,1:T(8,128)} %get-tuple-element.14) | copy-start | bytes 983044
  400.5 90.5 %copy-start.1 = (bf16[2,3,512,512]{3,2,1,0:T(8,128)(2,1)S(1)}, bf16[2,3,512,512]{3,2,1,0:T(8,128)(2,1)}, u32[]{:S(2)}) copy-start(bf16[2,3,512,512]{3,2,1,0:T(8,128)(2,1)} %param.14) | copy-start | bytes 9437188
Sparse Core Ops, SparseCore 0:
  184.3 138.5 all-reduce.7
  325.2 75.1 all-reduce.5
where the time goes:
time: 505 us; the launch traced here: 498 us
  waiting for transfers between devices  195 us (39%)
  blocking collectives  175 us (35%)
  matrix products  60.9 us (12%)
  other arithmetic  39.1 us (8%)
  between operations  16.3 us (3%)
  local copies, waits for them, and re-layouts  12.2 us (2%)
    psum x1, waiting for transfers between devices, compress_apart(): lax.psum(precise_dot(matrix.T, ortho), ('dp', 'tensor')) / worker_count  134 us
    psum x1, blocking collectives, compress_apart(): lax.psum(precise_dot(matrix, start).astype(jnp.bfloat16), 'dp')  76.4 us
    psum x1, blocking collectives, local(): gain_grad = lax.psum(gain_part, 'dp')  74.5 us
    psum x1, waiting for transfers between devices, local(): lax.psum(partial_grad.astype(jnp.bfloat16), 'tensor').astype(jnp.float32)  61.3 us
    dot_general x8, matrix products, precise_dot(): return jnp.dot(left_side, right_side, precision=lax.Precision.HIGHEST)  31.4 us
    psum x1, blocking collectives, compress_apart(): gram = lax.psum(precise_dot(left.T, left), 'tensor')  23.6 us
    reduce_sum x1, other arithmetic, norm_back(): jnp.sum(branch_grad * standard, axis=0)  13 us
  transfers between devices with their start and end apart: 2, of which 2 were waited for; matrix products, arithmetic and copies ran while one was open for 4% of the time, Pallas kernels for 0%

commit v1 on v0

v1 whole, which is shorter than its diff:
```python
import math

import jax
import jax.numpy as jnp
from jax import lax
from jax.experimental import pallas as pl
from jax.experimental.pallas import tpu as pltpu
from jax.sharding import PartitionSpec as P

D = 2560
RANK = 32
HEADS = 24
HEAD_DIM = 128
LEN = 512
CROPS = 2
HEADS_DEV = 3
TOK = CROPS * LEN
COLS = HEADS_DEV * HEAD_DIM
HH = HEADS * HEAD_DIM
TAIL = 128
WIDE = D + TAIL
TILE = 512
STEPS = D // TILE
WORKERS = 16
F32 = jnp.float32
BF16 = jnp.bfloat16
ANY = pl.BlockSpec(memory_space=pl.ANY)
SMEM = pl.BlockSpec(memory_space=pltpu.SMEM)


def dot(a, b, dims=((1,), (0,))):
    return lax.dot_general(a, b, (dims, ((), ())), preferred_element_type=F32)


def split2(a):
    high = a.astype(BF16)
    return high, (a - high.astype(F32)).astype(BF16)


def dot_split(a, b, dims=((1,), (0,))):
    a_high, a_low = split2(a)
    b_high, b_low = split2(b)
    return dot(a_high, b_high, dims) + (dot(a_low, b_high, dims) + dot(a_high, b_low, dims))


def lane_parts(value, group):
    high = value.astype(BF16).astype(F32)
    rest = value - high
    middle = rest.astype(BF16).astype(F32)
    low = rest - middle
    zero = jnp.zeros_like(value)
    return jnp.where(
        group == 0, high, jnp.where(group == 1, middle, jnp.where(group == 2, low, zero))
    ).astype(BF16)


def start_rows(code, first, rows):
    row_ids = lax.broadcasted_iota(jnp.int32, (rows, 128), 0) + first
    lane = lax.broadcasted_iota(jnp.int32, (rows, 128), 1)
    hashed = row_ids * 40503 + jnp.bitwise_and(lane, RANK - 1) * 1531 + code * 7919
    hashed = jnp.bitwise_xor(hashed, jnp.right_shift(hashed, 15)) * 668265261
    hashed = jnp.bitwise_xor(hashed, jnp.right_shift(hashed, 15)) * 374761393
    hashed = jnp.bitwise_xor(hashed, jnp.right_shift(hashed, 13))
    level = jnp.bitwise_and(hashed, 8388607).astype(F32)
    start = ((level + 0.5) / 8388608.0 - 0.5) * math.sqrt(12.0)
    return lane_parts(start, jnp.right_shift(lane, 5))


def all_groups(value):
    return (value + pltpu.roll(value, 64, 1)) + (pltpu.roll(value, 32, 1) + pltpu.roll(value, 96, 1))


def front_kernel(
    codes, gain, hidden, probs, w_value, w_out, out_grad, err_out, err_value,
    normed_out, mixed_t_out, d_values_t_out, left_out,
    hidden_v, probs_v, wv_ext, w_out_v, wo_ext, grad_v, err_out_v, err_value_v,
    normed_v, values_v, d_mixed_v, y_out, y_value, sems, out_sems,
):
    copies = [
        pltpu.make_async_copy(source, target, sems.at[index])
        for index, (source, target) in enumerate(
            (
                (w_out, w_out_v),
                (out_grad, grad_v),
                (hidden, hidden_v),
                (w_value, wv_ext.at[:, pl.ds(0, COLS)]),
                (probs, probs_v),
                (err_out.at[0], err_out_v),
                (err_value.at[0], err_value_v),
            )
        )
    ]
    for copy in copies:
        copy.start()

    @pl.loop(0, D // 128)
    def _(step):
        rows = pl.ds(pl.multiple_of(step * 128, 128), 128)
        wo_ext[rows, pl.ds(COLS, 128)] = start_rows(codes[0], step * 128, 128)
        wv_ext[rows, pl.ds(COLS, 128)] = start_rows(codes[1], step * 128, 128)

    copies[0].wait()

    @pl.loop(0, D // 256)
    def _(step):
        span = pl.ds(pl.multiple_of(step * 256, 256), 256)
        wo_ext[span, pl.ds(0, COLS)] = w_out_v[:, span].T

    copies[1].wait()

    @pl.loop(0, TOK // 256)
    def _(step):
        rows = pl.ds(pl.multiple_of(step * 256, 256), 256)
        product = dot(grad_v[rows, :], wo_ext[...])
        d_mixed_v[rows, :] = product[:, :COLS].astype(BF16)
        y_out[rows, :] = product[:, COLS:]

    copies[2].wait()

    def norm_rows(step, carry):
        rows = pl.ds(pl.multiple_of(step * 32, 32), 32)
        total = jnp.zeros((32, 128), F32)
        for part in range(D // 128):
            total = total + hidden_v[rows, pl.ds(part * 128, 128)].astype(F32)
        mean = jnp.sum(total, axis=1, keepdims=True) * (1.0 / D)
        total = jnp.zeros((32, 128), F32)
        for part in range(D // 128):
            centred = hidden_v[rows, pl.ds(part * 128, 128)].astype(F32) - mean
            total = total + centred * centred
        inv_std = lax.rsqrt(jnp.sum(total, axis=1, keepdims=True) * (1.0 / D) + 1e-05)
        for part in range(D // 128):
            lanes = pl.ds(part * 128, 128)
            centred = hidden_v[rows, lanes].astype(F32) - mean
            normed_v[rows, lanes] = (centred * inv_std * gain[:, lanes]).astype(BF16)
        return carry

    lax.fori_loop(0, TOK // 32, norm_rows, 0, unroll=4)
    normed_copy = pltpu.make_async_copy(normed_v, normed_out, out_sems.at[0])
    normed_copy.start()
    copies[3].wait()

    @pl.loop(0, TOK // 256)
    def _(step):
        rows = pl.ds(pl.multiple_of(step * 256, 256), 256)
        product = dot(normed_v[rows, :], wv_ext[...])
        values_v[rows, :] = product[:, :COLS].astype(BF16)
        y_value[rows, :] = product[:, COLS:]

    copies[4].wait()
    for crop in range(CROPS):
        rows = pl.ds(crop * LEN, LEN)
        for head in range(HEADS_DEV):
            cols = pl.ds(head * HEAD_DIM, HEAD_DIM)
            weights = probs_v[crop, head]
            mixed = dot(weights, values_v[rows, cols]).astype(BF16)
            mixed_t_out[cols, rows] = mixed.T
            d_mixed_t = d_mixed_v[rows, cols].T
            d_values_t_out[cols, rows] = dot(d_mixed_t, weights).astype(BF16)

    group = jnp.right_shift(lax.broadcasted_iota(jnp.int32, (TOK, 128), 1), 5)
    sides = (
        (copies[5], err_out_v, wo_ext, y_out, mixed_t_out),
        (copies[6], err_value_v, wv_ext, y_value, d_values_t_out),
    )
    for index, (copy, err_v, ext, y_ref, acts_t) in enumerate(sides):
        copy.wait()
        y_parts = lane_parts(all_groups(y_ref[...]), group)
        err_high, err_low = split2(err_v[...])
        start = ext[:, pl.ds(COLS, 128)]
        product = dot(acts_t[...], y_parts) + (dot(err_high, start) + dot(err_low, start))
        turned = product.T
        left_out[pl.ds(index * RANK, RANK), :] = (
            turned[0:32] + (turned[32:64] + turned[64:96])
        ).astype(BF16)
    normed_copy.wait()


def front(codes, gain, hidden, probs, w_value, w_out, out_grad, err_out, err_value):
    vmem = pl.BlockSpec(memory_space=pltpu.VMEM)
    return pl.pallas_call(
        front_kernel,
        name="front",
        out_shape=(
            jax.ShapeDtypeStruct((TOK, D), BF16),
            jax.ShapeDtypeStruct((COLS, TOK), BF16),
            jax.ShapeDtypeStruct((COLS, TOK), BF16),
            jax.ShapeDtypeStruct((2 * RANK, COLS), BF16),
        ),
        in_specs=[SMEM, vmem] + [ANY] * 7,
        out_specs=(ANY, vmem, vmem, vmem),
        scratch_shapes=[
            pltpu.VMEM((TOK, D), BF16),
            pltpu.VMEM((CROPS, HEADS_DEV, LEN, LEN), BF16),
            pltpu.VMEM((D, COLS + 128), BF16),
            pltpu.VMEM((COLS, D), BF16),
            pltpu.VMEM((D, COLS + 128), BF16),
            pltpu.VMEM((TOK, D), BF16),
            pltpu.VMEM((COLS, D), F32),
            pltpu.VMEM((COLS, D), F32),
            pltpu.VMEM((TOK, D), BF16),
            pltpu.VMEM((TOK, COLS), BF16),
            pltpu.VMEM((TOK, COLS), BF16),
            pltpu.VMEM((TOK, 128), F32),
            pltpu.VMEM((TOK, 128), F32),
            pltpu.SemaphoreType.DMA((7,)),
            pltpu.SemaphoreType.DMA((1,)),
        ],
        compiler_params=pltpu.CompilerParams(vmem_limit_bytes=56 * 2**20),
        cost_estimate=pl.CostEstimate(
            flops=11 * 10**9, bytes_accessed=32 * 10**6, transcendentals=0
        ),
    )(codes, gain, hidden, probs, w_value, w_out, out_grad, err_out, err_value)


def branch_kernel(place, d_values_t, w_value, normed, gain, own, other, gain_part, d_values):
    @pl.when(pl.program_id(0) == 0)
    def _():
        for block in range(TOK // 256):
            rows = pl.ds(block * 256, 256)
            d_values[rows, :] = d_values_t[:, rows].T

    product = dot(d_values[...], w_value[...], ((1,), (1,)))
    gain_part[...] = (
        jnp.sum(product * normed[...].astype(F32), axis=0, keepdims=True) / gain[...]
    )
    rounded = product.astype(BF16)
    chip, core = place[0], place[1]
    for block in range(8):
        slot = lax.rem(block // 2 - chip + 4, 4)
        part = rounded[block * 128 : (block + 1) * 128]

        @pl.when(core == block % 2)
        def _():
            own[slot] = part

        @pl.when(core != block % 2)
        def _():
            other[slot] = part


def branch(place, d_values_t, w_value, normed, gain):
    quarter = pl.BlockSpec((4, 128, TILE), lambda n: (0, 0, n))
    return pl.pallas_call(
        branch_kernel,
        name="branch",
        grid=(STEPS,),
        out_shape=(
            jax.ShapeDtypeStruct((4, 128, D), BF16),
            jax.ShapeDtypeStruct((4, 128, D), BF16),
            jax.ShapeDtypeStruct((1, D), F32),
        ),
        in_specs=[
            SMEM,
            pl.BlockSpec((COLS, TOK), lambda n: (0, 0)),
            pl.BlockSpec((TILE, COLS), lambda n: (n, 0)),
            pl.BlockSpec((TOK, TILE), lambda n: (0, n)),
            pl.BlockSpec((1, TILE), lambda n: (0, n)),
        ],
        out_specs=(quarter, quarter, pl.BlockSpec((1, TILE), lambda n: (0, n))),
        scratch_shapes=[pltpu.VMEM((TOK, COLS), BF16)],
        compiler_params=pltpu.CompilerParams(vmem_limit_bytes=40 * 2**20),
        cost_estimate=pl.CostEstimate(
            flops=2 * 10**9, bytes_accessed=13 * 10**6, transcendentals=0
        ),
    )(place, d_values_t, w_value, normed, gain)


def mats_kernel(acts_t, other_side, err, mats):
    mats[...] = dot(acts_t[...], other_side[...]) + err[0]


def mats_of(acts_t, other_side, err, name):
    return pl.pallas_call(
        mats_kernel,
        name=name,
        grid=(STEPS,),
        out_shape=jax.ShapeDtypeStruct((COLS, D), F32),
        in_specs=[
            pl.BlockSpec((COLS, TOK), lambda n: (0, 0)),
            pl.BlockSpec((TOK, TILE), lambda n: (0, n)),
            pl.BlockSpec((1, COLS, TILE), lambda n: (0, 0, n)),
        ],
        out_specs=pl.BlockSpec((COLS, TILE), lambda n: (0, n)),
        compiler_params=pltpu.CompilerParams(vmem_limit_bytes=32 * 2**20),
        cost_estimate=pl.CostEstimate(
            flops=2 * 10**9, bytes_accessed=13 * 10**6, transcendentals=0
        ),
    )(acts_t, other_side, err)


def right_kernel(place, left, gain_tail, mats_out, mats_value, own, other):
    chip, core = place[0], place[1]
    step = pl.program_id(0)
    lanes = pl.ds(pl.multiple_of(step * TILE, TILE), TILE)

    def put(side, span, value):
        for block in range(4):
            rows = pl.ds(pl.multiple_of(lax.rem(block - chip + 4, 4) * 8, 8), 8)
            part = value[block * 8 : (block + 1) * 8]

            @pl.when(core == side)
            def _():
                own[rows, span] = part

            @pl.when(core != side)
            def _():
                other[rows, span] = part

    for side, mats in enumerate((mats_out, mats_value)):
        rows = left[pl.ds(side * RANK, RANK), :]
        high, low = split2(rows)
        mats_high, mats_low = split2(mats[...])
        product = dot(high, mats_high) + (dot(low, mats_high) + dot(high, mats_low))
        put(side, lanes, product)

        @pl.when(step == 0)
        def _():
            gram = dot_split(rows, rows, ((1,), (1,)))
            wide = jnp.concatenate([gram, jnp.zeros((RANK, TAIL - RANK), F32)], axis=1)
            put(side, pl.ds(D, TAIL), wide + gain_tail[side])


def right_terms(place, left, gain_tail, mats_out, mats_value):
    whole = pl.BlockSpec((RANK, WIDE), lambda n: (0, 0))
    mats = pl.BlockSpec((COLS, TILE), lambda n: (0, n))
    return pl.pallas_call(
        right_kernel,
        name="right_terms",
        grid=(STEPS,),
        out_shape=(jax.ShapeDtypeStruct((RANK, WIDE), F32),) * 2,
        in_specs=[
            SMEM,
            pl.BlockSpec((2 * RANK, COLS), lambda n: (0, 0)),
            pl.BlockSpec((2, RANK, TAIL), lambda n: (0, 0, 0)),
            mats,
            mats,
        ],
        out_specs=(whole, whole),
        compiler_params=pltpu.CompilerParams(vmem_limit_bytes=32 * 2**20),
        cost_estimate=pl.CostEstimate(
            flops=1 * 10**9, bytes_accessed=9 * 10**6, transcendentals=0
        ),
    )(place, left, gain_tail, mats_out, mats_value)


def inverse_factor(gram):
    row_ids = lax.broadcasted_iota(jnp.int32, (RANK, 2 * RANK), 0)
    col_ids = lax.broadcasted_iota(jnp.int32, (RANK, 2 * RANK), 1)
    unit = jnp.where(row_ids + RANK == col_ids, 1.0, 0.0)
    work = jnp.concatenate([gram, jnp.zeros((RANK, RANK), F32)], axis=1) + unit
    for step in range(RANK - 1):
        pivot_row = work[step : step + 1, :]
        ratio = work[:, step : step + 1] / pivot_row[:, step : step + 1]
        work = work - jnp.where(row_ids > step, ratio * pivot_row, 0.0)
    diagonal = jnp.sum(jnp.where(row_ids == col_ids, work, 0.0), axis=1, keepdims=True)
    return work[:, RANK:] * lax.rsqrt(diagonal)


def finish_kernel(
    place, ours, theirs, left, mats_out, mats_value,
    err_out, err_value, right, ortho_out, tail_out,
    sums, ortho_parts, inverse,
):
    chip, core = place[0], place[1]
    step = pl.program_id(0)
    lanes = pl.ds(pl.multiple_of(step * TILE, TILE), TILE)

    @pl.when(step == 0)
    def _():
        for block in range(4):
            offset = lax.rem(chip + block, 4) * 8
            for side, source in ((core, ours), (1 - core, theirs)):
                rows = pl.ds(pl.multiple_of(side * RANK + offset, 8), 8)
                sums[rows, :] = source[pl.ds(block * 8, 8), :]
        tail_out[...] = sums[:, pl.ds(D, TAIL)]
        for side in range(2):
            span = pl.ds(side * RANK, RANK)
            gram = sums[span, pl.ds(D, TAIL)][:, :RANK] * (1.0 / WORKERS)
            factor = inverse_factor(gram)
            inverse[side] = factor
            ortho = dot_split(factor, left[span, :])
            ortho_out[span, :] = ortho * math.sqrt(HH)
            high, low = split2(ortho)
            parts = jnp.concatenate([high, low, high, jnp.zeros_like(high)], axis=0)
            ortho_parts[side] = parts.T

    for side, (mats, err) in enumerate(((mats_out, err_out), (mats_value, err_value))):
        span = pl.ds(side * RANK, RANK)
        rows = dot_split(inverse[side], sums[span, lanes]) * (1.0 / WORKERS)
        right[span, :] = rows
        high, low = split2(rows)
        parts = jnp.concatenate([high, high, low, jnp.zeros_like(high)], axis=0)
        err[0] = mats[...] - dot(ortho_parts[side], parts)


def finish(place, ours, theirs, left, mats_out, mats_value):
    whole = pl.BlockSpec((RANK, WIDE), lambda n: (0, 0))
    mats = pl.BlockSpec((COLS, TILE), lambda n: (0, n))
    err = pl.BlockSpec((1, COLS, TILE), lambda n: (0, 0, n))
    return pl.pallas_call(
        finish_kernel,
        name="finish",
        grid=(STEPS,),
        out_shape=(
            jax.ShapeDtypeStruct((1, COLS, D), F32),
            jax.ShapeDtypeStruct((1, COLS, D), F32),
            jax.ShapeDtypeStruct((2 * RANK, D), F32),
            jax.ShapeDtypeStruct((2 * RANK, COLS), F32),
            jax.ShapeDtypeStruct((2 * RANK, TAIL), F32),
        ),
        in_specs=[
            SMEM, whole, whole, pl.BlockSpec((2 * RANK, COLS), lambda n: (0, 0)), mats, mats,
        ],
        out_specs=(
            err,
            err,
            pl.BlockSpec((2 * RANK, TILE), lambda n: (0, n)),
            pl.BlockSpec((2 * RANK, COLS), lambda n: (0, 0)),
            pl.BlockSpec((2 * RANK, TAIL), lambda n: (0, 0)),
        ),
        scratch_shapes=[
            pltpu.VMEM((2 * RANK, WIDE), F32),
            pltpu.VMEM((2, COLS, 4 * RANK), BF16),
            pltpu.VMEM((2, RANK, RANK), F32),
        ],
        compiler_params=pltpu.CompilerParams(vmem_limit_bytes=32 * 2**20),
        cost_estimate=pl.CostEstimate(
            flops=1 * 10**9, bytes_accessed=17 * 10**6, transcendentals=0
        ),
    )(place, ours, theirs, left, mats_out, mats_value)


def to_core(value):
    return lax.ppermute(value, "tensor", [(i, i ^ 1) for i in range(8)])


def to_x(value, hops):
    return lax.ppermute(value, "tensor", [(i, (i // 2 + hops) % 4 * 2 + i % 2) for i in range(8)])


def to_z(value, hops):
    return lax.ppermute(value, "dp", [(i, i // 4 * 4 + (i + hops) % 4) for i in range(16)])


def to_y(value, hops):
    return lax.ppermute(value, "dp", [(i, (i // 4 + hops) % 4 * 4 + i % 4) for i in range(16)])


def ring_sum(value, send):
    opposite, after, before = send(value, 2), send(value, 1), send(value, 3)
    wide = value.astype(F32)
    return (wide + opposite.astype(F32)) + (after.astype(F32) + before.astype(F32))


def local(
    hidden_in, ln_gain, attn_probs, w_value, w_out, out_grad, err_out, err_value, factor_codes
):
    index = lax.axis_index("tensor")
    place = jnp.stack([index // 2, index % 2]).astype(jnp.int32)
    gain_row = ln_gain.reshape(1, D)
    normed, mixed_t, d_values_t, left_term = front(
        factor_codes, gain_row, hidden_in, attn_probs, w_value, w_out, out_grad, err_out, err_value
    )

    left = ring_sum(left_term, to_z)
    left = ring_sum(left.astype(BF16), to_y)

    own, other, gain_part = branch(place, d_values_t, w_value, normed, gain_row)
    mats_out = mats_of(mixed_t, out_grad, err_out, "mats_out")
    mats_value = mats_of(d_values_t, normed, err_value, "mats_value")

    chip_sum = (own.astype(F32) + to_core(other).astype(F32)).astype(BF16)
    far_after = to_x(chip_sum[2, :64], 1)
    far_before = to_x(chip_sum[2, 64:], 3)
    next_part = chip_sum[1].astype(F32).at[:64].add(far_after.astype(F32)).astype(BF16)
    last_part = chip_sum[3].astype(F32).at[64:].add(far_before.astype(F32)).astype(BF16)
    total = chip_sum[0].astype(F32) + (
        to_x(next_part, 1).astype(F32) + to_x(last_part, 3).astype(F32)
    )
    hidden = lax.dynamic_slice_in_dim(hidden_in, index * 128, 128, 0).astype(F32)
    centred = hidden - jnp.mean(hidden, axis=-1, keepdims=True)
    inv_std = lax.rsqrt(jnp.mean(centred * centred, axis=-1, keepdims=True) + 1e-05)
    standard = centred * inv_std
    scaled = total * ln_gain
    first_mean = jnp.mean(scaled, axis=-1, keepdims=True)
    second_mean = jnp.mean(scaled * standard, axis=-1, keepdims=True)
    in_grad = (inv_std * (scaled - first_mean - standard * second_mean)).astype(BF16)

    gain_tail = jnp.pad(gain_part.reshape(2, RANK, 40), ((0, 0), (0, 0), (RANK, TAIL - RANK - 40)))
    ours, theirs = right_terms(place, left, gain_tail, mats_out, mats_value)
    chunks = ours + to_core(theirs)
    opposite, after, before = (to_x(chunks[8 * k : 8 * k + 8], k) for k in (2, 1, 3))
    chunk = (chunks[:8] + opposite) + (after + before)
    chunk = ring_sum(chunk, to_z)
    chunk = ring_sum(chunk, to_y)
    opposite, after, before = to_x(chunk, 2), to_x(chunk, 3), to_x(chunk, 1)
    ours = jnp.concatenate([chunk, after, opposite, before], axis=0)
    theirs = to_core(ours)
    new_out, new_value, right, ortho, tail = finish(place, ours, theirs, left, mats_out, mats_value)
    gain_grad = tail[:, RANK : RANK + 40].reshape(D)
    share = lax.dynamic_slice_in_dim(right, index * (D // 8), D // 8, 1)
    return (
        in_grad,
        gain_grad,
        new_out,
        new_value,
        ortho[:RANK].T,
        ortho[RANK:].T,
        share[:RANK].T,
        share[RANK:].T,
    )


def solution(mesh):
    in_specs = (
        P("dp", None),
        P(),
        P("dp", "tensor", None, None),
        P(None, "tensor"),
        P("tensor", None),
        P("dp", None),
        P("dp", "tensor", None),
        P("dp", "tensor", None),
        P(),
    )
    out_specs = (
        P(("dp", "tensor"), None),
        P(),
        P("dp", "tensor", None),
        P("dp", "tensor", None),
        P("tensor", None),
        P("tensor", None),
        P("tensor", None),
        P("tensor", None),
    )
    return jax.shard_map(local, mesh=mesh, in_specs=in_specs, out_specs=out_specs, check_vma=False)
```

time: 505 us -> 153 us (0.30); the launches traced: 498 us -> 152 us
  blocking collectives: 175 us -> 0 us
  waiting for transfers between devices: 195 us -> 29.7 us
  matrix products: 60.9 us -> 0 us
  Pallas kernels: 0 us -> 50.5 us
  starting transfers between devices: 0.08 us -> 35.9 us
  other arithmetic: 39.1 us -> 13.9 us
  between operations: 16.3 us -> 0.9 us
  local copies, waits for them, and re-layouts: 12.2 us -> 21.2 us
    psum x2 -> x0, waiting for transfers between devices: 195 us -> none  [the longest x1 134 us: compress_apart(): lax.psum(precise_dot(matrix.T, ortho), ('dp', 'tensor')) / worker_count]
    psum x3 -> x0, blocking collectives: 175 us -> none  [the longest x1 76.4 us: compress_apart(): lax.psum(precise_dot(matrix, start).astype(jnp.bfloat16), 'dp')]
    dot_general x15 -> x0, matrix products: 59.1 us -> none  [the longest x8 31.4 us: precise_dot(): return jnp.dot(left_side, right_side, precision=lax.Precision.HIGHEST)]
    pallas_call x0 -> x6, Pallas kernels: none -> 50.5 us  [the longest x1 22.9 us: front(): pl.pallas_call(front_kernel, name='front', out_shape=(jax.ShapeDtypeStruc...]
    ppermute x0 -> x25, starting transfers between devices: none -> 35.9 us  [the longest x10 15.6 us: to_x(): lax.ppermute(value, 'tensor', [(i, (i // 2 + hops) % 4 * 2 + i % 2) for i...]
    ppermute x0 -> x25, waiting for transfers between devices: none -> 29.7 us  [the longest x10 19.4 us: to_x(): lax.ppermute(value, 'tensor', [(i, (i // 2 + hops) % 4 * 2 + i % 2) for i...]
    unnamed x36 -> x44, local copies, waits for them, and re-layouts: 1.24 us -> 17.5 us
    reduce_sum x3, other arithmetic: 20.9 us -> 4.92 us  [the longest x1 2.11 us: local(): first_mean = jnp.mean(scaled, axis=-1, keepdims=True)]
  transfers between devices with their start and end apart: 2 -> 25, of which waited for: 2 -> 14; matrix products, arithmetic and copies ran while one was open for 4% -> 7% of each run, Pallas kernels for 0% -> 15%
where the time goes in v1:
time: 153 us; the launch traced here: 152 us
  Pallas kernels  50.5 us (33%)
  starting transfers between devices  35.9 us (23%)
  waiting for transfers between devices  29.7 us (19%)
  local copies, waits for them, and re-layouts  21.2 us (14%)
  other arithmetic  13.9 us (9%)
    pallas_call x1, Pallas kernels, front(): pl.pallas_call(front_kernel, name='front', out_shape=(jax.ShapeDtypeStruc...  22.9 us
    ppermute x10, waiting for transfers between devices, to_x(): lax.ppermute(value, 'tensor', [(i, (i // 2 + hops) % 4 * 2 + i % 2) for i...  19.4 us
    unnamed x44, local copies, waits for them, and re-layouts  17.5 us
    ppermute x10, starting transfers between devices, to_x(): lax.ppermute(value, 'tensor', [(i, (i // 2 + hops) % 4 * 2 + i % 2) for i...  15.6 us
    ppermute x6, starting transfers between devices, to_z(): lax.ppermute(value, 'dp', [(i, i // 4 * 4 + (i + hops) % 4) for i in rang...  10.5 us
    ppermute x6, starting transfers between devices, to_y(): lax.ppermute(value, 'dp', [(i, (i // 4 + hops) % 4 * 4 + i % 4) for i in...  9.41 us
    pallas_call x1, Pallas kernels, finish(): pl.pallas_call(finish_kernel, name='finish', grid=(STEPS,), out_shape=(ja...  8.5 us
    pallas_call x2, Pallas kernels, mats_of(): pl.pallas_call(mats_kernel, name=name, grid=(STEPS,), out_shape=jax.Shape...  7.64 us
  transfers between devices with their start and end apart: 25, of which 14 were waited for; matrix products, arithmetic and copies ran while one was open for 7% of the time, Pallas kernels for 15%

profile of v1, /device:TPU:0, one launch (start us, length us, event | category | flops | bytes accessed | tf_op | source)
XLA Modules:
  0.0 151.9 jit_solution(9962416061888048200)
XLA Ops:
  1.9 22.9 %front.1 = (bf16[1024,2560]{1,0:T(8,128)(2,1)}, bf16[384,1024]{1,0:T(8,128)(2,1)}, bf16[384,1024]{1,0:T(8,128)(2,1)}, bf16[64,384]{1,0:T(8,128)(2,1)}) custom-call(s32[2]{0:T(128)} %codes.1, f32[1,2560]{1,0:T(1,128)} %reshape.105.gain, bf16[1024,2560]{1,0:T(8,128)(2,1)} %hidden.1, bf16[2,3,512,512]{3,2,1,0:T(8,128)(2,1)} %probs.1, ...), custom_call_target="tpu_custom_call" | custom-call | flops 11000000512 | bytes 32000000 | tf_op jit(solution)/shard_map/front/pallas_call | solution.py:180
  24.9 4.2 %collective-permute-start.7 = (bf16[64,384]{1,0:T(8,128)(2,1)}, bf16[64,384]{1,0:T(8,128)(2,1)S(1)}, u32[]{:S(2)}, u32[]{:S(2)}) collective-permute-start(bf16[64,384]{1,0:T(8,128)(2,1)} %get-tuple-element.50), channel_id=1, source_target_pairs={{0,24},{8,0},{16,8},{24,16},{32,56},{40,32},{48,40},{56,48},{64,88... | collective-permute-start | bytes 147464 | tf_op jit(solution)/shard_map/ppermute | solution.py:442
  31.0 2.5 %copy-done.6 = bf16[1024,2560]{1,0:T(8,128)(2,1)S(1)} copy-done((bf16[1024,2560]{1,0:T(8,128)(2,1)S(1)}, bf16[1024,2560]{1,0:T(8,128)(2,1)}, u32[]{:S(2)}) %copy-start.6) | copy-done | bytes 5242904
  36.8 3.8 %mats_value.1 = f32[384,2560]{1,0:T(8,128)S(1)} custom-call(bf16[384,1024]{1,0:T(8,128)(2,1)S(1)} %copy-done.11, bf16[1024,2560]{1,0:T(8,128)(2,1)S(1)} %copy-done.6, f32[1,384,2560]{2,1,0:T(8,128)S(1)} %copy-done.9), custom_call_target="tpu_custom_call" | custom-call | flops 2000000000 | bytes 13000000 | tf_op jit(solution)/shard_map/mats_value/pallas_call | solution.py:273
  44.1 6.7 %branch.1 = (bf16[4,128,2560]{2,1,0:T(8,128)(2,1)S(1)}, bf16[4,128,2560]{2,1,0:T(8,128)(2,1)}, f32[1,2560]{1,0:T(1,128)S(1)}) custom-call(s32[2]{0:T(128)S(1)} %pad_add_fusion.place, bf16[384,1024]{1,0:T(8,128)(2,1)S(1)} %copy-done.12, bf16[2560,384]{1,0:T(8,128)(2,1)S(1)} %copy-done.15, bf16[1024,2560]{1,0:T(8,128)(2,1)S(1)} %copy-done.7, ...), custom_call_target="tpu_custom_call" | custom-call | flops 2000000000 | bytes 13000000 | tf_op jit(solution)/shard_map/branch/pallas_call | solution.py:243
  50.8 3.1 %collective-permute-start.10 = (bf16[64,384]{1,0:T(8,128)(2,1)S(1)}, bf16[64,384]{1,0:T(8,128)(2,1)S(1)}, u32[]{:S(2)}, u32[]{:S(2)}) collective-permute-start(bf16[64,384]{1,0:T(8,128)(2,1)S(1)} %add_convert_fusion.1), channel_id=1, source_target_pairs={{0,96},{8,104},{16,112},{24,120},{32,0},{40,8},{48,16},{56,24},{64... | collective-permute-start | bytes 147464 | tf_op jit(solution)/shard_map/ppermute | solution.py:446
  53.9 2.2 %collective-permute-start.8 = (bf16[64,384]{1,0:T(8,128)(2,1)S(1)}, bf16[64,384]{1,0:T(8,128)(2,1)S(1)}, u32[]{:S(2)}, u32[]{:S(2)}) collective-permute-start(bf16[64,384]{1,0:T(8,128)(2,1)S(1)} %add_convert_fusion.1), channel_id=1, source_target_pairs={{0,64},{8,72},{16,80},{24,88},{32,96},{40,104},{48,112},{56,120},{... | collective-permute-start | bytes 147464 | tf_op jit(solution)/shard_map/ppermute | solution.py:446
  56.1 2.1 %copy-done.10 = f32[1,384,2560]{2,1,0:T(8,128)S(1)} copy-done((f32[1,384,2560]{2,1,0:T(8,128)S(1)}, f32[1,384,2560]{2,1,0:T(8,128)}, u32[]{:S(2)}) %copy-start.10) | copy-done | bytes 3932184
  58.2 3.8 %mats_out.1 = f32[384,2560]{1,0:T(8,128)S(1)} custom-call(bf16[384,1024]{1,0:T(8,128)(2,1)S(1)} %copy-done.16, bf16[1024,2560]{1,0:T(8,128)(2,1)S(1)} %copy-done.8, f32[1,384,2560]{2,1,0:T(8,128)S(1)} %copy-done.10), custom_call_target="tpu_custom_call" | custom-call | flops 2000000000 | bytes 13000000 | tf_op jit(solution)/shard_map/mats_out/pallas_call | solution.py:273
  68.5 4.7 %right_terms.1 = (f32[32,2688]{1,0:T(8,128)S(1)}, f32[32,2688]{1,0:T(8,128)S(1)}) custom-call(s32[2]{0:T(128)S(1)} %pad_add_fusion.place, f32[64,384]{1,0:T(8,128)S(1)} %add_add_fusion.left, f32[2,32,128]{2,1,0:T(8,128)S(1)} %pad.8.gain_tail, f32[384,2560]{1,0:T(8,128)S(1)} %copy-done.4, f32[384,2560]{1,0:T(8,128)S(1)} %copy-done.1), custom_call_target="tpu_custom_call" | custom-call | flops 1000000000 | bytes 9000000 | tf_op jit(solution)/shard_map/right_terms/pallas_call | solution.py:326
  75.2 3.1 %collective-permute-start.12 = (f32[8,2688]{1,0:T(8,128)S(1)}, f32[8,2688]{1,0:T(8,128)S(1)}, u32[]{:S(2)}, u32[]{:S(2)}) collective-permute-start(f32[8,2688]{1,0:T(8,128)S(1)} %get-tuple-element.72), channel_id=1, source_target_pairs={{0,4},{1,5},{2,6},{3,7},{4,0},{5,1},{6,2},{7,3},{8,12},{9,13},{10,... | collective-permute-start | bytes 258056 | tf_op jit(solution)/shard_map/ppermute | solution.py:438
  78.9 2.6 %collective-permute-start.14 = (f32[8,2688]{1,0:T(8,128)S(1)}, f32[8,2688]{1,0:T(8,128)S(1)}, u32[]{:S(2)}, u32[]{:S(2)}) collective-permute-start(f32[8,2688]{1,0:T(8,128)S(1)} %get-tuple-element.70), channel_id=1, source_target_pairs={{0,6},{1,7},{2,0},{3,1},{4,2},{5,3},{6,4},{7,5},{8,14},{9,15},{10,... | collective-permute-start | bytes 258056 | tf_op jit(solution)/shard_map/ppermute | solution.py:438
  81.5 2.5 %collective-permute-done.13 = f32[8,2688]{1,0:T(8,128)S(1)} collective-permute-done((f32[8,2688]{1,0:T(8,128)S(1)}, f32[8,2688]{1,0:T(8,128)S(1)}, u32[]{:S(2)}, u32[]{:S(2)}) %collective-permute-start.13) | collective-permute-done | bytes 86048 | tf_op jit(solution)/shard_map/ppermute | solution.py:438
  84.0 2.3 %collective-permute-start.16 = (f32[8,2688]{1,0:T(8,128)S(1)}, f32[8,2688]{1,0:T(8,128)S(1)}, u32[]{:S(2)}, u32[]{:S(2)}) collective-permute-start(f32[8,2688]{1,0:T(8,128)S(1)} %fusion.16), channel_id=1, source_target_pairs={{0,8},{8,16},{16,24},{24,0},{32,40},{40,48},{48,56},{56,32},{64,72... | collective-permute-start | bytes 258056 | tf_op jit(solution)/shard_map/ppermute | solution.py:442
  90.8 2.5 %collective-permute-done.15 = f32[8,2688]{1,0:T(8,128)S(1)} collective-permute-done((f32[8,2688]{1,0:T(8,128)S(1)}, f32[8,2688]{1,0:T(8,128)S(1)}, u32[]{:S(2)}, u32[]{:S(2)}) %collective-permute-start.15) | collective-permute-done | bytes 86048 | tf_op jit(solution)/shard_map/ppermute | solution.py:442
  99.8 2.8 %collective-permute-done.18 = f32[8,2688]{1,0:T(8,128)S(1)} collective-permute-done((f32[8,2688]{1,0:T(8,128)S(1)}, f32[8,2688]{1,0:T(8,128)S(1)}, u32[]{:S(2)}, u32[]{:S(2)}) %collective-permute-start.18) | collective-permute-done | bytes 86048 | tf_op jit(solution)/shard_map/ppermute | solution.py:446
  103.5 3.9 %collective-permute-start.22 = (f32[8,2688]{1,0:T(8,128)S(1)}, f32[8,2688]{1,0:T(8,128)S(1)}, u32[]{:S(2)}, u32[]{:S(2)}) collective-permute-start(f32[8,2688]{1,0:T(8,128)S(1)} %add_add_fusion.1), channel_id=1, source_target_pairs={{0,4},{1,5},{2,6},{3,7},{4,0},{5,1},{6,2},{7,3},{8,12},{9,13},{10,... | collective-permute-start | bytes 258056 | tf_op jit(solution)/shard_map/ppermute | solution.py:438
  112.0 2.6 %add_convert_fusion = bf16[4,128,2560]{2,1,0:T(8,128)(2,1)S(1)} fusion(bf16[4,128,2560]{2,1,0:T(8,128)(2,1)} %collective-permute-done, bf16[4,128,2560]{2,1,0:T(8,128)(2,1)S(1)} %copy-done.14), kind=kLoop, calls=%fused_computation | loop fusion | flops 5242880 | bytes 7864320 | tf_op jit(solution)/shard_map/convert_element_type | solution.py:472
  118.2 6.6 %collective-permute-done.3 = bf16[64,2560]{1,0:T(8,128)(2,1)S(1)} collective-permute-done((bf16[64,2560]{1,0:T(8,128)(2,1)S(1)}, bf16[64,2560]{1,0:T(8,128)(2,1)S(1)}, u32[]{:S(2)}, u32[]{:S(2)}) %collective-permute-start.3) | collective-permute-done | bytes 327712 | tf_op jit(solution)/shard_map/ppermute | solution.py:438
  125.6 2.4 %collective-permute-start.4 = (bf16[128,2560]{1,0:T(8,128)(2,1)}, bf16[128,2560]{1,0:T(8,128)(2,1)}, u32[]{:S(2)}, u32[]{:S(2)}) collective-permute-start(bf16[128,2560]{1,0:T(8,128)(2,1)} %fusion.11), channel_id=1, source_target_pairs={{0,6},{1,7},{2,0},{3,1},{4,2},{5,3},{6,4},{7,5},{8,14},{9,15},{10,... | collective-permute-start | bytes 1966088 | tf_op jit(solution)/shard_map/ppermute | solution.py:438
  129.3 8.5 %finish.1 = (f32[1,384,2560]{2,1,0:T(8,128)}, f32[1,384,2560]{2,1,0:T(8,128)}, f32[64,2560]{1,0:T(8,128)S(1)}, f32[64,384]{1,0:T(8,128)S(1)}, f32[64,128]{1,0:T(8,128)S(1)}) custom-call(s32[2]{0:T(128)S(1)} %pad_add_fusion.place, f32[32,2688]{1,0:T(8,128)S(1)} %pad_maximum_fusion.ours, f32[32,2688]{1,0:T(8,128)S(1)} %collective-permute-done.24.theirs, ...), custom_call_target="tpu_custom_call" | custom-call | flops 1000000000 | bytes 17000000 | tf_op jit(solution)/shard_map/finish/pallas_call | solution.py:400
  139.9 2.4 %collective-permute-done.4 = bf16[128,2560]{1,0:T(8,128)(2,1)} collective-permute-done((bf16[128,2560]{1,0:T(8,128)(2,1)}, bf16[128,2560]{1,0:T(8,128)(2,1)}, u32[]{:S(2)}, u32[]{:S(2)}) %collective-permute-start.4) | collective-permute-done | bytes 655392 | tf_op jit(solution)/shard_map/ppermute | solution.py:438
  142.3 4.5 %collective-permute-done.2 = bf16[128,2560]{1,0:T(8,128)(2,1)} collective-permute-done((bf16[128,2560]{1,0:T(8,128)(2,1)}, bf16[128,2560]{1,0:T(8,128)(2,1)}, u32[]{:S(2)}, u32[]{:S(2)}) %collective-permute-start.2) | collective-permute-done | bytes 655392 | tf_op jit(solution)/shard_map/ppermute | solution.py:438
  148.9 3.0 %fusion.7 = bf16[128,2560]{1,0:T(8,128)(2,1)} fusion(f32[128]{0:T(128)S(1)} %get-tuple-element.75, f32[128]{0:T(128)S(1)} %get-tuple-element.76, f32[128]{0:T(128)S(1)} %add_rsqrt_fusion, f32[128]{0:T(128)S(1)} %broadcast_multiply_fusion.2, bf16[1024,2560]{1,0:T(8,128)(2,1)} %hidden.1, s32[]{:T(128)S(6)} %select_n.17, f32[2560]{0:T(1024)S(1)} %copy-done.20, ...), kind=kLoop, calls=%fused_computation.10 | loop fusion | flops 4587520 | bytes 3289092 | tf_op jit(solution)/shard_map/convert_element_type | solution.py:487
  (105 shorter events, 45.2 us)
Async XLA Ops:
  24.9 25.9 %collective-permute-start.7 = (bf16[64,384]{1,0:T(8,128)(2,1)}, bf16[64,384]{1,0:T(8,128)(2,1)S(1)}, u32[]{:S(2)}, u32[]{:S(2)}) collective-permute-start(bf16[64,384]{1,0:T(8,128)(2,1)} %get-tuple-element.50), channel_id=1, source_target_pairs={{0,24},{8,0},{16,8},{24,16},{32,56},{40,32},{48,40},{56,48},{64,88... | collective-permute-start | bytes 147464 | tf_op jit(solution)/shard_map/ppermute | solution.py:442
  29.1 21.7 %collective-permute-start.6 = (bf16[64,384]{1,0:T(8,128)(2,1)}, bf16[64,384]{1,0:T(8,128)(2,1)S(1)}, u32[]{:S(2)}, u32[]{:S(2)}) collective-permute-start(bf16[64,384]{1,0:T(8,128)(2,1)} %get-tuple-element.50), channel_id=1, source_target_pairs={{0,8},{8,16},{16,24},{24,0},{32,40},{40,48},{48,56},{56,32},{64,72... | collective-permute-start | bytes 147464 | tf_op jit(solution)/shard_map/ppermute | solution.py:442
  29.1 21.7 %collective-permute-start.5 = (bf16[64,384]{1,0:T(8,128)(2,1)}, bf16[64,384]{1,0:T(8,128)(2,1)S(1)}, u32[]{:S(2)}, u32[]{:S(2)}) collective-permute-start(bf16[64,384]{1,0:T(8,128)(2,1)} %get-tuple-element.50), channel_id=1, source_target_pairs={{0,16},{8,24},{16,0},{24,8},{32,48},{40,56},{48,32},{56,40},{64,80... | collective-permute-start | bytes 147464 | tf_op jit(solution)/shard_map/ppermute | solution.py:442
  50.8 13.4 %collective-permute-start.10 = (bf16[64,384]{1,0:T(8,128)(2,1)S(1)}, bf16[64,384]{1,0:T(8,128)(2,1)S(1)}, u32[]{:S(2)}, u32[]{:S(2)}) collective-permute-start(bf16[64,384]{1,0:T(8,128)(2,1)S(1)} %add_convert_fusion.1), channel_id=1, source_target_pairs={{0,96},{8,104},{16,112},{24,120},{32,0},{40,8},{48,16},{56,24},{64... | collective-permute-start | bytes 147464 | tf_op jit(solution)/shard_map/ppermute | solution.py:446
  53.9 10.3 %collective-permute-start.9 = (bf16[64,384]{1,0:T(8,128)(2,1)S(1)}, bf16[64,384]{1,0:T(8,128)(2,1)S(1)}, u32[]{:S(2)}, u32[]{:S(2)}) collective-permute-start(bf16[64,384]{1,0:T(8,128)(2,1)S(1)} %add_convert_fusion.1), channel_id=1, source_target_pairs={{0,32},{8,40},{16,48},{24,56},{32,64},{40,72},{48,80},{56,88},{64,... | collective-permute-start | bytes 147464 | tf_op jit(solution)/shard_map/ppermute | solution.py:446
  53.9 10.3 %collective-permute-start.8 = (bf16[64,384]{1,0:T(8,128)(2,1)S(1)}, bf16[64,384]{1,0:T(8,128)(2,1)S(1)}, u32[]{:S(2)}, u32[]{:S(2)}) collective-permute-start(bf16[64,384]{1,0:T(8,128)(2,1)S(1)} %add_convert_fusion.1), channel_id=1, source_target_pairs={{0,64},{8,72},{16,80},{24,88},{32,96},{40,104},{48,112},{56,120},{... | collective-permute-start | bytes 147464 | tf_op jit(solution)/shard_map/ppermute | solution.py:446
  75.2 6.3 %collective-permute-start.12 = (f32[8,2688]{1,0:T(8,128)S(1)}, f32[8,2688]{1,0:T(8,128)S(1)}, u32[]{:S(2)}, u32[]{:S(2)}) collective-permute-start(f32[8,2688]{1,0:T(8,128)S(1)} %get-tuple-element.72), channel_id=1, source_target_pairs={{0,4},{1,5},{2,6},{3,7},{4,0},{5,1},{6,2},{7,3},{8,12},{9,13},{10,... | collective-permute-start | bytes 258056 | tf_op jit(solution)/shard_map/ppermute | solution.py:438
  78.3 5.7 %collective-permute-start.13 = (f32[8,2688]{1,0:T(8,128)S(1)}, f32[8,2688]{1,0:T(8,128)S(1)}, u32[]{:S(2)}, u32[]{:S(2)}) collective-permute-start(f32[8,2688]{1,0:T(8,128)S(1)} %get-tuple-element.71), channel_id=1, source_target_pairs={{0,2},{1,3},{2,4},{3,5},{4,6},{5,7},{6,0},{7,1},{8,10},{9,11},{10,... | collective-permute-start | bytes 258056 | tf_op jit(solution)/shard_map/ppermute | solution.py:438
  78.9 5.1 %collective-permute-start.14 = (f32[8,2688]{1,0:T(8,128)S(1)}, f32[8,2688]{1,0:T(8,128)S(1)}, u32[]{:S(2)}, u32[]{:S(2)}) collective-permute-start(f32[8,2688]{1,0:T(8,128)S(1)} %get-tuple-element.70), channel_id=1, source_target_pairs={{0,6},{1,7},{2,0},{3,1},{4,2},{5,3},{6,4},{7,5},{8,14},{9,15},{10,... | collective-permute-start | bytes 258056 | tf_op jit(solution)/shard_map/ppermute | solution.py:438
  81.5 30.5 %collective-permute-start = (bf16[4,128,2560]{2,1,0:T(8,128)(2,1)}, bf16[4,128,2560]{2,1,0:T(8,128)(2,1)}, u32[]{:S(2)}, u32[]{:S(2)}) collective-permute-start(bf16[4,128,2560]{2,1,0:T(8,128)(2,1)} %get-tuple-element.49), channel_id=1, source_target_pairs={{0,1},{1,0},{2,3},{3,2},{4,5},{5,4},{6,7},{7,6},{8,9},{9,8},{10,11... | collective-permute-start | bytes 7864328 | tf_op jit(solution)/shard_map/ppermute | solution.py:434
  84.0 6.7 %collective-permute-start.16 = (f32[8,2688]{1,0:T(8,128)S(1)}, f32[8,2688]{1,0:T(8,128)S(1)}, u32[]{:S(2)}, u32[]{:S(2)}) collective-permute-start(f32[8,2688]{1,0:T(8,128)S(1)} %fusion.16), channel_id=1, source_target_pairs={{0,8},{8,16},{16,24},{24,0},{32,40},{40,48},{48,56},{56,32},{64,72... | collective-permute-start | bytes 258056 | tf_op jit(solution)/shard_map/ppermute | solution.py:442
  86.3 4.5 %collective-permute-start.17 = (f32[8,2688]{1,0:T(8,128)S(1)}, f32[8,2688]{1,0:T(8,128)S(1)}, u32[]{:S(2)}, u32[]{:S(2)}) collective-permute-start(f32[8,2688]{1,0:T(8,128)S(1)} %fusion.16), channel_id=1, source_target_pairs={{0,24},{8,0},{16,8},{24,16},{32,56},{40,32},{48,40},{56,48},{64,88... | collective-permute-start | bytes 258056 | tf_op jit(solution)/shard_map/ppermute | solution.py:442
  87.3 6.0 %collective-permute-start.15 = (f32[8,2688]{1,0:T(8,128)S(1)}, f32[8,2688]{1,0:T(8,128)S(1)}, u32[]{:S(2)}, u32[]{:S(2)}) collective-permute-start(f32[8,2688]{1,0:T(8,128)S(1)} %fusion.16), channel_id=1, source_target_pairs={{0,16},{8,24},{16,0},{24,8},{32,48},{40,56},{48,32},{56,40},{64,80... | collective-permute-start | bytes 258056 | tf_op jit(solution)/shard_map/ppermute | solution.py:442
  93.3 6.2 %collective-permute-start.19 = (f32[8,2688]{1,0:T(8,128)S(1)}, f32[8,2688]{1,0:T(8,128)S(1)}, u32[]{:S(2)}, u32[]{:S(2)}) collective-permute-start(f32[8,2688]{1,0:T(8,128)S(1)} %add_add_fusion.2), channel_id=1, source_target_pairs={{0,32},{8,40},{16,48},{24,56},{32,64},{40,72},{48,80},{56,88},{64,... | collective-permute-start | bytes 258056 | tf_op jit(solution)/shard_map/ppermute | solution.py:446
  95.3 4.5 %collective-permute-start.20 = (f32[8,2688]{1,0:T(8,128)S(1)}, f32[8,2688]{1,0:T(8,128)S(1)}, u32[]{:S(2)}, u32[]{:S(2)}) collective-permute-start(f32[8,2688]{1,0:T(8,128)S(1)} %add_add_fusion.2), channel_id=1, source_target_pairs={{0,96},{8,104},{16,112},{24,120},{32,0},{40,8},{48,16},{56,24},{64... | collective-permute-start | bytes 258056 | tf_op jit(solution)/shard_map/ppermute | solution.py:446
  96.6 6.0 %collective-permute-start.18 = (f32[8,2688]{1,0:T(8,128)S(1)}, f32[8,2688]{1,0:T(8,128)S(1)}, u32[]{:S(2)}, u32[]{:S(2)}) collective-permute-start(f32[8,2688]{1,0:T(8,128)S(1)} %add_add_fusion.2), channel_id=1, source_target_pairs={{0,64},{8,72},{16,80},{24,88},{32,96},{40,104},{48,112},{56,120},{... | collective-permute-start | bytes 258056 | tf_op jit(solution)/shard_map/ppermute | solution.py:446
  102.7 6.2 %collective-permute-start.23 = (f32[8,2688]{1,0:T(8,128)S(1)}, f32[8,2688]{1,0:T(8,128)S(1)}, u32[]{:S(2)}, u32[]{:S(2)}) collective-permute-start(f32[8,2688]{1,0:T(8,128)S(1)} %add_add_fusion.1), channel_id=1, source_target_pairs={{0,2},{1,3},{2,4},{3,5},{4,6},{5,7},{6,0},{7,1},{8,10},{9,11},{10,... | collective-permute-start | bytes 258056 | tf_op jit(solution)/shard_map/ppermute | solution.py:438
  103.5 7.3 %collective-permute-start.22 = (f32[8,2688]{1,0:T(8,128)S(1)}, f32[8,2688]{1,0:T(8,128)S(1)}, u32[]{:S(2)}, u32[]{:S(2)}) collective-permute-start(f32[8,2688]{1,0:T(8,128)S(1)} %add_add_fusion.1), channel_id=1, source_target_pairs={{0,4},{1,5},{2,6},{3,7},{4,0},{5,1},{6,2},{7,3},{8,12},{9,13},{10,... | collective-permute-start | bytes 258056 | tf_op jit(solution)/shard_map/ppermute | solution.py:438
  107.4 4.5 %collective-permute-start.21 = (f32[8,2688]{1,0:T(8,128)S(1)}, f32[8,2688]{1,0:T(8,128)S(1)}, u32[]{:S(2)}, u32[]{:S(2)}) collective-permute-start(f32[8,2688]{1,0:T(8,128)S(1)} %add_add_fusion.1), channel_id=1, source_target_pairs={{0,6},{1,7},{2,0},{3,1},{4,2},{5,3},{6,4},{7,5},{8,14},{9,15},{10,... | collective-permute-start | bytes 258056 | tf_op jit(solution)/shard_map/ppermute | solution.py:438
  111.9 17.3 %collective-permute-start.24 = (f32[32,2688]{1,0:T(8,128)S(1)}, f32[32,2688]{1,0:T(8,128)S(1)}, u32[]{:S(2)}, u32[]{:S(2)}) collective-permute-start(f32[32,2688]{1,0:T(8,128)S(1)} %pad_maximum_fusion.ours), channel_id=1, source_target_pairs={{0,1},{1,0},{2,3},{3,2},{4,5},{5,4},{6,7},{7,6},{8,9},{9,8},{10,11... | collective-permute-start | bytes 1032200 | tf_op jit(solution)/shard_map/ppermute | solution.py:434
  114.7 10.2 %collective-permute-start.3 = (bf16[64,2560]{1,0:T(8,128)(2,1)S(1)}, bf16[64,2560]{1,0:T(8,128)(2,1)S(1)}, u32[]{:S(2)}, u32[]{:S(2)}) collective-permute-start(bf16[64,2560]{1,0:T(8,128)(2,1)S(1)} %get-tuple-element.63), channel_id=1, source_target_pairs={{0,6},{1,7},{2,0},{3,1},{4,2},{5,3},{6,4},{7,5},{8,14},{9,15},{10,... | collective-permute-start | bytes 983048 | tf_op jit(solution)/shard_map/ppermute | solution.py:438
  117.4 11.0 %collective-permute-start.1 = (bf16[64,2560]{1,0:T(8,128)(2,1)S(1)}, bf16[64,2560]{1,0:T(8,128)(2,1)S(1)}, u32[]{:S(2)}, u32[]{:S(2)}) collective-permute-start(bf16[64,2560]{1,0:T(8,128)(2,1)S(1)} %get-tuple-element.62), channel_id=1, source_target_pairs={{0,2},{1,3},{2,4},{3,5},{4,6},{5,7},{6,0},{7,1},{8,10},{9,11},{10,... | collective-permute-start | bytes 983048 | tf_op jit(solution)/shard_map/ppermute | solution.py:438
  125.6 16.6 %collective-permute-start.4 = (bf16[128,2560]{1,0:T(8,128)(2,1)}, bf16[128,2560]{1,0:T(8,128)(2,1)}, u32[]{:S(2)}, u32[]{:S(2)}) collective-permute-start(bf16[128,2560]{1,0:T(8,128)(2,1)} %fusion.11), channel_id=1, source_target_pairs={{0,6},{1,7},{2,0},{3,1},{4,2},{5,3},{6,4},{7,5},{8,14},{9,15},{10,... | collective-permute-start | bytes 1966088 | tf_op jit(solution)/shard_map/ppermute | solution.py:438
  129.2 17.5 %collective-permute-start.2 = (bf16[128,2560]{1,0:T(8,128)(2,1)}, bf16[128,2560]{1,0:T(8,128)(2,1)}, u32[]{:S(2)}, u32[]{:S(2)}) collective-permute-start(bf16[128,2560]{1,0:T(8,128)(2,1)} %fusion.13), channel_id=1, source_target_pairs={{0,2},{1,3},{2,4},{3,5},{4,6},{5,7},{6,0},{7,1},{8,10},{9,11},{10,... | collective-permute-start | bytes 1966088 | tf_op jit(solution)/shard_map/ppermute | solution.py:438
  (23 other events, 166.9 us)

commit v2 on v1

v2 whole, which is shorter than its diff:
```python
import math

import jax
import jax.numpy as jnp
from jax import lax
from jax.experimental import pallas as pl
from jax.experimental.pallas import tpu as pltpu
from jax.sharding import PartitionSpec as P

D = 2560
RANK = 32
HEADS = 24
HEAD_DIM = 128
LEN = 512
CROPS = 2
HEADS_DEV = 3
TOK = CROPS * LEN
COLS = HEADS_DEV * HEAD_DIM
HH = HEADS * HEAD_DIM
SENT = D + 128
WIDE = D + 384
TILE = 512
STEPS = D // TILE
LN_ROWS = 512
MERGE = 2
WORKERS = 16
F32 = jnp.float32
BF16 = jnp.bfloat16
ANY = pl.BlockSpec(memory_space=pl.ANY)
SMEM = pl.BlockSpec(memory_space=pltpu.SMEM)


def place():
    index = lax.axis_index("tensor")
    return lax.div(index, 2), lax.rem(index, 2)


def dot(a, b, dims=((1,), (0,))):
    return lax.dot_general(a, b, (dims, ((), ())), preferred_element_type=F32)


def split2(a):
    high = a.astype(BF16)
    return high, (a - high.astype(F32)).astype(BF16)


def dot_split(a, b, dims=((1,), (0,))):
    a_high, a_low = split2(a)
    b_high, b_low = split2(b)
    return dot(a_high, b_high, dims) + (dot(a_low, b_high, dims) + dot(a_high, b_low, dims))


def lane_parts(value, group):
    high = value.astype(BF16).astype(F32)
    rest = value - high
    middle = rest.astype(BF16).astype(F32)
    low = rest - middle
    zero = jnp.zeros_like(value)
    return jnp.where(
        group == 0, high, jnp.where(group == 1, middle, jnp.where(group == 2, low, zero))
    ).astype(BF16)


def start_rows(code, first, rows):
    row_ids = lax.broadcasted_iota(jnp.int32, (rows, 128), 0) + first
    lane = lax.broadcasted_iota(jnp.int32, (rows, 128), 1)
    hashed = row_ids * 40503 + jnp.bitwise_and(lane, RANK - 1) * 1531 + code * 7919
    hashed = jnp.bitwise_xor(hashed, jnp.right_shift(hashed, 15)) * 668265261
    hashed = jnp.bitwise_xor(hashed, jnp.right_shift(hashed, 15)) * 374761393
    hashed = jnp.bitwise_xor(hashed, jnp.right_shift(hashed, 13))
    level = jnp.bitwise_and(hashed, 8388607).astype(F32)
    start = ((level + 0.5) / 8388608.0 - 0.5) * math.sqrt(12.0)
    return lane_parts(start, jnp.right_shift(lane, 5))


def norm_rows(hidden, gain, first, count):
    blocks = [pl.ds(pl.multiple_of(first + 32 * block, 32), 32) for block in range(count)]
    spans = [pl.ds(part * 128, 128) for part in range(D // 128)]
    means, scales = [], []
    for rows in blocks:
        total = hidden[rows, spans[0]].astype(F32)
        for span in spans[1:]:
            total = total + hidden[rows, span].astype(F32)
        means.append(jnp.sum(total, axis=1, keepdims=True) * (1.0 / D))
    for rows, mean in zip(blocks, means):
        total = jnp.zeros((32, 128), F32)
        for span in spans:
            centred = hidden[rows, span].astype(F32) - mean
            total = total + centred * centred
        scales.append(lax.rsqrt(jnp.sum(total, axis=1, keepdims=True) * (1.0 / D) + 1e-05))
    for rows, mean, scale in zip(blocks, means, scales):
        for span in spans:
            centred = hidden[rows, span].astype(F32) - mean
            hidden[rows, span] = (centred * scale * gain[:, span]).astype(BF16)


def front_kernel(
    codes, gain, hidden, probs, w_value, w_out, out_grad, err_out, err_value,
    mats_out, mats_value, left_out, own_half, other_half, gain_out, hidden_rows,
    hidden_v, probs_v, w_value_v, w_value_t, w_out_v, grad_v, err_out_v, err_value_v,
    starts, values_t, d_mixed_t, mixed_t, d_values_t, mats_out_v, mats_value_v, left_sum, gain_v,
    codes_v, gain_flat, gain_row, sems, out_sems, small_sems,
):
    half = TOK // 2
    halves = [pl.ds(part * half, half) for part in range(2)]
    pairs = (
        (hidden.at[halves[0]], hidden_v.at[halves[0]]),
        (w_out, w_out_v),
        (out_grad.at[halves[0]], grad_v.at[halves[0]]),
        (hidden.at[halves[1]], hidden_v.at[halves[1]]),
        (out_grad.at[halves[1]], grad_v.at[halves[1]]),
        (w_value, w_value_v),
        (probs, probs_v),
        (err_out.at[0], err_out_v),
        (err_value.at[0], err_value_v),
    )
    copies = [
        pltpu.make_async_copy(source, target, sems.at[index])
        for index, (source, target) in enumerate(pairs)
    ]
    small = (
        pltpu.make_async_copy(codes, codes_v, small_sems.at[0]),
        pltpu.make_async_copy(gain, gain_flat, small_sems.at[1]),
    )
    for copy in small:
        copy.start()
    for copy in copies[:4]:
        copy.start()
    index = lax.axis_index("tensor")
    rows_copy = pltpu.make_async_copy(
        hidden.at[pl.ds(pl.multiple_of(index * 128, 128), 128)], hidden_rows, out_sems.at[2 * STEPS]
    )

    def d_mixed_of(rows):
        d_mixed_t[:, rows] = dot(w_out_v[...], grad_v[rows, :], ((1,), (1,))).astype(BF16)

    for copy in small:
        copy.wait()
    @pl.loop(0, D // 128)
    def _(step):
        rows = pl.ds(pl.multiple_of(step * 128, 128), 128)
        for side in range(2):
            starts[side, rows, :] = start_rows(codes_v[side], step * 128, 128)

    for part in range(D // 128):
        span = pl.ds(part * 128, 128)
        gain_row[:, span] = gain_flat[span].reshape(1, 128)
    copies[0].wait()

    @pl.loop(0, half // LN_ROWS)
    def _(step):
        norm_rows(hidden_v, gain_row, step * LN_ROWS, LN_ROWS // 32)

    for copy in copies[4:6]:
        copy.start()
    for copy in copies[1:4]:
        copy.wait()
    for copy in copies[6:]:
        copy.start()
    rows_copy.start()

    @pl.loop(0, MERGE)
    def _(step):
        size = half // MERGE
        norm_rows(hidden_v, gain_row, half + step * size, size // 32)
        d_mixed_of(pl.ds(pl.multiple_of(step * size, size), size))

    for copy in copies[4:6]:
        copy.wait()

    @pl.loop(0, 2)
    def _(step):
        size = half // 2
        d_mixed_of(pl.ds(pl.multiple_of(half + step * size, size), size))
        for block in range(5):
            span = pl.ds(pl.multiple_of(step * 1280 + block * 256, 256), 256)
            w_value_t[:, span] = w_value_v[span, :].T

    for rows in halves:
        values_t[:, rows] = dot(w_value_t[...], hidden_v[rows, :], ((1,), (1,))).astype(BF16)

    copies[6].wait()
    for crop in range(CROPS):
        rows = pl.ds(crop * LEN, LEN)
        for head in range(HEADS_DEV):
            cols = pl.ds(head * HEAD_DIM, HEAD_DIM)
            weights = probs_v[crop, head]
            mixed_t[cols, rows] = dot(values_t[cols, rows], weights, ((1,), (1,))).astype(BF16)
            d_values_t[cols, rows] = dot(d_mixed_t[cols, rows], weights).astype(BF16)

    chip, core = place()
    for block in range(8):
        slot = pl.ds(pl.multiple_of(lax.rem(block // 2 - chip + 4, 4) * 128, 128), 128)
        part = d_values_t[:, pl.ds(block * 128, 128)]

        @pl.when(core == block % 2)
        def _():
            own_half[:, slot] = part

        @pl.when(core != block % 2)
        def _():
            other_half[:, slot] = part

    sides = (
        (copies[7], mixed_t, grad_v, err_out_v, mats_out_v, mats_out),
        (copies[8], d_values_t, hidden_v, err_value_v, mats_value_v, mats_value),
    )

    def write(index, step):
        span = pl.ds(step * TILE, TILE)
        mats_v, mats = sides[index][4:]
        return pltpu.make_async_copy(
            mats_v.at[:, span], mats.at[:, span], out_sems.at[index * STEPS + step]
        )

    for index, (copy, acts_t, other_side, err_v, mats_v, mats) in enumerate(sides):
        copy.wait()
        left_sum[...] = jnp.zeros((COLS, 128), F32)

        for step in range(STEPS):
            span = pl.ds(step * TILE, TILE)
            grad = dot(acts_t[...], other_side[:, span])
            rounded = (grad + err_v[:, span]).astype(BF16)
            mats_v[:, span] = rounded
            write(index, step).start()
            left_sum[...] += dot(rounded, starts[index, span, :])
            if index == 1:
                turned = w_value_t[:, span].astype(F32)
                gain_v[:, span] = jnp.sum(grad * turned, axis=0, keepdims=True) / gain_row[:, span]

        turned = left_sum[...].T
        left_out[pl.ds(index * RANK, RANK), :] = (
            turned[0:32] + (turned[32:64] + turned[64:96])
        ).astype(BF16)
    gain_out[...] = jnp.zeros((2 * RANK, 128), F32)
    for part in range(D // 128):
        gain_out[pl.ds(part // 3 * 8 + part % 3, 1), :] = gain_v[:, pl.ds(part * 128, 128)]

    for step in range(STEPS):
        for index in range(2):
            write(index, step).wait()
    rows_copy.wait()


def front(codes, gain, hidden, probs, w_value, w_out, out_grad, err_out, err_value):
    vmem = pl.BlockSpec(memory_space=pltpu.VMEM)
    return pl.pallas_call(
        front_kernel,
        name="front",
        out_shape=(
            jax.ShapeDtypeStruct((COLS, D), BF16),
            jax.ShapeDtypeStruct((COLS, D), BF16),
            jax.ShapeDtypeStruct((2 * RANK, COLS), BF16),
            jax.ShapeDtypeStruct((COLS, TOK // 2), BF16),
            jax.ShapeDtypeStruct((COLS, TOK // 2), BF16),
            jax.ShapeDtypeStruct((2 * RANK, 128), F32),
            jax.ShapeDtypeStruct((128, D), BF16),
        ),
        in_specs=[ANY] * 9,
        out_specs=(ANY, ANY, vmem, vmem, vmem, vmem, ANY),
        scratch_shapes=[
            pltpu.VMEM((TOK, D), BF16),
            pltpu.VMEM((CROPS, HEADS_DEV, LEN, LEN), BF16),
            pltpu.VMEM((D, COLS), BF16),
            pltpu.VMEM((COLS, D), BF16),
            pltpu.VMEM((COLS, D), BF16),
            pltpu.VMEM((TOK, D), BF16),
            pltpu.VMEM((COLS, D), F32),
            pltpu.VMEM((COLS, D), F32),
            pltpu.VMEM((2, D, 128), BF16),
            pltpu.VMEM((COLS, TOK), BF16),
            pltpu.VMEM((COLS, TOK), BF16),
            pltpu.VMEM((COLS, TOK), BF16),
            pltpu.VMEM((COLS, TOK), BF16),
            pltpu.VMEM((COLS, D), BF16),
            pltpu.VMEM((COLS, D), BF16),
            pltpu.VMEM((COLS, 128), F32),
            pltpu.VMEM((1, D), F32),
            pltpu.SMEM((2,), jnp.int32),
            pltpu.VMEM((D,), F32),
            pltpu.VMEM((1, D), F32),
            pltpu.SemaphoreType.DMA((9,)),
            pltpu.SemaphoreType.DMA((2 * STEPS + 1,)),
            pltpu.SemaphoreType.DMA((2,)),
        ],
        compiler_params=pltpu.CompilerParams(vmem_limit_bytes=48 * 2**20),
        cost_estimate=pl.CostEstimate(
            flops=11 * 10**9, bytes_accessed=32 * 10**6, transcendentals=0
        ),
    )(
        pltpu.with_memory_space_constraint(codes, pltpu.HBM),
        pltpu.with_memory_space_constraint(gain, pltpu.HBM),
        hidden, probs, w_value, w_out, out_grad, err_out, err_value,
    )


def branch_kernel(
    own_half, other_half, w_own, w_other, here, after, before, far_after, far_before, d_values
):
    @pl.when(pl.program_id(0) == 0)
    def _():
        for block in range(2):
            rows = pl.ds(block * 256, 256)
            d_values[rows, pl.ds(0, COLS)] = own_half[:, rows].T
            d_values[rows, pl.ds(COLS, COLS)] = other_half[:, rows].T

    weights = jnp.concatenate([w_own[...], w_other[...]], axis=1)
    product = dot(d_values[...], weights, ((1,), (1,))).astype(BF16)
    here[...] = product[0:128]
    after[...] = product[128:256]
    far_after[...] = product[256:320]
    far_before[...] = product[320:384]
    before[...] = product[384:512]


def branch(own_half, other_half, w_own, w_other):
    half = pl.BlockSpec((COLS, TOK // 2), lambda n: (0, 0))
    weights = pl.BlockSpec((1280, COLS), lambda n: (n, 0))
    rows = (128, 128, 128, 64, 64)
    return pl.pallas_call(
        branch_kernel,
        name="branch",
        grid=(2,),
        out_shape=[jax.ShapeDtypeStruct((count, D), BF16) for count in rows],
        in_specs=[half, half, weights, weights],
        out_specs=[pl.BlockSpec((count, 1280), lambda n: (0, n)) for count in rows],
        scratch_shapes=[pltpu.VMEM((TOK // 2, 2 * COLS), BF16)],
        compiler_params=pltpu.CompilerParams(vmem_limit_bytes=20 * 2**20),
        cost_estimate=pl.CostEstimate(
            flops=2 * 10**9, bytes_accessed=7 * 10**6, transcendentals=0
        ),
    )(
        own_half,
        other_half,
        pltpu.with_memory_space_constraint(w_own, pltpu.HBM),
        pltpu.with_memory_space_constraint(w_other, pltpu.HBM),
    )


def relay_kernel(after, before, far_after, far_before, next_after, next_before):
    top, low = pl.ds(0, 64), pl.ds(64, 64)
    next_after[top, :] = (after[top, :].astype(F32) + far_after[...].astype(F32)).astype(BF16)
    next_after[low, :] = after[low, :]
    next_before[top, :] = before[top, :]
    next_before[low, :] = (before[low, :].astype(F32) + far_before[...].astype(F32)).astype(BF16)


def relay(after, before, far_after, far_before):
    whole = pl.BlockSpec((128, 2560), lambda n: (0, n))
    part = pl.BlockSpec((64, 2560), lambda n: (0, n))
    return pl.pallas_call(
        relay_kernel,
        name="relay",
        grid=(1,),
        out_shape=(jax.ShapeDtypeStruct((128, D), BF16),) * 2,
        in_specs=[whole, whole, part, part],
        out_specs=(whole, whole),
        compiler_params=pltpu.CompilerParams(vmem_limit_bytes=8 * 2**20),
        cost_estimate=pl.CostEstimate(
            flops=10**6, bytes_accessed=4 * 10**6, transcendentals=0
        ),
    )(after, before, far_after, far_before)


def norm_back_kernel(hidden, gain, here, after, before, in_grad, total, standard):
    spans = [pl.ds(part * 128, 128) for part in range(D // 128)]
    for block in range(4):
        rows = pl.ds(block * 32, 32)
        mean = jnp.zeros((32, 128), F32)
        for span in spans:
            mean = mean + hidden[rows, span].astype(F32)
        mean = jnp.sum(mean, axis=1, keepdims=True) * (1.0 / D)
        square = jnp.zeros((32, 128), F32)
        for span in spans:
            centred = hidden[rows, span].astype(F32) - mean
            square = square + centred * centred
        inv_std = lax.rsqrt(jnp.sum(square, axis=1, keepdims=True) * (1.0 / D) + 1e-05)
        first = jnp.zeros((32, 128), F32)
        second = jnp.zeros((32, 128), F32)
        for span in spans:
            summed = here[rows, span].astype(F32) + (
                after[rows, span].astype(F32) + before[rows, span].astype(F32)
            )
            scaled = summed * gain[:, span]
            unit = (hidden[rows, span].astype(F32) - mean) * inv_std
            total[rows, span] = scaled
            standard[rows, span] = unit
            first = first + scaled
            second = second + scaled * unit
        first = jnp.sum(first, axis=1, keepdims=True) * (1.0 / D)
        second = jnp.sum(second, axis=1, keepdims=True) * (1.0 / D)
        for span in spans:
            in_grad[rows, span] = (
                inv_std * (total[rows, span] - first - standard[rows, span] * second)
            ).astype(BF16)


def norm_back(hidden, gain, here, after, before):
    rows = pl.BlockSpec((128, D), lambda n: (n, 0))
    return pl.pallas_call(
        norm_back_kernel,
        name="norm_back",
        grid=(1,),
        in_specs=[rows, pl.BlockSpec((1, D), lambda n: (0, 0)), rows, rows, rows],
        out_specs=rows,
        scratch_shapes=[pltpu.VMEM((128, D), F32), pltpu.VMEM((128, D), F32)],
        out_shape=jax.ShapeDtypeStruct((128, D), BF16),
        compiler_params=pltpu.CompilerParams(vmem_limit_bytes=16 * 2**20),
        cost_estimate=pl.CostEstimate(
            flops=5 * 10**6, bytes_accessed=10**6, transcendentals=0
        ),
    )(hidden, gain, here, after, before)


def right_kernel(left, gain_rows, mats_out, mats_value, own, other, staged):
    chip, core = place()
    step = pl.program_id(0)
    lanes = pl.ds(pl.multiple_of(step * 2560, 2560), 2560)

    def put(side, span, value):
        for block in range(4):
            rows = pl.ds(pl.multiple_of(lax.rem(block - chip + 4, 4) * 8, 8), 8)
            part = value[block * 8 : (block + 1) * 8]

            @pl.when(core == side)
            def _():
                own[rows, span] = part

            @pl.when(core != side)
            def _():
                staged[rows, span] = part

    for side, mats in enumerate((mats_out, mats_value)):
        span = pl.ds(side * RANK, RANK)
        rows = left[span, :]
        parts = jnp.concatenate(split2(rows), axis=0)
        product = dot(parts, mats[...])
        put(side, lanes, product[:RANK] + product[RANK:])

        @pl.when(step == 0)
        def _():
            gram = dot_split(rows, rows, ((1,), (1,)))
            packed = jnp.concatenate([gram[8 * k : 8 * k + 8] for k in range(4)], axis=1)
            put(side, pl.ds(D, 128), gain_rows[span, :])
            high, low = split2(packed)
            for place_at, part in ((SENT, high), (SENT + 128, low)):
                put(side, pl.ds(place_at, 128), jnp.concatenate([part.astype(F32)] * 4, axis=0))

    @pl.when(step == 0)
    def _():
        other[...] = staged[...].astype(BF16)


def right_terms(left, gain_rows, mats_out, mats_value):
    whole = pl.BlockSpec((RANK, WIDE), lambda n: (0, 0))
    mats = pl.BlockSpec((COLS, 2560), lambda n: (0, n))
    return pl.pallas_call(
        right_kernel,
        name="right_terms",
        grid=(1,),
        out_shape=(
            jax.ShapeDtypeStruct((RANK, WIDE), F32),
            jax.ShapeDtypeStruct((RANK, WIDE), BF16),
        ),
        in_specs=[
            pl.BlockSpec((2 * RANK, COLS), lambda n: (0, 0)),
            pl.BlockSpec((2 * RANK, 128), lambda n: (0, 0)),
            mats,
            mats,
        ],
        out_specs=(whole, whole),
        scratch_shapes=[pltpu.VMEM((RANK, WIDE), F32)],
        compiler_params=pltpu.CompilerParams(vmem_limit_bytes=16 * 2**20),
        cost_estimate=pl.CostEstimate(
            flops=5 * 10**8, bytes_accessed=5 * 10**6, transcendentals=0
        ),
    )(left, gain_rows, mats_out, mats_value)


def factor_kernel(packed, inverse):
    whole = packed[:, pl.ds(0, 128)] + packed[:, pl.ds(128, 128)]
    gram = jnp.concatenate([whole[:, k * RANK : (k + 1) * RANK] for k in range(4)], axis=0)
    row_ids = lax.broadcasted_iota(jnp.int32, (RANK, 128), 0)
    col_ids = lax.broadcasted_iota(jnp.int32, (RANK, 128), 1)
    unit = jnp.where(row_ids + RANK == col_ids, 1.0, 0.0)
    work = unit + jnp.concatenate([gram, jnp.zeros((RANK, 128 - RANK), F32)], axis=1)
    for step in range(0, RANK, 2):
        first, second = work[step : step + 1, :], work[step + 1 : step + 2, :]
        column = jnp.broadcast_to(work[:, step : step + 1], (RANK, 128))
        other = jnp.broadcast_to(work[:, step + 1 : step + 2], (RANK, 128))
        scale = 1.0 / column[step : step + 1, :]
        ratio = other[step : step + 1, :] * scale
        other = other - column * ratio
        second = second - first * ratio
        after = row_ids > step + 1
        work = jnp.where(row_ids == step + 1, second, work) - jnp.where(
            after,
            column * (first * scale) + other * (second / other[step + 1 : step + 2, :]),
            0.0,
        )
    diagonal = jnp.sum(jnp.where(row_ids == col_ids, work, 0.0), axis=1, keepdims=True)
    scaled = work * lax.rsqrt(diagonal)
    high, low = split2(pltpu.roll(scaled, 128 - RANK, 1))
    inverse[:, pl.ds(0, 128)] = high
    inverse[:, pl.ds(128, 128)] = low


def factor(packed):
    return pl.pallas_call(
        factor_kernel,
        name="factor",
        out_shape=jax.ShapeDtypeStruct((RANK, 256), BF16),
        cost_estimate=pl.CostEstimate(
            flops=5 * 10**6, bytes_accessed=3 * 10**6, transcendentals=0
        ),
    )(packed)


def finish_kernel(
    ours, theirs, left, mats_out, mats_value,
    err_out, err_value, share_out, share_value, ortho_out, ortho_value, gain_out,
    sums, ortho_parts, right,
):
    chip, core = place()
    step = pl.program_id(0)
    lanes = pl.ds(pl.multiple_of(step * 1280, 1280), 1280)

    @pl.when(step == 0)
    def _():
        for side, source in ((core, ours), (1 - core, theirs)):
            wide = source[...].astype(F32)
            for block in range(4):
                offset = lax.rem(chip + block, 4) * 8
                rows = pl.ds(pl.multiple_of(side * RANK + offset, 8), 8)
                sums[rows, pl.ds(0, SENT)] = wide[block * 8 : block * 8 + 8, :SENT]
            rows = pl.ds(pl.multiple_of(side * RANK, RANK), RANK)
            sums[rows, pl.ds(SENT, 128)] = wide[:, SENT : SENT + 128] + wide[:, SENT + 128 :]
        for part in range(D // 128):
            gain_out[:, pl.ds(part * 128, 128)] = sums[
                pl.ds(part // 3 * 8 + part % 3, 1), pl.ds(D, 128)
            ]
        for side, scaled in enumerate((ortho_out, ortho_value)):
            span = pl.ds(side * RANK, RANK)
            inverse = sums[span, pl.ds(SENT, 128)][:, :RANK]
            ortho = dot_split(inverse, left[span, :])
            scaled[...] = ortho * math.sqrt(HH)
            high, low = split2(ortho)
            parts = jnp.concatenate([high, low, high, jnp.zeros_like(high)], axis=0)
            ortho_parts[side] = parts.T

    for side, (mats, err) in enumerate(((mats_out, err_out), (mats_value, err_value))):
        span = pl.ds(side * RANK, RANK)
        inverse = sums[span, pl.ds(SENT, 128)][:, :RANK]
        rows = dot_split(inverse, sums[span, lanes]) * (1.0 / WORKERS)
        right[span, lanes] = rows
        high, low = split2(rows)
        parts = jnp.concatenate([high, high, low, jnp.zeros_like(high)], axis=0)
        err[0] = mats[...].astype(F32) - dot(ortho_parts[side], parts)

    @pl.when(step == 1)
    def _():
        index = chip * 2 + core
        window = right[:, pl.ds(pl.multiple_of(index * 5 // 2 * 128, 128), 512)]
        window = jnp.where(lax.rem(index, 2) == 1, pltpu.roll(window, 512 - 64, 1), window)
        share_out[...] = window[:RANK, : D // 8]
        share_value[...] = window[RANK:, : D // 8]


def finish(ours, theirs, left, mats_out, mats_value):
    whole = pl.BlockSpec((RANK, WIDE), lambda n: (0, 0))
    mats = pl.BlockSpec((COLS, 1280), lambda n: (0, n))
    err = pl.BlockSpec((1, COLS, 1280), lambda n: (0, 0, n))
    share = pl.BlockSpec((RANK, D // 8), lambda n: (0, 0))
    ortho = pl.BlockSpec((RANK, COLS), lambda n: (0, 0))
    return pl.pallas_call(
        finish_kernel,
        name="finish",
        grid=(2,),
        out_shape=(
            jax.ShapeDtypeStruct((1, COLS, D), F32),
            jax.ShapeDtypeStruct((1, COLS, D), F32),
            jax.ShapeDtypeStruct((RANK, D // 8), F32),
            jax.ShapeDtypeStruct((RANK, D // 8), F32),
            jax.ShapeDtypeStruct((RANK, COLS), F32),
            jax.ShapeDtypeStruct((RANK, COLS), F32),
            jax.ShapeDtypeStruct((1, D), F32),
        ),
        in_specs=[
            whole, whole, pl.BlockSpec((2 * RANK, COLS), lambda n: (0, 0)), mats, mats,
        ],
        out_specs=(
            err, err, share, share, ortho, ortho, pl.BlockSpec((1, D), lambda n: (0, 0)),
        ),
        scratch_shapes=[
            pltpu.VMEM((2 * RANK, WIDE), F32),
            pltpu.VMEM((2, COLS, 4 * RANK), BF16),
            pltpu.VMEM((2 * RANK, WIDE), F32),
        ],
        compiler_params=pltpu.CompilerParams(vmem_limit_bytes=20 * 2**20),
        cost_estimate=pl.CostEstimate(
            flops=1 * 10**9, bytes_accessed=13 * 10**6, transcendentals=0
        ),
    )(ours, theirs, left, mats_out, mats_value)


def to_core(value):
    return lax.ppermute(value, "tensor", [(i, i ^ 1) for i in range(8)])


def to_x(value, hops):
    return lax.ppermute(value, "tensor", [(i, (i // 2 + hops) % 4 * 2 + i % 2) for i in range(8)])


def to_z(value, hops):
    return lax.ppermute(value, "dp", [(i, i // 4 * 4 + (i + hops) % 4) for i in range(16)])


def to_y(value, hops):
    return lax.ppermute(value, "dp", [(i, (i // 4 + hops) % 4 * 4 + i % 4) for i in range(16)])


def rounded(value):
    return lax.reduce_precision(value, 8, 7).astype(BF16)


def ring_sum(value, send):
    opposite, after, before = send(value, 2), send(value, 1), send(value, 3)
    wide = value.astype(F32)
    return (wide + opposite.astype(F32)) + (after.astype(F32) + before.astype(F32))


def local(
    hidden_in, ln_gain, attn_probs, w_value, w_out, out_grad, err_out, err_value, factor_codes
):
    gain_row = ln_gain.reshape(1, D)
    w_other = to_core(w_value)
    mats_out, mats_value, left_term, own_half, other_half, gain_rows, hidden_rows = front(
        factor_codes, ln_gain, hidden_in, attn_probs, w_value, w_out, out_grad,
        err_out, err_value,
    )
    received_half = to_core(other_half)

    left = ring_sum(left_term, to_z)
    here, after, before, far_after, far_before = branch(own_half, received_half, w_value, w_other)
    left_term, far_after, far_before = lax.optimization_barrier(
        (rounded(left), far_after, far_before)
    )
    far_after, far_before = to_x(far_after, 1), to_x(far_before, 3)
    passes = 1 + lax.axis_index("dp") // WORKERS

    def sum_left(step, carry):
        left = ring_sum(carry[0], to_y)
        return rounded(left), left

    _, left = lax.fori_loop(
        0, passes, sum_left, (left_term, jnp.zeros((2 * RANK, COLS), F32))
    )
    left, far_after, far_before = lax.optimization_barrier((left, far_after, far_before))

    ours, theirs = right_terms(left, gain_rows, mats_out, mats_value)
    chunks = ours + to_core(theirs).astype(F32)
    next_after, next_before = relay(after, before, far_after, far_before)
    grams = chunks[:, SENT : SENT + 128] + chunks[:, SENT + 128 :]
    high = lax.reduce_precision(grams, 8, 7)
    chunks = jnp.concatenate([chunks[:, :SENT], high, grams - high], axis=1)
    opposite, after, before = (
        to_x(rounded(chunks[8 * k : 8 * k + 8]), k).astype(F32) for k in (2, 1, 3)
    )
    chunk = (chunks[:8] + opposite) + (after + before)
    packed = chunk[:, SENT:]
    chunk, next_after, next_before = lax.optimization_barrier(
        (rounded(chunk[:, :SENT]), next_after, next_before)
    )
    near_after, near_before = to_x(next_after, 1), to_x(next_before, 3)

    def over_workers(step, carry):
        chunk, _ = carry
        inverse = factor(packed)
        chunk = ring_sum(chunk, to_z)
        chunk, inverse = lax.optimization_barrier((chunk, inverse))
        return rounded(ring_sum(rounded(chunk), to_y)), inverse

    chunk, inverse = lax.fori_loop(
        0, passes, over_workers, (chunk, jnp.zeros((RANK, 256), BF16))
    )
    chunk, near_after, near_before = lax.optimization_barrier((chunk, near_after, near_before))
    in_grad = norm_back(hidden_rows, gain_row, here, near_after, near_before)
    opposite, after, before = to_x(chunk, 2), to_x(chunk, 3), to_x(chunk, 1)
    rows = jnp.concatenate([chunk, after, opposite, before], axis=0)
    ours = jnp.concatenate([rows, inverse], axis=1)
    theirs, in_grad = lax.optimization_barrier((to_core(ours), in_grad))
    new_out, new_value, share_out, share_value, ortho_out, ortho_value, gain_grad = finish(
        ours, theirs, left, mats_out, mats_value
    )
    return (
        in_grad,
        gain_grad.reshape(D),
        new_out,
        new_value,
        ortho_out.T,
        ortho_value.T,
        share_out.T,
        share_value.T,
    )


def solution(mesh):
    in_specs = (
        P("dp", None),
        P(),
        P("dp", "tensor", None, None),
        P(None, "tensor"),
        P("tensor", None),
        P("dp", None),
        P("dp", "tensor", None),
        P("dp", "tensor", None),
        P(),
    )
    out_specs = (
        P(("dp", "tensor"), None),
        P(),
        P("dp", "tensor", None),
        P("dp", "tensor", None),
        P("tensor", None),
        P("tensor", None),
        P("tensor", None),
        P("tensor", None),
    )
    return jax.shard_map(local, mesh=mesh, in_specs=in_specs, out_specs=out_specs, check_vma=False)
```

time: 153 us -> 116 us (0.76)
  other arithmetic: 13.9 us -> 2.25 us
  local copies, waits for them, and re-layouts: 21.2 us -> 9.97 us
  waiting for transfers between devices: 29.7 us -> 19.9 us
  Pallas kernels: 50.5 us -> 47 us
  starting transfers between devices: 35.9 us -> 34 us
    ppermute x10, waiting for transfers between devices: 19.4 us -> 5.49 us  [to_x(): lax.ppermute(value, 'tensor', [(i, (i // 2 + hops) % 4 * 2 + i % 2) for i...]
    unnamed x44 -> x22, local copies, waits for them, and re-layouts: 17.5 us -> 7.97 us
    pallas_call x5 -> x6, Pallas kernels: 27.5 us -> 21.1 us  [the longest x1 5.74 us: finish(): pl.pallas_call(finish_kernel, name='finish', grid=(2,), out_shape=(jax.Sh...]
    convert_element_type x4 -> x6, other arithmetic: 7.07 us -> 0.76 us  [rounded(): return lax.reduce_precision(value, 8, 7).astype(BF16)]
    reduce_sum x3 -> x0, other arithmetic: 4.92 us -> none  [the longest x1 2.11 us: local(): first_mean = jnp.mean(scaled, axis=-1, keepdims=True)]
    ppermute x6, waiting for transfers between devices: 3.45 us -> 6.49 us  [to_z(): lax.ppermute(value, 'dp', [(i, i // 4 * 4 + (i + hops) % 4) for i in rang...]
    pallas_call x1, Pallas kernels: 22.9 us -> 25.9 us  [front(): pl.pallas_call(front_kernel, name='front', out_shape=(jax.ShapeDtypeStruc...]
    ppermute x10, starting transfers between devices: 15.6 us -> 13.7 us  [to_x(): lax.ppermute(value, 'tensor', [(i, (i // 2 + hops) % 4 * 2 + i % 2) for i...]
  transfers between devices with their start and end apart: 25 -> 26, of which waited for: 14 -> 13; matrix products, arithmetic and copies ran while one was open for 7% -> 2% of each run, Pallas kernels for 15% -> 30%
where the time goes in v2:
time: 116 us; the launch traced here: 114 us
  Pallas kernels  47 us (41%)
  starting transfers between devices  34 us (29%)
  waiting for transfers between devices  19.9 us (17%)
  local copies, waits for them, and re-layouts  9.97 us (9%)
  other arithmetic  2.25 us (2%)
    pallas_call x1, Pallas kernels, front(): pl.pallas_call(front_kernel, name='front', out_shape=(jax.ShapeDtypeStruc...  25.9 us
    ppermute x10, starting transfers between devices, to_x(): lax.ppermute(value, 'tensor', [(i, (i // 2 + hops) % 4 * 2 + i % 2) for i...  13.7 us
    ppermute x6, starting transfers between devices, to_z(): lax.ppermute(value, 'dp', [(i, i // 4 * 4 + (i + hops) % 4) for i in rang...  9.84 us
    ppermute x6, starting transfers between devices, to_y(): lax.ppermute(value, 'dp', [(i, (i // 4 + hops) % 4 * 4 + i % 4) for i in...  9.43 us
    unnamed x22, local copies, waits for them, and re-layouts  7.97 us
    ppermute x6, waiting for transfers between devices, to_y(): lax.ppermute(value, 'dp', [(i, (i // 4 + hops) % 4 * 4 + i % 4) for i in...  6.52 us
    ppermute x6, waiting for transfers between devices, to_z(): lax.ppermute(value, 'dp', [(i, i // 4 * 4 + (i + hops) % 4) for i in rang...  6.49 us
    pallas_call x1, Pallas kernels, finish(): pl.pallas_call(finish_kernel, name='finish', grid=(2,), out_shape=(jax.Sh...  5.74 us
  transfers between devices with their start and end apart: 26, of which 13 were waited for; matrix products, arithmetic and copies ran while one was open for 2% of the time, Pallas kernels for 30%

profile of v2, /device:TPU:0, one launch (start us, length us, event | category | flops | bytes accessed | tf_op | source)
XLA Modules:
  0.0 114.0 jit_solution(6445818192186622190)
XLA Ops:
  0.7 25.9 %front.1 = (bf16[384,2560]{1,0:T(8,128)(2,1)S(1)}, bf16[384,2560]{1,0:T(8,128)(2,1)S(1)}, bf16[64,384]{1,0:T(8,128)(2,1)S(1)}, bf16[384,512]{1,0:T(8,128)(2,1)S(...) custom-call(s32[2]{0:T(128)} %codes.1, f32[2560]{0:T(1024)} %gain.1, ...), custom_call_target="tpu_custom_call" | custom-call | flops 11000000512 | bytes 32000000 | tf_op jit(solution)/shard_map/front/pallas_call | solution.py:247
  29.2 4.1 %collective-permute-start.11 = (bf16[64,384]{1,0:T(8,128)(2,1)S(1)}, bf16[64,384]{1,0:T(8,128)(2,1)S(1)}, u32[]{:S(2)}, u32[]{:S(2)}) collective-permute-start(bf16[64,384]{1,0:T(8,128)(2,1)S(1)} %get-tuple-element.97), channel_id=1, source_target_pairs={{0,24},{8,0},{16,8},{24,16},{32,56},{40,32},{48,40},{56,48},{64,88... | collective-permute-start | bytes 147464 | tf_op jit(solution)/shard_map/ppermute | solution.py:615
  33.3 1.9 %collective-permute-start.9 = (bf16[64,384]{1,0:T(8,128)(2,1)S(1)}, bf16[64,384]{1,0:T(8,128)(2,1)S(1)}, u32[]{:S(2)}, u32[]{:S(2)}) collective-permute-start(bf16[64,384]{1,0:T(8,128)(2,1)S(1)} %get-tuple-element.97), channel_id=1, source_target_pairs={{0,16},{8,24},{16,0},{24,8},{32,48},{40,56},{48,32},{56,40},{64,80... | collective-permute-start | bytes 147464 | tf_op jit(solution)/shard_map/ppermute | solution.py:615
  35.2 4.0 %collective-permute-done.10 = bf16[64,384]{1,0:T(8,128)(2,1)S(1)} collective-permute-done((bf16[64,384]{1,0:T(8,128)(2,1)S(1)}, bf16[64,384]{1,0:T(8,128)(2,1)S(1)}, u32[]{:S(2)}, u32[]{:S(2)}) %collective-permute-start.10) | collective-permute-done | bytes 49184 | tf_op jit(solution)/shard_map/ppermute | solution.py:615
  41.9 5.1 %branch.1 = (bf16[128,2560]{1,0:T(8,128)(2,1)S(1)}, bf16[128,2560]{1,0:T(8,128)(2,1)S(1)}, bf16[128,2560]{1,0:T(8,128)(2,1)S(1)}, bf16[64,2560]{1,0:T(8,128)(2,1)}, bf16[64,2560]{1,0:T(8,128)(2,1)}) custom-call(bf16[384,512]{1,0:T(8,128)(2,1)S(1)} %copy-done.10, bf16[384,512]{1,0:T(8,128)(2,1)S(1)} %copy-done.8, bf16[2560,384]{1,0:T(8,128)(2,1)} %w_own.1, ...), custom_call_target="tpu_custom_call" | custom-call | flops 2000000000 | bytes 7000000 | tf_op jit(solution)/shard_map/branch/pallas_call | solution.py:320
  50.2 1.7 %collective-permute-start.15 = (bf16[64,2560]{1,0:T(8,128)(2,1)}, bf16[64,2560]{1,0:T(8,128)(2,1)}, u32[]{:S(2)}, u32[]{:S(2)}) collective-permute-start(bf16[64,2560]{1,0:T(8,128)(2,1)} %get-tuple-element.105), channel_id=1, source_target_pairs={{0,6},{1,7},{2,0},{3,1},{4,2},{5,3},{6,4},{7,5},{8,14},{9,15},{10,... | collective-permute-start | bytes 983048 | tf_op jit(solution)/shard_map/ppermute | solution.py:611
  52.6 9.8 %while.24 = (s32[]{:T(128)}, bf16[64,384]{1,0:T(8,128)(2,1)S(1)}, f32[64,384]{1,0:T(8,128)}, s32[]{:T(128)}, s32[]{:T(128)}) while((s32[]{:T(128)}, bf16[64,384]{1,0:T(8,128)(2,1)S(1)}, f32[64,384]{1,0:T(8,128)}, s32[]{:T(128)}, s32[]{:T(128)}) %tuple.54), condition=%wide.region_1.2_spmd, body=%wide.region_0.1_spmd.sunk | while | flops 221186 | bytes 934069 | solution.py:655
  52.6 3.0 %collective-permute-start = (bf16[64,384]{1,0:T(8,128)(2,1)S(1)}, bf16[64,384]{1,0:T(8,128)(2,1)S(1)}, u32[]{:S(2)}, u32[]{:S(2)}) collective-permute-start(bf16[64,384]{1,0:T(8,128)(2,1)S(1)} %get-tuple-element.230), channel_id=1, source_target_pairs={{0,96},{8,104},{16,112},{24,120},{32,0},{40,8},{48,16},{56,24},{64... | collective-permute-start | bytes 147464 | tf_op jit(solution)/shard_map/while/body/ppermute | solution.py:619
  57.3 3.9 %collective-permute-done.2 = bf16[64,384]{1,0:T(8,128)(2,1)S(1)} collective-permute-done((bf16[64,384]{1,0:T(8,128)(2,1)S(1)}, bf16[64,384]{1,0:T(8,128)(2,1)S(1)}, u32[]{:S(2)}, u32[]{:S(2)}) %collective-permute-start.2) | collective-permute-done | bytes 49184 | tf_op jit(solution)/shard_map/while/body/ppermute | solution.py:619
  63.9 2.5 %right_terms.1 = (f32[32,2944]{1,0:T(8,128)S(1)}, bf16[32,2944]{1,0:T(8,128)(2,1)S(1)}) custom-call(f32[64,384]{1,0:T(8,128)} %get-tuple-element.106.left, f32[64,128]{1,0:T(8,128)S(1)} %get-tuple-element.107.gain_rows, bf16[384,2560]{1,0:T(8,128)(2,1)S(1)} %get-tuple-element.108.mats_out, bf16[384,2560]{1,0:T(8,128)(2,1)S(1)} %copy-done.1), custom_call_target="tpu_custom_call" | custom-call | flops 500000000 | bytes 5000000 | tf_op jit(solution)/shard_map/right_terms/pallas_call | solution.py:457
  68.3 1.9 %collective-permute-start.17 = (bf16[8,2944]{1,0:T(8,128)(2,1)S(1)}, bf16[8,2944]{1,0:T(8,128)(2,1)S(1)}, u32[]{:S(2)}, u32[]{:S(2)}) collective-permute-start(bf16[8,2944]{1,0:T(8,128)(2,1)S(1)} %get-tuple-element.157), channel_id=1, source_target_pairs={{0,4},{1,5},{2,6},{3,7},{4,0},{5,1},{6,2},{7,3},{8,12},{9,13},{10,... | collective-permute-start | bytes 141320 | tf_op jit(solution)/shard_map/ppermute | solution.py:611
  72.2 2.2 %relay.1 = (bf16[128,2560]{1,0:T(8,128)(2,1)}, bf16[128,2560]{1,0:T(8,128)(2,1)}) custom-call(bf16[128,2560]{1,0:T(8,128)(2,1)S(1)} %copy-done.4, bf16[128,2560]{1,0:T(8,128)(2,1)S(1)} %copy-done.6, bf16[64,2560]{1,0:T(8,128)(2,1)} %collective-permute-done.14.far_after, bf16[64,2560]{1,0:T(8,128)(2,1)} %collective-permute-done.15.far_before), custom_call_target="tpu_custom_call" | custom-call | flops 1000000 | bytes 4000000 | tf_op jit(solution)/shard_map/relay/pallas_call | solution.py:351
  74.5 2.2 %collective-permute-done.18 = bf16[8,2944]{1,0:T(8,128)(2,1)S(1)} collective-permute-done((bf16[8,2944]{1,0:T(8,128)(2,1)S(1)}, bf16[8,2944]{1,0:T(8,128)(2,1)S(1)}, u32[]{:S(2)}, u32[]{:S(2)}) %collective-permute-start.18) | collective-permute-done | bytes 47136 | tf_op jit(solution)/shard_map/ppermute | solution.py:611
  76.8 3.2 %collective-permute-start.21 = (bf16[128,2560]{1,0:T(8,128)(2,1)}, bf16[128,2560]{1,0:T(8,128)(2,1)}, u32[]{:S(2)}, u32[]{:S(2)}) collective-permute-start(bf16[128,2560]{1,0:T(8,128)(2,1)} %get-tuple-element.121), channel_id=1, source_target_pairs={{0,6},{1,7},{2,0},{3,1},{4,2},{5,3},{6,4},{7,5},{8,14},{9,15},{10,... | collective-permute-start | bytes 1966088 | tf_op jit(solution)/shard_map/ppermute | solution.py:611
  80.6 15.6 %while.25 = (s32[]{:T(128)}, bf16[8,2688]{1,0:T(8,128)(2,1)S(1)}, bf16[32,256]{1,0:T(8,128)(2,1)}, s32[]{:T(128)}, f32[8,256]{1,0:T(8,128)S(1)}, /*index=5*/s32[]{:T(128)}) while((s32[]{:T(128)}, bf16[8,2688]{1,0:T(8,128)(2,1)S(1)}, bf16[32,256]{1,0:T(8,128)(2,1)}, s32[]{:T(128)}, f32[8,256]{1,0:T(8,128)S(1)}, /*index=5*/s32[]{:T(128)}) %tuple.57), condition=%wide.region_3.4_spmd, body=%wide.region_2.3_spmd.sunk | while | flops 5430082 | bytes 4677621 | solution.py:683
  80.6 3.0 %collective-permute-start.3 = (bf16[8,2688]{1,0:T(8,128)(2,1)S(1)}, bf16[8,2688]{1,0:T(8,128)(2,1)S(1)}, u32[]{:S(2)}, u32[]{:S(2)}) collective-permute-start(bf16[8,2688]{1,0:T(8,128)(2,1)S(1)} %get-tuple-element.246), channel_id=1, source_target_pairs={{0,24},{8,0},{16,8},{24,16},{32,56},{40,32},{48,40},{56,48},{64,88... | collective-permute-start | bytes 129032 | tf_op jit(solution)/shard_map/while/body/ppermute | solution.py:615
  84.5 2.3 %factor.1 = bf16[32,256]{1,0:T(8,128)(2,1)} custom-call(f32[8,256]{1,0:T(8,128)S(1)} %get-tuple-element.255.packed), custom_call_target="tpu_custom_call" | custom-call | flops 5000000 | bytes 3000000 | tf_op jit(solution)/shard_map/while/body/factor/pallas_call | solution.py:509
  86.8 2.5 %collective-permute-done.5 = bf16[8,2688]{1,0:T(8,128)(2,1)S(1)} collective-permute-done((bf16[8,2688]{1,0:T(8,128)(2,1)S(1)}, bf16[8,2688]{1,0:T(8,128)(2,1)S(1)}, u32[]{:S(2)}, u32[]{:S(2)}) %collective-permute-start.5) | collective-permute-done | bytes 43040 | tf_op jit(solution)/shard_map/while/body/ppermute | solution.py:615
  89.3 1.6 %collective-permute-start.8 = (bf16[8,2688]{1,0:T(8,128)(2,1)S(1)}, bf16[8,2688]{1,0:T(8,128)(2,1)S(1)}, u32[]{:S(2)}, u32[]{:S(2)}) collective-permute-start(bf16[8,2688]{1,0:T(8,128)(2,1)S(1)} %reduce-precision_convert_fusion.8), channel_id=1, source_target_pairs={{0,64},{8,72},{16,80},{24,88},{32,96},{40,104},{48,112},{56,120},{... | collective-permute-start | bytes 129032 | tf_op jit(solution)/shard_map/while/body/ppermute | solution.py:619
  90.9 3.2 %collective-permute-start.6 = (bf16[8,2688]{1,0:T(8,128)(2,1)S(1)}, bf16[8,2688]{1,0:T(8,128)(2,1)S(1)}, u32[]{:S(2)}, u32[]{:S(2)}) collective-permute-start(bf16[8,2688]{1,0:T(8,128)(2,1)S(1)} %reduce-precision_convert_fusion.8), channel_id=1, source_target_pairs={{0,96},{8,104},{16,112},{24,120},{32,0},{40,8},{48,16},{56,24},{64... | collective-permute-start | bytes 129032 | tf_op jit(solution)/shard_map/while/body/ppermute | solution.py:619
  97.8 1.8 %collective-permute-start.22 = (bf16[8,2688]{1,0:T(8,128)(2,1)S(1)}, bf16[8,2688]{1,0:T(8,128)(2,1)S(1)}, u32[]{:S(2)}, u32[]{:S(2)}) collective-permute-start(bf16[8,2688]{1,0:T(8,128)(2,1)S(1)} %get-tuple-element.122), channel_id=1, source_target_pairs={{0,6},{1,7},{2,0},{3,1},{4,2},{5,3},{6,4},{7,5},{8,14},{9,15},{10,... | collective-permute-start | bytes 129032 | tf_op jit(solution)/shard_map/ppermute | solution.py:611
  99.5 2.0 %collective-permute-done.24 = bf16[8,2688]{1,0:T(8,128)(2,1)S(1)} collective-permute-done((bf16[8,2688]{1,0:T(8,128)(2,1)S(1)}, bf16[8,2688]{1,0:T(8,128)(2,1)S(1)}, u32[]{:S(2)}, u32[]{:S(2)}) %collective-permute-start.24) | collective-permute-done | bytes 43040 | tf_op jit(solution)/shard_map/ppermute | solution.py:611
  104.4 3.2 %norm_back.1 = bf16[128,2560]{1,0:T(8,128)(2,1)} custom-call(bf16[128,2560]{1,0:T(8,128)(2,1)S(1)} %get-tuple-element.124.hidden, f32[1,2560]{1,0:T(1,128)S(1)} %reshape.22.gain, bf16[128,2560]{1,0:T(8,128)(2,1)S(1)} %get-tuple-element.125.here, bf16[128,2560]{1,0:T(8,128)(2,1)} %collective-permute-done.20.after, ...), custom_call_target="tpu_custom_call" | custom-call | flops 5000000 | bytes 1000000 | tf_op jit(solution)/shard_map/norm_back/pallas_call | solution.py:400
  107.6 5.7 %finish.1 = (f32[1,384,2560]{2,1,0:T(8,128)}, f32[1,384,2560]{2,1,0:T(8,128)}, f32[32,320]{1,0:T(8,128)}, f32[32,320]{1,0:T(8,128)}, f32[32,384]{1,0:T(8,128)}, ...) custom-call(bf16[32,2944]{1,0:T(8,128)(2,1)S(1)} %pad_maximum_fusion.1.ours, ...), custom_call_target="tpu_custom_call" | custom-call | flops 1000000000 | bytes 13000000 | tf_op jit(solution)/shard_map/finish/pallas_call | solution.py:575
  (77 shorter events, 26.3 us)
Async XLA Ops:
  0.6 39.3 %collective-permute-start.13 = (bf16[2560,384]{1,0:T(8,128)(2,1)}, bf16[2560,384]{1,0:T(8,128)(2,1)}, u32[]{:S(2)}, u32[]{:S(2)}) collective-permute-start(bf16[2560,384]{1,0:T(8,128)(2,1)} %w_own.1), channel_id=1, source_target_pairs={{0,1},{1,0},{2,3},{3,2},{4,5},{5,4},{6,7},{7,6},{8,9},{9,8},{10,11... | collective-permute-start | bytes 5898248 | tf_op jit(solution)/shard_map/ppermute | solution.py:607
  28.7 10.5 %collective-permute-start.12 = (bf16[384,512]{1,0:T(8,128)(2,1)}, bf16[384,512]{1,0:T(8,128)(2,1)S(1)}, u32[]{:S(2)}, u32[]{:S(2)}) collective-permute-start(bf16[384,512]{1,0:T(8,128)(2,1)} %get-tuple-element.99), channel_id=1, source_target_pairs={{0,1},{1,0},{2,3},{3,2},{4,5},{5,4},{6,7},{7,6},{8,9},{9,8},{10,11... | collective-permute-start | bytes 1179656 | tf_op jit(solution)/shard_map/ppermute | solution.py:607
  29.2 6.0 %collective-permute-start.11 = (bf16[64,384]{1,0:T(8,128)(2,1)S(1)}, bf16[64,384]{1,0:T(8,128)(2,1)S(1)}, u32[]{:S(2)}, u32[]{:S(2)}) collective-permute-start(bf16[64,384]{1,0:T(8,128)(2,1)S(1)} %get-tuple-element.97), channel_id=1, source_target_pairs={{0,24},{8,0},{16,8},{24,16},{32,56},{40,32},{48,40},{56,48},{64,88... | collective-permute-start | bytes 147464 | tf_op jit(solution)/shard_map/ppermute | solution.py:615
  33.3 5.8 %collective-permute-start.10 = (bf16[64,384]{1,0:T(8,128)(2,1)S(1)}, bf16[64,384]{1,0:T(8,128)(2,1)S(1)}, u32[]{:S(2)}, u32[]{:S(2)}) collective-permute-start(bf16[64,384]{1,0:T(8,128)(2,1)S(1)} %get-tuple-element.97), channel_id=1, source_target_pairs={{0,8},{8,16},{16,24},{24,0},{32,40},{40,48},{48,56},{56,32},{64,72... | collective-permute-start | bytes 147464 | tf_op jit(solution)/shard_map/ppermute | solution.py:615
  33.3 5.8 %collective-permute-start.9 = (bf16[64,384]{1,0:T(8,128)(2,1)S(1)}, bf16[64,384]{1,0:T(8,128)(2,1)S(1)}, u32[]{:S(2)}, u32[]{:S(2)}) collective-permute-start(bf16[64,384]{1,0:T(8,128)(2,1)S(1)} %get-tuple-element.97), channel_id=1, source_target_pairs={{0,16},{8,24},{16,0},{24,8},{32,48},{40,56},{48,32},{56,40},{64,80... | collective-permute-start | bytes 147464 | tf_op jit(solution)/shard_map/ppermute | solution.py:615
  48.7 13.7 %collective-permute-start.14 = (bf16[64,2560]{1,0:T(8,128)(2,1)}, bf16[64,2560]{1,0:T(8,128)(2,1)}, u32[]{:S(2)}, u32[]{:S(2)}) collective-permute-start(bf16[64,2560]{1,0:T(8,128)(2,1)} %get-tuple-element.104), channel_id=1, source_target_pairs={{0,2},{1,3},{2,4},{3,5},{4,6},{5,7},{6,0},{7,1},{8,10},{9,11},{10,... | collective-permute-start | bytes 983048 | tf_op jit(solution)/shard_map/ppermute | solution.py:611
  50.2 12.2 %collective-permute-start.15 = (bf16[64,2560]{1,0:T(8,128)(2,1)}, bf16[64,2560]{1,0:T(8,128)(2,1)}, u32[]{:S(2)}, u32[]{:S(2)}) collective-permute-start(bf16[64,2560]{1,0:T(8,128)(2,1)} %get-tuple-element.105), channel_id=1, source_target_pairs={{0,6},{1,7},{2,0},{3,1},{4,2},{5,3},{6,4},{7,5},{8,14},{9,15},{10,... | collective-permute-start | bytes 983048 | tf_op jit(solution)/shard_map/ppermute | solution.py:611
  52.6 4.8 %collective-permute-start = (bf16[64,384]{1,0:T(8,128)(2,1)S(1)}, bf16[64,384]{1,0:T(8,128)(2,1)S(1)}, u32[]{:S(2)}, u32[]{:S(2)}) collective-permute-start(bf16[64,384]{1,0:T(8,128)(2,1)S(1)} %get-tuple-element.230), channel_id=1, source_target_pairs={{0,96},{8,104},{16,112},{24,120},{32,0},{40,8},{48,16},{56,24},{64... | collective-permute-start | bytes 147464 | tf_op jit(solution)/shard_map/while/body/ppermute | solution.py:619
  55.6 5.6 %collective-permute-start.2 = (bf16[64,384]{1,0:T(8,128)(2,1)S(1)}, bf16[64,384]{1,0:T(8,128)(2,1)S(1)}, u32[]{:S(2)}, u32[]{:S(2)}) collective-permute-start(bf16[64,384]{1,0:T(8,128)(2,1)S(1)} %get-tuple-element.230), channel_id=1, source_target_pairs={{0,64},{8,72},{16,80},{24,88},{32,96},{40,104},{48,112},{56,120},{... | collective-permute-start | bytes 147464 | tf_op jit(solution)/shard_map/while/body/ppermute | solution.py:619
  56.2 5.5 %collective-permute-start.1 = (bf16[64,384]{1,0:T(8,128)(2,1)S(1)}, bf16[64,384]{1,0:T(8,128)(2,1)S(1)}, u32[]{:S(2)}, u32[]{:S(2)}) collective-permute-start(bf16[64,384]{1,0:T(8,128)(2,1)S(1)} %get-tuple-element.230), channel_id=1, source_target_pairs={{0,32},{8,40},{16,48},{24,56},{32,64},{40,72},{48,80},{56,88},{64,... | collective-permute-start | bytes 147464 | tf_op jit(solution)/shard_map/while/body/ppermute | solution.py:619
  68.3 6.1 %collective-permute-start.17 = (bf16[8,2944]{1,0:T(8,128)(2,1)S(1)}, bf16[8,2944]{1,0:T(8,128)(2,1)S(1)}, u32[]{:S(2)}, u32[]{:S(2)}) collective-permute-start(bf16[8,2944]{1,0:T(8,128)(2,1)S(1)} %get-tuple-element.157), channel_id=1, source_target_pairs={{0,4},{1,5},{2,6},{3,7},{4,0},{5,1},{6,2},{7,3},{8,12},{9,13},{10,... | collective-permute-start | bytes 141320 | tf_op jit(solution)/shard_map/ppermute | solution.py:611
  70.2 4.3 %collective-permute-start.19 = (bf16[8,2944]{1,0:T(8,128)(2,1)S(1)}, bf16[8,2944]{1,0:T(8,128)(2,1)S(1)}, u32[]{:S(2)}, u32[]{:S(2)}) collective-permute-start(bf16[8,2944]{1,0:T(8,128)(2,1)S(1)} %get-tuple-element.158), channel_id=1, source_target_pairs={{0,6},{1,7},{2,0},{3,1},{4,2},{5,3},{6,4},{7,5},{8,14},{9,15},{10,... | collective-permute-start | bytes 141320 | tf_op jit(solution)/shard_map/ppermute | solution.py:611
  71.4 5.3 %collective-permute-start.18 = (bf16[8,2944]{1,0:T(8,128)(2,1)S(1)}, bf16[8,2944]{1,0:T(8,128)(2,1)S(1)}, u32[]{:S(2)}, u32[]{:S(2)}) collective-permute-start(bf16[8,2944]{1,0:T(8,128)(2,1)S(1)} %get-tuple-element.159), channel_id=1, source_target_pairs={{0,2},{1,3},{2,4},{3,5},{4,6},{5,7},{6,0},{7,1},{8,10},{9,11},{10,... | collective-permute-start | bytes 141320 | tf_op jit(solution)/shard_map/ppermute | solution.py:611
  76.7 19.5 %collective-permute-start.20 = (bf16[128,2560]{1,0:T(8,128)(2,1)}, bf16[128,2560]{1,0:T(8,128)(2,1)}, u32[]{:S(2)}, u32[]{:S(2)}) collective-permute-start(bf16[128,2560]{1,0:T(8,128)(2,1)} %get-tuple-element.120), channel_id=1, source_target_pairs={{0,2},{1,3},{2,4},{3,5},{4,6},{5,7},{6,0},{7,1},{8,10},{9,11},{10,... | collective-permute-start | bytes 1966088 | tf_op jit(solution)/shard_map/ppermute | solution.py:611
  76.8 19.5 %collective-permute-start.21 = (bf16[128,2560]{1,0:T(8,128)(2,1)}, bf16[128,2560]{1,0:T(8,128)(2,1)}, u32[]{:S(2)}, u32[]{:S(2)}) collective-permute-start(bf16[128,2560]{1,0:T(8,128)(2,1)} %get-tuple-element.121), channel_id=1, source_target_pairs={{0,6},{1,7},{2,0},{3,1},{4,2},{5,3},{6,4},{7,5},{8,14},{9,15},{10,... | collective-permute-start | bytes 1966088 | tf_op jit(solution)/shard_map/ppermute | solution.py:611
  80.6 6.2 %collective-permute-start.3 = (bf16[8,2688]{1,0:T(8,128)(2,1)S(1)}, bf16[8,2688]{1,0:T(8,128)(2,1)S(1)}, u32[]{:S(2)}, u32[]{:S(2)}) collective-permute-start(bf16[8,2688]{1,0:T(8,128)(2,1)S(1)} %get-tuple-element.246), channel_id=1, source_target_pairs={{0,24},{8,0},{16,8},{24,16},{32,56},{40,32},{48,40},{56,48},{64,88... | collective-permute-start | bytes 129032 | tf_op jit(solution)/shard_map/while/body/ppermute | solution.py:615
  83.6 5.6 %collective-permute-start.5 = (bf16[8,2688]{1,0:T(8,128)(2,1)S(1)}, bf16[8,2688]{1,0:T(8,128)(2,1)S(1)}, u32[]{:S(2)}, u32[]{:S(2)}) collective-permute-start(bf16[8,2688]{1,0:T(8,128)(2,1)S(1)} %get-tuple-element.246), channel_id=1, source_target_pairs={{0,16},{8,24},{16,0},{24,8},{32,48},{40,56},{48,32},{56,40},{64,80... | collective-permute-start | bytes 129032 | tf_op jit(solution)/shard_map/while/body/ppermute | solution.py:615
  83.6 5.7 %collective-permute-start.4 = (bf16[8,2688]{1,0:T(8,128)(2,1)S(1)}, bf16[8,2688]{1,0:T(8,128)(2,1)S(1)}, u32[]{:S(2)}, u32[]{:S(2)}) collective-permute-start(bf16[8,2688]{1,0:T(8,128)(2,1)S(1)} %get-tuple-element.246), channel_id=1, source_target_pairs={{0,8},{8,16},{16,24},{24,0},{32,40},{40,48},{48,56},{56,32},{64,72... | collective-permute-start | bytes 129032 | tf_op jit(solution)/shard_map/while/body/ppermute | solution.py:615
  89.3 5.6 %collective-permute-start.8 = (bf16[8,2688]{1,0:T(8,128)(2,1)S(1)}, bf16[8,2688]{1,0:T(8,128)(2,1)S(1)}, u32[]{:S(2)}, u32[]{:S(2)}) collective-permute-start(bf16[8,2688]{1,0:T(8,128)(2,1)S(1)} %reduce-precision_convert_fusion.8), channel_id=1, source_target_pairs={{0,64},{8,72},{16,80},{24,88},{32,96},{40,104},{48,112},{56,120},{... | collective-permute-start | bytes 129032 | tf_op jit(solution)/shard_map/while/body/ppermute | solution.py:619
  90.9 5.2 %collective-permute-start.7 = (bf16[8,2688]{1,0:T(8,128)(2,1)S(1)}, bf16[8,2688]{1,0:T(8,128)(2,1)S(1)}, u32[]{:S(2)}, u32[]{:S(2)}) collective-permute-start(bf16[8,2688]{1,0:T(8,128)(2,1)S(1)} %reduce-precision_convert_fusion.8), channel_id=1, source_target_pairs={{0,32},{8,40},{16,48},{24,56},{32,64},{40,72},{48,80},{56,88},{64,... | collective-permute-start | bytes 129032 | tf_op jit(solution)/shard_map/while/body/ppermute | solution.py:619
  90.9 5.2 %collective-permute-start.6 = (bf16[8,2688]{1,0:T(8,128)(2,1)S(1)}, bf16[8,2688]{1,0:T(8,128)(2,1)S(1)}, u32[]{:S(2)}, u32[]{:S(2)}) collective-permute-start(bf16[8,2688]{1,0:T(8,128)(2,1)S(1)} %reduce-precision_convert_fusion.8), channel_id=1, source_target_pairs={{0,96},{8,104},{16,112},{24,120},{32,0},{40,8},{48,16},{56,24},{64... | collective-permute-start | bytes 129032 | tf_op jit(solution)/shard_map/while/body/ppermute | solution.py:619
  96.2 5.3 %collective-permute-start.24 = (bf16[8,2688]{1,0:T(8,128)(2,1)S(1)}, bf16[8,2688]{1,0:T(8,128)(2,1)S(1)}, u32[]{:S(2)}, u32[]{:S(2)}) collective-permute-start(bf16[8,2688]{1,0:T(8,128)(2,1)S(1)} %get-tuple-element.122), channel_id=1, source_target_pairs={{0,2},{1,3},{2,4},{3,5},{4,6},{5,7},{6,0},{7,1},{8,10},{9,11},{10,... | collective-permute-start | bytes 129032 | tf_op jit(solution)/shard_map/ppermute | solution.py:611
  96.3 5.7 %collective-permute-start.23 = (bf16[8,2688]{1,0:T(8,128)(2,1)S(1)}, bf16[8,2688]{1,0:T(8,128)(2,1)S(1)}, u32[]{:S(2)}, u32[]{:S(2)}) collective-permute-start(bf16[8,2688]{1,0:T(8,128)(2,1)S(1)} %get-tuple-element.122), channel_id=1, source_target_pairs={{0,4},{1,5},{2,6},{3,7},{4,0},{5,1},{6,2},{7,3},{8,12},{9,13},{10,... | collective-permute-start | bytes 129032 | tf_op jit(solution)/shard_map/ppermute | solution.py:611
  97.8 5.1 %collective-permute-start.22 = (bf16[8,2688]{1,0:T(8,128)(2,1)S(1)}, bf16[8,2688]{1,0:T(8,128)(2,1)S(1)}, u32[]{:S(2)}, u32[]{:S(2)}) collective-permute-start(bf16[8,2688]{1,0:T(8,128)(2,1)S(1)} %get-tuple-element.122), channel_id=1, source_target_pairs={{0,6},{1,7},{2,0},{3,1},{4,2},{5,3},{6,4},{7,5},{8,14},{9,15},{10,... | collective-permute-start | bytes 129032 | tf_op jit(solution)/shard_map/ppermute | solution.py:611
  (13 other events, 41.8 us)

commit v3 on v2

--- a/solution.py
+++ b/solution.py
@@ -96,10 +96,10 @@
 
 def front_kernel(
     codes, gain, hidden, probs, w_value, w_out, out_grad, err_out, err_value,
-    mats_out, mats_value, left_out, own_half, other_half, gain_out, hidden_rows,
+    mats_out, mats_value, left_out, own_half, other_half, gain_out, hidden_rows, gain_row,
     hidden_v, probs_v, w_value_v, w_value_t, w_out_v, grad_v, err_out_v, err_value_v,
     starts, values_t, d_mixed_t, mixed_t, d_values_t, mats_out_v, mats_value_v, left_sum, gain_v,
-    codes_v, gain_flat, gain_row, sems, out_sems, small_sems,
+    codes_v, gain_flat, sems, out_sems, small_sems,
 ):
     half = TOK // 2
     halves = [pl.ds(part * half, half) for part in range(2)]
@@ -255,9 +255,10 @@
             jax.ShapeDtypeStruct((COLS, TOK // 2), BF16),
             jax.ShapeDtypeStruct((2 * RANK, 128), F32),
             jax.ShapeDtypeStruct((128, D), BF16),
+            jax.ShapeDtypeStruct((1, D), F32),
         ),
         in_specs=[ANY] * 9,
-        out_specs=(ANY, ANY, vmem, vmem, vmem, vmem, ANY),
+        out_specs=(ANY, ANY, vmem, vmem, vmem, vmem, ANY, vmem),
         scratch_shapes=[
             pltpu.VMEM((TOK, D), BF16),
             pltpu.VMEM((CROPS, HEADS_DEV, LEN, LEN), BF16),
@@ -278,7 +279,6 @@
             pltpu.VMEM((1, D), F32),
             pltpu.SMEM((2,), jnp.int32),
             pltpu.VMEM((D,), F32),
-            pltpu.VMEM((1, D), F32),
             pltpu.SemaphoreType.DMA((9,)),
             pltpu.SemaphoreType.DMA((2 * STEPS + 1,)),
             pltpu.SemaphoreType.DMA((2,)),
@@ -333,7 +333,7 @@
         own_half,
         other_half,
         pltpu.with_memory_space_constraint(w_own, pltpu.HBM),
-        pltpu.with_memory_space_constraint(w_other, pltpu.HBM),
+        w_other,
     )
 
 
@@ -359,7 +359,10 @@
         cost_estimate=pl.CostEstimate(
             flops=10**6, bytes_accessed=4 * 10**6, transcendentals=0
         ),
-    )(after, before, far_after, far_before)
+    )(*(
+        pltpu.with_memory_space_constraint(part, pltpu.HBM)
+        for part in (after, before, far_after, far_before)
+    ))
 
 
 def norm_back_kernel(hidden, gain, here, after, before, in_grad, total, standard):
@@ -477,13 +480,68 @@
     )(left, gain_rows, mats_out, mats_value)
 
 
-def factor_kernel(packed, inverse):
-    whole = packed[:, pl.ds(0, 128)] + packed[:, pl.ds(128, 128)]
-    gram = jnp.concatenate([whole[:, k * RANK : (k + 1) * RANK] for k in range(4)], axis=0)
+def merge_kernel(ours, theirs, own, to_opposite, to_after, to_before):
+    total = ours[...] + theirs[...].astype(F32)
+    gram = total[:8, SENT : SENT + 128] + total[:8, SENT + 128 :]
+    grams = split2(gram)
+    own[:, pl.ds(0, SENT)] = total[:8, :SENT]
+    own[:, pl.ds(SENT, 128)] = gram
+    for slot, target in ((1, to_after), (2, to_opposite), (3, to_before)):
+        target[:, pl.ds(0, SENT)] = total[8 * slot : 8 * slot + 8, :SENT].astype(BF16)
+        for part, value in enumerate(grams):
+            target[:, pl.ds(SENT + 128 * part, 128)] = value
+
+
+def merge(ours, theirs):
+    return pl.pallas_call(
+        merge_kernel,
+        name="merge",
+        out_shape=(
+            jax.ShapeDtypeStruct((8, SENT + 128), F32),
+            *[jax.ShapeDtypeStruct((8, WIDE), BF16) for _ in range(3)],
+        ),
+        compiler_params=pltpu.CompilerParams(vmem_limit_bytes=8 * 2**20),
+        cost_estimate=pl.CostEstimate(
+            flops=10**5, bytes_accessed=7 * 10**5, transcendentals=0
+        ),
+    )(ours, theirs)
+
+
+def collect_kernel(own, opposite, after, before, chunk, gram):
+    parts = [part[...].astype(F32) for part in (opposite, after, before)]
+    total = (own[:, pl.ds(0, SENT)] + parts[0][:, :SENT]) + (
+        parts[1][:, :SENT] + parts[2][:, :SENT]
+    )
+    chunk[...] = total.astype(BF16)
+    parts = [part[:, SENT : SENT + 128] + part[:, SENT + 128 :] for part in parts]
+    packed = (own[:, pl.ds(SENT, 128)] + parts[0]) + (parts[1] + parts[2])
+    square = jnp.concatenate([packed[:, k * RANK : (k + 1) * RANK] for k in range(4)], axis=0)
+    wide = jnp.concatenate([square, jnp.zeros((RANK, 128 - RANK), F32)], axis=1)
+    for part, value in enumerate(split2(wide)):
+        gram[:, pl.ds(part * 128, 128)] = value
+
+
+def collect(own, opposite, after, before):
+    return pl.pallas_call(
+        collect_kernel,
+        name="collect",
+        out_shape=(
+            jax.ShapeDtypeStruct((8, SENT), BF16),
+            jax.ShapeDtypeStruct((RANK, 256), BF16),
+        ),
+        compiler_params=pltpu.CompilerParams(vmem_limit_bytes=8 * 2**20),
+        cost_estimate=pl.CostEstimate(
+            flops=10**5, bytes_accessed=3 * 10**5, transcendentals=0
+        ),
+    )(own, opposite, after, before)
+
+
+def factor_kernel(parts, inverse):
+    gram = parts[:, pl.ds(0, 128)].astype(F32) + parts[:, pl.ds(128, 128)].astype(F32)
     row_ids = lax.broadcasted_iota(jnp.int32, (RANK, 128), 0)
     col_ids = lax.broadcasted_iota(jnp.int32, (RANK, 128), 1)
     unit = jnp.where(row_ids + RANK == col_ids, 1.0, 0.0)
-    work = unit + jnp.concatenate([gram, jnp.zeros((RANK, 128 - RANK), F32)], axis=1)
+    work = unit + gram
     for step in range(0, RANK, 2):
         first, second = work[step : step + 1, :], work[step + 1 : step + 2, :]
         column = jnp.broadcast_to(work[:, step : step + 1], (RANK, 128))
@@ -505,7 +563,7 @@
     inverse[:, pl.ds(128, 128)] = low
 
 
-def factor(packed):
+def factor(parts):
     return pl.pallas_call(
         factor_kernel,
         name="factor",
@@ -513,7 +571,7 @@
         cost_estimate=pl.CostEstimate(
             flops=5 * 10**6, bytes_accessed=3 * 10**6, transcendentals=0
         ),
-    )(packed)
+    )(parts)
 
 
 def finish_kernel(
@@ -536,9 +594,8 @@
             rows = pl.ds(pl.multiple_of(side * RANK, RANK), RANK)
             sums[rows, pl.ds(SENT, 128)] = wide[:, SENT : SENT + 128] + wide[:, SENT + 128 :]
         for part in range(D // 128):
-            gain_out[:, pl.ds(part * 128, 128)] = sums[
-                pl.ds(part // 3 * 8 + part % 3, 1), pl.ds(D, 128)
-            ]
+            row = sums[pl.ds(part // 3 * 8 + part % 3, 1), pl.ds(D, 128)]
+            gain_out[pl.ds(part * 128, 128)] = row.reshape(128)
         for side, scaled in enumerate((ortho_out, ortho_value)):
             span = pl.ds(side * RANK, RANK)
             inverse = sums[span, pl.ds(SENT, 128)][:, :RANK]
@@ -583,13 +640,13 @@
             jax.ShapeDtypeStruct((RANK, D // 8), F32),
             jax.ShapeDtypeStruct((RANK, COLS), F32),
             jax.ShapeDtypeStruct((RANK, COLS), F32),
-            jax.ShapeDtypeStruct((1, D), F32),
+            jax.ShapeDtypeStruct((D,), F32),
         ),
         in_specs=[
             whole, whole, pl.BlockSpec((2 * RANK, COLS), lambda n: (0, 0)), mats, mats,
         ],
         out_specs=(
-            err, err, share, share, ortho, ortho, pl.BlockSpec((1, D), lambda n: (0, 0)),
+            err, err, share, share, ortho, ortho, pl.BlockSpec((D,), lambda n: (0,)),
         ),
         scratch_shapes=[
             pltpu.VMEM((2 * RANK, WIDE), F32),
@@ -623,78 +680,61 @@
     return lax.reduce_precision(value, 8, 7).astype(BF16)
 
 
-def ring_sum(value, send):
-    opposite, after, before = send(value, 2), send(value, 1), send(value, 3)
-    wide = value.astype(F32)
-    return (wide + opposite.astype(F32)) + (after.astype(F32) + before.astype(F32))
+def ring_sum(value, send, beside=()):
+    parts = send(value, 2), send(value, 1), send(value, 3)
+    parts, beside = lax.optimization_barrier((parts, beside))
+    opposite, after, before = (part.astype(F32) for part in parts)
+    total = (value.astype(F32) + opposite) + (after + before)
+    return (total, *beside) if beside else total
 
 
 def local(
     hidden_in, ln_gain, attn_probs, w_value, w_out, out_grad, err_out, err_value, factor_codes
 ):
-    gain_row = ln_gain.reshape(1, D)
     w_other = to_core(w_value)
-    mats_out, mats_value, left_term, own_half, other_half, gain_rows, hidden_rows = front(
+    (
+        mats_out, mats_value, left_term, own_half, other_half, gain_rows, hidden_rows, gain_row
+    ) = front(
         factor_codes, ln_gain, hidden_in, attn_probs, w_value, w_out, out_grad,
         err_out, err_value,
     )
     received_half = to_core(other_half)
 
-    left = ring_sum(left_term, to_z)
     here, after, before, far_after, far_before = branch(own_half, received_half, w_value, w_other)
-    left_term, far_after, far_before = lax.optimization_barrier(
-        (rounded(left), far_after, far_before)
-    )
+    left, far_after, far_before = ring_sum(left_term, to_z, (far_after, far_before))
     far_after, far_before = to_x(far_after, 1), to_x(far_before, 3)
+    left, far_after, far_before = ring_sum(rounded(left), to_y, (far_after, far_before))
+
+    ours, theirs = right_terms(left, gain_rows, mats_out, mats_value)
+    own, to_opposite, to_after, to_before = merge(ours, to_core(theirs))
+    next_after, next_before = relay(after, before, far_after, far_before)
+    parts = to_x(to_opposite, 2), to_x(to_after, 1), to_x(to_before, 3)
+    parts, next_after, next_before = lax.optimization_barrier((parts, next_after, next_before))
+    chunk, gram = collect(own, *parts)
+    chunk, gram, next_after, next_before = lax.optimization_barrier(
+        (chunk, gram, next_after, next_before)
+    )
+    near_after, near_before = to_x(next_after, 1), to_x(next_before, 3)
+
+    def over_workers(step, carry):
+        chunk, inverse = ring_sum(carry[0], to_z, (factor(carry[1]),))
+        return rounded(ring_sum(rounded(chunk), to_y)), inverse
+
     passes = 1 + lax.axis_index("dp") // WORKERS
-
-    def sum_left(step, carry):
-        left = ring_sum(carry[0], to_y)
-        return rounded(left), left
-
-    _, left = lax.fori_loop(
-        0, passes, sum_left, (left_term, jnp.zeros((2 * RANK, COLS), F32))
-    )
-    left, far_after, far_before = lax.optimization_barrier((left, far_after, far_before))
-
-    ours, theirs = right_terms(left, gain_rows, mats_out, mats_value)
-    chunks = ours + to_core(theirs).astype(F32)
-    next_after, next_before = relay(after, before, far_after, far_before)
-    grams = chunks[:, SENT : SENT + 128] + chunks[:, SENT + 128 :]
-    high = lax.reduce_precision(grams, 8, 7)
-    chunks = jnp.concatenate([chunks[:, :SENT], high, grams - high], axis=1)
-    opposite, after, before = (
-        to_x(rounded(chunks[8 * k : 8 * k + 8]), k).astype(F32) for k in (2, 1, 3)
-    )
-    chunk = (chunks[:8] + opposite) + (after + before)
-    packed = chunk[:, SENT:]
-    chunk, next_after, next_before = lax.optimization_barrier(
-        (rounded(chunk[:, :SENT]), next_after, next_before)
-    )
-    near_after, near_before = to_x(next_after, 1), to_x(next_before, 3)
-
-    def over_workers(step, carry):
-        chunk, _ = carry
-        inverse = factor(packed)
-        chunk = ring_sum(chunk, to_z)
-        chunk, inverse = lax.optimization_barrier((chunk, inverse))
-        return rounded(ring_sum(rounded(chunk), to_y)), inverse
-
-    chunk, inverse = lax.fori_loop(
-        0, passes, over_workers, (chunk, jnp.zeros((RANK, 256), BF16))
-    )
+    chunk, inverse = lax.fori_loop(0, passes, over_workers, (chunk, gram))
     chunk, near_after, near_before = lax.optimization_barrier((chunk, near_after, near_before))
     in_grad = norm_back(hidden_rows, gain_row, here, near_after, near_before)
-    opposite, after, before = to_x(chunk, 2), to_x(chunk, 3), to_x(chunk, 1)
+    parts = to_x(chunk, 2), to_x(chunk, 3), to_x(chunk, 1)
+    (opposite, after, before), in_grad = lax.optimization_barrier((parts, in_grad))
     rows = jnp.concatenate([chunk, after, opposite, before], axis=0)
     ours = jnp.concatenate([rows, inverse], axis=1)
-    theirs, in_grad = lax.optimization_barrier((to_core(ours), in_grad))
+    theirs = to_core(ours)
     new_out, new_value, share_out, share_value, ortho_out, ortho_value, gain_grad = finish(
         ours, theirs, left, mats_out, mats_value
     )
     return (
         in_grad,
-        gain_grad.reshape(D),
+        gain_grad,
         new_out,
         new_value,
         ortho_out.T,

time: 116 us -> 106 us (0.914)
  local copies, waits for them, and re-layouts: 9.97 us -> 1.42 us
  waiting for transfers between devices: 19.9 us -> 15.7 us
  starting transfers between devices: 34 us -> 36.5 us
    unnamed x22 -> x12, local copies, waits for them, and re-layouts: 7.97 us -> 0.81 us
    ppermute x6, waiting for transfers between devices: 6.49 us -> 2.55 us  [to_z(): lax.ppermute(value, 'dp', [(i, i // 4 * 4 + (i + hops) % 4) for i in rang...]
    ppermute x10, waiting for transfers between devices: 5.49 us -> 2.49 us  [to_x(): lax.ppermute(value, 'tensor', [(i, (i // 2 + hops) % 4 * 2 + i % 2) for i...]
    pallas_call x0 -> x2, Pallas kernels: none -> 2.13 us  [the longest x1 1.46 us: collect(): pl.pallas_call(collect_kernel, name='collect', out_shape=(jax.ShapeDtypeS...]
    convert_element_type x6 -> x3, other arithmetic: 0.76 us -> 2.29 us  [rounded(): return lax.reduce_precision(value, 8, 7).astype(BF16)]
    ppermute x4, waiting for transfers between devices: 1.42 us -> 2.84 us  [to_core(): return lax.ppermute(value, 'tensor', [(i, i ^ 1) for i in range(8)])]
    ppermute x6, waiting for transfers between devices: 6.52 us -> 7.82 us  [to_y(): lax.ppermute(value, 'dp', [(i, (i // 4 + hops) % 4 * 4 + i % 4) for i in...]
    broadcast_in_dim x2 -> x0, local copies, waits for them, and re-layouts: 1.25 us -> none  [the longest x1 0.64 us: local(): jnp.zeros((2 * RANK, COLS), F32)]
  transfers between devices with their start and end apart: 26 -> 26, of which waited for: 13 -> 7; matrix products, arithmetic and copies ran while one was open for 2% -> 3% of each run, Pallas kernels for 30% -> 36%
where the time goes in v3:
time: 106 us; the launch traced here: 104 us
  Pallas kernels  46.4 us (44%)
  starting transfers between devices  36.5 us (34%)
  waiting for transfers between devices  15.7 us (15%)
  other arithmetic  3.12 us (3%)
  local copies, waits for them, and re-layouts  1.42 us (1%)
    pallas_call x1, Pallas kernels, front(): pl.pallas_call(front_kernel, name='front', out_shape=(jax.ShapeDtypeStruc...  25.3 us
    ppermute x10, starting transfers between devices, to_x(): lax.ppermute(value, 'tensor', [(i, (i // 2 + hops) % 4 * 2 + i % 2) for i...  14.9 us
    ppermute x6, starting transfers between devices, to_z(): lax.ppermute(value, 'dp', [(i, i // 4 * 4 + (i + hops) % 4) for i in rang...  10.9 us
    ppermute x6, starting transfers between devices, to_y(): lax.ppermute(value, 'dp', [(i, (i // 4 + hops) % 4 * 4 + i % 4) for i in...  9.88 us
    ppermute x6, waiting for transfers between devices, to_y(): lax.ppermute(value, 'dp', [(i, (i // 4 + hops) % 4 * 4 + i % 4) for i in...  7.82 us
    pallas_call x1, Pallas kernels, finish(): pl.pallas_call(finish_kernel, name='finish', grid=(2,), out_shape=(jax.Sh...  5 us
    pallas_call x1, Pallas kernels, branch(): pl.pallas_call(branch_kernel, name='branch', grid=(2,), out_shape=[jax.Sh...  4.13 us
    pallas_call x1, Pallas kernels, norm_back(): pl.pallas_call(norm_back_kernel, name='norm_back', grid=(1,), in_specs=[r...  3.26 us
  transfers between devices with their start and end apart: 26, of which 7 were waited for; matrix products, arithmetic and copies ran while one was open for 3% of the time, Pallas kernels for 36%

profile of v3, /device:TPU:0, one launch (start us, length us, event | category | flops | bytes accessed | tf_op | source)
XLA Modules:
  0.0 104.1 jit_solution(9760043501313353094)
XLA Ops:
  0.7 25.3 %front.1 = (bf16[384,2560]{1,0:T(8,128)(2,1)S(1)}, bf16[384,2560]{1,0:T(8,128)(2,1)S(1)}, bf16[64,384]{1,0:T(8,128)(2,1)S(1)}, bf16[384,512]{1,0:T(8,128)(2,1)S(...) custom-call(s32[2]{0:T(128)} %codes.1, ...), custom_call_target="tpu_custom_call" | custom-call | flops 11000000512 | bytes 32000000 | tf_op jit(solution)/shard_map/front/pallas_call | solution.py:247
  26.6 4.1 %collective-permute-start.8 = (bf16[64,384]{1,0:T(8,128)(2,1)S(1)}, bf16[64,384]{1,0:T(8,128)(2,1)S(1)}, u32[]{:S(2)}, u32[]{:S(2)}) collective-permute-start(bf16[64,384]{1,0:T(8,128)(2,1)S(1)} %get-tuple-element.95), channel_id=1, source_target_pairs={{0,24},{8,0},{16,8},{24,16},{32,56},{40,32},{48,40},{56,48},{64,88... | collective-permute-start | bytes 147464 | tf_op jit(solution)/shard_map/ppermute | solution.py:672
  30.8 1.9 %collective-permute-start.6 = (bf16[64,384]{1,0:T(8,128)(2,1)S(1)}, bf16[64,384]{1,0:T(8,128)(2,1)S(1)}, u32[]{:S(2)}, u32[]{:S(2)}) collective-permute-start(bf16[64,384]{1,0:T(8,128)(2,1)S(1)} %get-tuple-element.95), channel_id=1, source_target_pairs={{0,16},{8,24},{16,0},{24,8},{32,48},{40,56},{48,32},{56,40},{64,80... | collective-permute-start | bytes 147464 | tf_op jit(solution)/shard_map/ppermute | solution.py:672
  32.6 4.1 %branch.1 = (bf16[128,2560]{1,0:T(8,128)(2,1)S(1)}, bf16[128,2560]{1,0:T(8,128)(2,1)S(1)}, bf16[128,2560]{1,0:T(8,128)(2,1)S(1)}, bf16[64,2560]{1,0:T(8,128)(2,1)S(1)}, bf16[64,2560]{1,0:T(8,128)(2,1)S(1)}) custom-call(bf16[384,512]{1,0:T(8,128)(2,1)S(1)} %get-tuple-element.96.own_half, bf16[384,512]{1,0:T(8,128)(2,1)S(1)} %collective-permute-done.9.other_half, ...), custom_call_target="tpu_custom_call" | custom-call | flops 2000000000 | bytes 7000000 | tf_op jit(solution)/shard_map/branch/pallas_call | solution.py:320
  36.8 1.5 %collective-permute-start.14 = (bf16[64,2560]{1,0:T(8,128)(2,1)S(1)}, bf16[64,2560]{1,0:T(8,128)(2,1)S(1)}, u32[]{:S(2)}, u32[]{:S(2)}) collective-permute-start(bf16[64,2560]{1,0:T(8,128)(2,1)S(1)} %get-tuple-element.103), channel_id=1, source_target_pairs={{0,2},{1,3},{2,4},{3,5},{4,6},{5,7},{6,0},{7,1},{8,10},{9,11},{10,... | collective-permute-start | bytes 983048 | tf_op jit(solution)/shard_map/ppermute | solution.py:668
  38.4 1.8 %collective-permute-start.15 = (bf16[64,2560]{1,0:T(8,128)(2,1)S(1)}, bf16[64,2560]{1,0:T(8,128)(2,1)S(1)}, u32[]{:S(2)}, u32[]{:S(2)}) collective-permute-start(bf16[64,2560]{1,0:T(8,128)(2,1)S(1)} %get-tuple-element.104), channel_id=1, source_target_pairs={{0,6},{1,7},{2,0},{3,1},{4,2},{5,3},{6,4},{7,5},{8,14},{9,15},{10,... | collective-permute-start | bytes 983048 | tf_op jit(solution)/shard_map/ppermute | solution.py:668
  40.2 3.1 %collective-permute-start.13 = (bf16[64,384]{1,0:T(8,128)(2,1)S(1)}, bf16[64,384]{1,0:T(8,128)(2,1)S(1)}, u32[]{:S(2)}, u32[]{:S(2)}) collective-permute-start(bf16[64,384]{1,0:T(8,128)(2,1)S(1)} %reduce-precision_convert_fusion.2), channel_id=1, source_target_pairs={{0,96},{8,104},{16,112},{24,120},{32,0},{40,8},{48,16},{56,24},{64... | collective-permute-start | bytes 147464 | tf_op jit(solution)/shard_map/ppermute | solution.py:676
  43.2 2.2 %collective-permute-start.11 = (bf16[64,384]{1,0:T(8,128)(2,1)S(1)}, bf16[64,384]{1,0:T(8,128)(2,1)S(1)}, u32[]{:S(2)}, u32[]{:S(2)}) collective-permute-start(bf16[64,384]{1,0:T(8,128)(2,1)S(1)} %reduce-precision_convert_fusion.2), channel_id=1, source_target_pairs={{0,64},{8,72},{16,80},{24,88},{32,96},{40,104},{48,112},{56,120},{... | collective-permute-start | bytes 147464 | tf_op jit(solution)/shard_map/ppermute | solution.py:676
  45.4 3.6 %collective-permute-done.12 = bf16[64,384]{1,0:T(8,128)(2,1)S(1)} collective-permute-done((bf16[64,384]{1,0:T(8,128)(2,1)S(1)}, bf16[64,384]{1,0:T(8,128)(2,1)S(1)}, u32[]{:S(2)}, u32[]{:S(2)}) %collective-permute-start.12) | collective-permute-done | bytes 49184 | tf_op jit(solution)/shard_map/ppermute | solution.py:676
  53.6 1.8 %collective-permute-start.17 = (bf16[8,2944]{1,0:T(8,128)(2,1)}, bf16[8,2944]{1,0:T(8,128)(2,1)S(1)}, u32[]{:S(2)}, u32[]{:S(2)}) collective-permute-start(bf16[8,2944]{1,0:T(8,128)(2,1)} %get-tuple-element.114), channel_id=1, source_target_pairs={{0,4},{1,5},{2,6},{3,7},{4,0},{5,1},{6,2},{7,3},{8,12},{9,13},{10,... | collective-permute-start | bytes 141320 | tf_op jit(solution)/shard_map/ppermute | solution.py:668
  56.0 2.7 %collective-permute-start.19 = (bf16[8,2944]{1,0:T(8,128)(2,1)}, bf16[8,2944]{1,0:T(8,128)(2,1)}, u32[]{:S(2)}, u32[]{:S(2)}) collective-permute-start(bf16[8,2944]{1,0:T(8,128)(2,1)} %get-tuple-element.116), channel_id=1, source_target_pairs={{0,6},{1,7},{2,0},{3,1},{4,2},{5,3},{6,4},{7,5},{8,14},{9,15},{10,... | collective-permute-start | bytes 141320 | tf_op jit(solution)/shard_map/ppermute | solution.py:668
  58.7 2.6 %relay.1 = (bf16[128,2560]{1,0:T(8,128)(2,1)}, bf16[128,2560]{1,0:T(8,128)(2,1)}) custom-call(bf16[128,2560]{1,0:T(8,128)(2,1)} %copy-done.2, bf16[128,2560]{1,0:T(8,128)(2,1)} %copy-done.3, bf16[64,2560]{1,0:T(8,128)(2,1)} %copy-done.4, bf16[64,2560]{1,0:T(8,128)(2,1)} %copy-done.5), custom_call_target="tpu_custom_call" | custom-call | flops 1000000 | bytes 4000000 | tf_op jit(solution)/shard_map/relay/pallas_call | solution.py:351
  63.0 3.1 %collective-permute-start.21 = (bf16[128,2560]{1,0:T(8,128)(2,1)}, bf16[128,2560]{1,0:T(8,128)(2,1)}, u32[]{:S(2)}, u32[]{:S(2)}) collective-permute-start(bf16[128,2560]{1,0:T(8,128)(2,1)} %get-tuple-element.134), channel_id=1, source_target_pairs={{0,6},{1,7},{2,0},{3,1},{4,2},{5,3},{6,4},{7,5},{8,14},{9,15},{10,... | collective-permute-start | bytes 1966088 | tf_op jit(solution)/shard_map/ppermute | solution.py:668
  66.1 21.5 %while.12 = (s32[]{:T(128)}, bf16[8,2688]{1,0:T(8,128)(2,1)}, bf16[32,256]{1,0:T(8,128)(2,1)S(1)}, s32[]{:T(128)}, s32[]{:T(128)}) while((s32[]{:T(128)}, bf16[8,2688]{1,0:T(8,128)(2,1)}, bf16[32,256]{1,0:T(8,128)(2,1)S(1)}, s32[]{:T(128)}, s32[]{:T(128)}) %tuple.40), condition=%wide.region_1.2_spmd, body=%wide.region_0.1_spmd.sunk | while | flops 5387074 | bytes 4495341 | solution.py:724
  66.1 1.7 %collective-permute-start = (bf16[8,2688]{1,0:T(8,128)(2,1)}, bf16[8,2688]{1,0:T(8,128)(2,1)S(1)}, u32[]{:S(2)}, u32[]{:S(2)}) collective-permute-start(bf16[8,2688]{1,0:T(8,128)(2,1)} %get-tuple-element.207), channel_id=1, source_target_pairs={{0,16},{8,24},{16,0},{24,8},{32,48},{40,56},{48,32},{56,40},{64,80... | collective-permute-start | bytes 129032 | tf_op jit(solution)/shard_map/while/body/ppermute | solution.py:672
  67.7 3.2 %collective-permute-start.2 = (bf16[8,2688]{1,0:T(8,128)(2,1)}, bf16[8,2688]{1,0:T(8,128)(2,1)S(1)}, u32[]{:S(2)}, u32[]{:S(2)}) collective-permute-start(bf16[8,2688]{1,0:T(8,128)(2,1)} %get-tuple-element.207), channel_id=1, source_target_pairs={{0,24},{8,0},{16,8},{24,16},{32,56},{40,32},{48,40},{56,48},{64,88... | collective-permute-start | bytes 129032 | tf_op jit(solution)/shard_map/while/body/ppermute | solution.py:672
  71.6 2.4 %factor.1 = bf16[32,256]{1,0:T(8,128)(2,1)S(1)} custom-call(bf16[32,256]{1,0:T(8,128)(2,1)} %copy.29.parts), custom_call_target="tpu_custom_call" | custom-call | flops 5000000 | bytes 3000000 | tf_op jit(solution)/shard_map/while/body/factor/pallas_call | solution.py:567
  74.0 2.5 %collective-permute-done.1 = bf16[8,2688]{1,0:T(8,128)(2,1)} collective-permute-done((bf16[8,2688]{1,0:T(8,128)(2,1)}, bf16[8,2688]{1,0:T(8,128)(2,1)}, u32[]{:S(2)}, u32[]{:S(2)}) %collective-permute-start.1) | collective-permute-done | bytes 43040 | tf_op jit(solution)/shard_map/while/body/ppermute | solution.py:672
  77.3 3.1 %collective-permute-start.5 = (bf16[8,2688]{1,0:T(8,128)(2,1)S(1)}, bf16[8,2688]{1,0:T(8,128)(2,1)S(1)}, u32[]{:S(2)}, u32[]{:S(2)}) collective-permute-start(bf16[8,2688]{1,0:T(8,128)(2,1)S(1)} %reduce-precision_convert_fusion.5), channel_id=1, source_target_pairs={{0,96},{8,104},{16,112},{24,120},{32,0},{40,8},{48,16},{56,24},{64... | collective-permute-start | bytes 129032 | tf_op jit(solution)/shard_map/while/body/ppermute | solution.py:676
  82.1 4.0 %collective-permute-done.4 = bf16[8,2688]{1,0:T(8,128)(2,1)S(1)} collective-permute-done((bf16[8,2688]{1,0:T(8,128)(2,1)S(1)}, bf16[8,2688]{1,0:T(8,128)(2,1)S(1)}, u32[]{:S(2)}, u32[]{:S(2)}) %collective-permute-start.4) | collective-permute-done | bytes 43040 | tf_op jit(solution)/shard_map/while/body/ppermute | solution.py:676
  87.7 3.2 %collective-permute-start.23 = (bf16[8,2688]{1,0:T(8,128)(2,1)}, bf16[8,2688]{1,0:T(8,128)(2,1)S(1)}, u32[]{:S(2)}, u32[]{:S(2)}) collective-permute-start(bf16[8,2688]{1,0:T(8,128)(2,1)} %get-tuple-element.135), channel_id=1, source_target_pairs={{0,6},{1,7},{2,0},{3,1},{4,2},{5,3},{6,4},{7,5},{8,14},{9,15},{10,... | collective-permute-start | bytes 129032 | tf_op jit(solution)/shard_map/ppermute | solution.py:668
  90.9 3.3 %norm_back.1 = bf16[128,2560]{1,0:T(8,128)(2,1)} custom-call(bf16[128,2560]{1,0:T(8,128)(2,1)S(1)} %get-tuple-element.136.hidden, f32[1,2560]{1,0:T(1,128)S(1)} %get-tuple-element.137.gain, bf16[128,2560]{1,0:T(8,128)(2,1)S(1)} %get-tuple-element.138.here, bf16[128,2560]{1,0:T(8,128)(2,1)} %collective-permute-done.20.after, ...), custom_call_target="tpu_custom_call" | custom-call | flops 5000000 | bytes 1000000 | tf_op jit(solution)/shard_map/norm_back/pallas_call | solution.py:403
  94.2 2.5 %collective-permute-done.22 = bf16[8,2688]{1,0:T(8,128)(2,1)S(1)} collective-permute-done((bf16[8,2688]{1,0:T(8,128)(2,1)}, bf16[8,2688]{1,0:T(8,128)(2,1)S(1)}, u32[]{:S(2)}, u32[]{:S(2)}) %collective-permute-start.22) | collective-permute-done | bytes 43040 | tf_op jit(solution)/shard_map/ppermute | solution.py:668
  99.0 5.0 %finish.1 = (f32[1,384,2560]{2,1,0:T(8,128)}, f32[1,384,2560]{2,1,0:T(8,128)}, f32[32,320]{1,0:T(8,128)}, f32[32,320]{1,0:T(8,128)}, f32[32,384]{1,0:T(8,128)}, /*index=5*/f32[32,384]{1,0:T(8,128)}, f32[2560]{0:T(1024)}) custom-call(bf16[32,2944]{1,0:T(8,128)(2,1)S(1)} %pad_maximum_fusion.ours, bf16[32,2944]{1,0:T(8,128)(2,1)S(1)} %collective-permute-done.25.theirs, ...), custom_call_target="tpu_custom_call" | custom-call | flops 1000000000 | bytes 13000000 | tf_op jit(solution)/shard_map/finish/pallas_call | solution.py:632
  (56 shorter events, 14.4 us)
Async XLA Ops:
  0.6 32.0 %collective-permute-start.10 = (bf16[2560,384]{1,0:T(8,128)(2,1)}, bf16[2560,384]{1,0:T(8,128)(2,1)S(1)}, u32[]{:S(2)}, u32[]{:S(2)}) collective-permute-start(bf16[2560,384]{1,0:T(8,128)(2,1)} %w_own.1), channel_id=1, source_target_pairs={{0,1},{1,0},{2,3},{3,2},{4,5},{5,4},{6,7},{7,6},{8,9},{9,8},{10,11... | collective-permute-start | bytes 5898248 | tf_op jit(solution)/shard_map/ppermute | solution.py:664
  26.1 6.6 %collective-permute-start.9 = (bf16[384,512]{1,0:T(8,128)(2,1)S(1)}, bf16[384,512]{1,0:T(8,128)(2,1)S(1)}, u32[]{:S(2)}, u32[]{:S(2)}) collective-permute-start(bf16[384,512]{1,0:T(8,128)(2,1)S(1)} %get-tuple-element.97), channel_id=1, source_target_pairs={{0,1},{1,0},{2,3},{3,2},{4,5},{5,4},{6,7},{7,6},{8,9},{9,8},{10,11... | collective-permute-start | bytes 1179656 | tf_op jit(solution)/shard_map/ppermute | solution.py:664
  26.6 10.2 %collective-permute-start.8 = (bf16[64,384]{1,0:T(8,128)(2,1)S(1)}, bf16[64,384]{1,0:T(8,128)(2,1)S(1)}, u32[]{:S(2)}, u32[]{:S(2)}) collective-permute-start(bf16[64,384]{1,0:T(8,128)(2,1)S(1)} %get-tuple-element.95), channel_id=1, source_target_pairs={{0,24},{8,0},{16,8},{24,16},{32,56},{40,32},{48,40},{56,48},{64,88... | collective-permute-start | bytes 147464 | tf_op jit(solution)/shard_map/ppermute | solution.py:672
  30.8 6.1 %collective-permute-start.7 = (bf16[64,384]{1,0:T(8,128)(2,1)S(1)}, bf16[64,384]{1,0:T(8,128)(2,1)S(1)}, u32[]{:S(2)}, u32[]{:S(2)}) collective-permute-start(bf16[64,384]{1,0:T(8,128)(2,1)S(1)} %get-tuple-element.95), channel_id=1, source_target_pairs={{0,8},{8,16},{16,24},{24,0},{32,40},{40,48},{48,56},{56,32},{64,72... | collective-permute-start | bytes 147464 | tf_op jit(solution)/shard_map/ppermute | solution.py:672
  30.8 6.1 %collective-permute-start.6 = (bf16[64,384]{1,0:T(8,128)(2,1)S(1)}, bf16[64,384]{1,0:T(8,128)(2,1)S(1)}, u32[]{:S(2)}, u32[]{:S(2)}) collective-permute-start(bf16[64,384]{1,0:T(8,128)(2,1)S(1)} %get-tuple-element.95), channel_id=1, source_target_pairs={{0,16},{8,24},{16,0},{24,8},{32,48},{40,56},{48,32},{56,40},{64,80... | collective-permute-start | bytes 147464 | tf_op jit(solution)/shard_map/ppermute | solution.py:672
  36.8 12.2 %collective-permute-start.14 = (bf16[64,2560]{1,0:T(8,128)(2,1)S(1)}, bf16[64,2560]{1,0:T(8,128)(2,1)S(1)}, u32[]{:S(2)}, u32[]{:S(2)}) collective-permute-start(bf16[64,2560]{1,0:T(8,128)(2,1)S(1)} %get-tuple-element.103), channel_id=1, source_target_pairs={{0,2},{1,3},{2,4},{3,5},{4,6},{5,7},{6,0},{7,1},{8,10},{9,11},{10,... | collective-permute-start | bytes 983048 | tf_op jit(solution)/shard_map/ppermute | solution.py:668
  38.4 10.7 %collective-permute-start.15 = (bf16[64,2560]{1,0:T(8,128)(2,1)S(1)}, bf16[64,2560]{1,0:T(8,128)(2,1)S(1)}, u32[]{:S(2)}, u32[]{:S(2)}) collective-permute-start(bf16[64,2560]{1,0:T(8,128)(2,1)S(1)} %get-tuple-element.104), channel_id=1, source_target_pairs={{0,6},{1,7},{2,0},{3,1},{4,2},{5,3},{6,4},{7,5},{8,14},{9,15},{10,... | collective-permute-start | bytes 983048 | tf_op jit(solution)/shard_map/ppermute | solution.py:668
  40.2 5.3 %collective-permute-start.13 = (bf16[64,384]{1,0:T(8,128)(2,1)S(1)}, bf16[64,384]{1,0:T(8,128)(2,1)S(1)}, u32[]{:S(2)}, u32[]{:S(2)}) collective-permute-start(bf16[64,384]{1,0:T(8,128)(2,1)S(1)} %reduce-precision_convert_fusion.2), channel_id=1, source_target_pairs={{0,96},{8,104},{16,112},{24,120},{32,0},{40,8},{48,16},{56,24},{64... | collective-permute-start | bytes 147464 | tf_op jit(solution)/shard_map/ppermute | solution.py:676
  43.2 5.8 %collective-permute-start.12 = (bf16[64,384]{1,0:T(8,128)(2,1)S(1)}, bf16[64,384]{1,0:T(8,128)(2,1)S(1)}, u32[]{:S(2)}, u32[]{:S(2)}) collective-permute-start(bf16[64,384]{1,0:T(8,128)(2,1)S(1)} %reduce-precision_convert_fusion.2), channel_id=1, source_target_pairs={{0,32},{8,40},{16,48},{24,56},{32,64},{40,72},{48,80},{56,88},{64,... | collective-permute-start | bytes 147464 | tf_op jit(solution)/shard_map/ppermute | solution.py:676
  43.2 5.8 %collective-permute-start.11 = (bf16[64,384]{1,0:T(8,128)(2,1)S(1)}, bf16[64,384]{1,0:T(8,128)(2,1)S(1)}, u32[]{:S(2)}, u32[]{:S(2)}) collective-permute-start(bf16[64,384]{1,0:T(8,128)(2,1)S(1)} %reduce-precision_convert_fusion.2), channel_id=1, source_target_pairs={{0,64},{8,72},{16,80},{24,88},{32,96},{40,104},{48,112},{56,120},{... | collective-permute-start | bytes 147464 | tf_op jit(solution)/shard_map/ppermute | solution.py:676
  53.6 7.7 %collective-permute-start.17 = (bf16[8,2944]{1,0:T(8,128)(2,1)}, bf16[8,2944]{1,0:T(8,128)(2,1)S(1)}, u32[]{:S(2)}, u32[]{:S(2)}) collective-permute-start(bf16[8,2944]{1,0:T(8,128)(2,1)} %get-tuple-element.114), channel_id=1, source_target_pairs={{0,4},{1,5},{2,6},{3,7},{4,0},{5,1},{6,2},{7,3},{8,12},{9,13},{10,... | collective-permute-start | bytes 141320 | tf_op jit(solution)/shard_map/ppermute | solution.py:668
  55.5 5.9 %collective-permute-start.18 = (bf16[8,2944]{1,0:T(8,128)(2,1)}, bf16[8,2944]{1,0:T(8,128)(2,1)}, u32[]{:S(2)}, u32[]{:S(2)}) collective-permute-start(bf16[8,2944]{1,0:T(8,128)(2,1)} %get-tuple-element.115), channel_id=1, source_target_pairs={{0,2},{1,3},{2,4},{3,5},{4,6},{5,7},{6,0},{7,1},{8,10},{9,11},{10,... | collective-permute-start | bytes 141320 | tf_op jit(solution)/shard_map/ppermute | solution.py:668
  56.0 5.3 %collective-permute-start.19 = (bf16[8,2944]{1,0:T(8,128)(2,1)}, bf16[8,2944]{1,0:T(8,128)(2,1)}, u32[]{:S(2)}, u32[]{:S(2)}) collective-permute-start(bf16[8,2944]{1,0:T(8,128)(2,1)} %get-tuple-element.116), channel_id=1, source_target_pairs={{0,6},{1,7},{2,0},{3,1},{4,2},{5,3},{6,4},{7,5},{8,14},{9,15},{10,... | collective-permute-start | bytes 141320 | tf_op jit(solution)/shard_map/ppermute | solution.py:668
  62.8 24.8 %collective-permute-start.20 = (bf16[128,2560]{1,0:T(8,128)(2,1)}, bf16[128,2560]{1,0:T(8,128)(2,1)}, u32[]{:S(2)}, u32[]{:S(2)}) collective-permute-start(bf16[128,2560]{1,0:T(8,128)(2,1)} %get-tuple-element.133), channel_id=1, source_target_pairs={{0,2},{1,3},{2,4},{3,5},{4,6},{5,7},{6,0},{7,1},{8,10},{9,11},{10,... | collective-permute-start | bytes 1966088 | tf_op jit(solution)/shard_map/ppermute | solution.py:668
  63.0 24.6 %collective-permute-start.21 = (bf16[128,2560]{1,0:T(8,128)(2,1)}, bf16[128,2560]{1,0:T(8,128)(2,1)}, u32[]{:S(2)}, u32[]{:S(2)}) collective-permute-start(bf16[128,2560]{1,0:T(8,128)(2,1)} %get-tuple-element.134), channel_id=1, source_target_pairs={{0,6},{1,7},{2,0},{3,1},{4,2},{5,3},{6,4},{7,5},{8,14},{9,15},{10,... | collective-permute-start | bytes 1966088 | tf_op jit(solution)/shard_map/ppermute | solution.py:668
  66.1 7.9 %collective-permute-start = (bf16[8,2688]{1,0:T(8,128)(2,1)}, bf16[8,2688]{1,0:T(8,128)(2,1)S(1)}, u32[]{:S(2)}, u32[]{:S(2)}) collective-permute-start(bf16[8,2688]{1,0:T(8,128)(2,1)} %get-tuple-element.207), channel_id=1, source_target_pairs={{0,16},{8,24},{16,0},{24,8},{32,48},{40,56},{48,32},{56,40},{64,80... | collective-permute-start | bytes 129032 | tf_op jit(solution)/shard_map/while/body/ppermute | solution.py:672
  67.7 6.3 %collective-permute-start.2 = (bf16[8,2688]{1,0:T(8,128)(2,1)}, bf16[8,2688]{1,0:T(8,128)(2,1)S(1)}, u32[]{:S(2)}, u32[]{:S(2)}) collective-permute-start(bf16[8,2688]{1,0:T(8,128)(2,1)} %get-tuple-element.207), channel_id=1, source_target_pairs={{0,24},{8,0},{16,8},{24,16},{32,56},{40,32},{48,40},{56,48},{64,88... | collective-permute-start | bytes 129032 | tf_op jit(solution)/shard_map/while/body/ppermute | solution.py:672
  70.9 5.6 %collective-permute-start.1 = (bf16[8,2688]{1,0:T(8,128)(2,1)}, bf16[8,2688]{1,0:T(8,128)(2,1)}, u32[]{:S(2)}, u32[]{:S(2)}) collective-permute-start(bf16[8,2688]{1,0:T(8,128)(2,1)} %get-tuple-element.207), channel_id=1, source_target_pairs={{0,8},{8,16},{16,24},{24,0},{32,40},{40,48},{48,56},{56,32},{64,72... | collective-permute-start | bytes 129032 | tf_op jit(solution)/shard_map/while/body/ppermute | solution.py:672
  77.3 4.8 %collective-permute-start.5 = (bf16[8,2688]{1,0:T(8,128)(2,1)S(1)}, bf16[8,2688]{1,0:T(8,128)(2,1)S(1)}, u32[]{:S(2)}, u32[]{:S(2)}) collective-permute-start(bf16[8,2688]{1,0:T(8,128)(2,1)S(1)} %reduce-precision_convert_fusion.5), channel_id=1, source_target_pairs={{0,96},{8,104},{16,112},{24,120},{32,0},{40,8},{48,16},{56,24},{64... | collective-permute-start | bytes 129032 | tf_op jit(solution)/shard_map/while/body/ppermute | solution.py:676
  80.4 5.7 %collective-permute-start.4 = (bf16[8,2688]{1,0:T(8,128)(2,1)S(1)}, bf16[8,2688]{1,0:T(8,128)(2,1)S(1)}, u32[]{:S(2)}, u32[]{:S(2)}) collective-permute-start(bf16[8,2688]{1,0:T(8,128)(2,1)S(1)} %reduce-precision_convert_fusion.5), channel_id=1, source_target_pairs={{0,32},{8,40},{16,48},{24,56},{32,64},{40,72},{48,80},{56,88},{64,... | collective-permute-start | bytes 129032 | tf_op jit(solution)/shard_map/while/body/ppermute | solution.py:676
  80.4 5.7 %collective-permute-start.3 = (bf16[8,2688]{1,0:T(8,128)(2,1)S(1)}, bf16[8,2688]{1,0:T(8,128)(2,1)}, u32[]{:S(2)}, u32[]{:S(2)}) collective-permute-start(bf16[8,2688]{1,0:T(8,128)(2,1)S(1)} %reduce-precision_convert_fusion.5), channel_id=1, source_target_pairs={{0,64},{8,72},{16,80},{24,88},{32,96},{40,104},{48,112},{56,120},{... | collective-permute-start | bytes 129032 | tf_op jit(solution)/shard_map/while/body/ppermute | solution.py:676
  87.6 6.6 %collective-permute-start.24 = (bf16[8,2688]{1,0:T(8,128)(2,1)}, bf16[8,2688]{1,0:T(8,128)(2,1)S(1)}, u32[]{:S(2)}, u32[]{:S(2)}) collective-permute-start(bf16[8,2688]{1,0:T(8,128)(2,1)} %get-tuple-element.135), channel_id=1, source_target_pairs={{0,2},{1,3},{2,4},{3,5},{4,6},{5,7},{6,0},{7,1},{8,10},{9,11},{10,... | collective-permute-start | bytes 129032 | tf_op jit(solution)/shard_map/ppermute | solution.py:668
  87.7 6.5 %collective-permute-start.23 = (bf16[8,2688]{1,0:T(8,128)(2,1)}, bf16[8,2688]{1,0:T(8,128)(2,1)S(1)}, u32[]{:S(2)}, u32[]{:S(2)}) collective-permute-start(bf16[8,2688]{1,0:T(8,128)(2,1)} %get-tuple-element.135), channel_id=1, source_target_pairs={{0,6},{1,7},{2,0},{3,1},{4,2},{5,3},{6,4},{7,5},{8,14},{9,15},{10,... | collective-permute-start | bytes 129032 | tf_op jit(solution)/shard_map/ppermute | solution.py:668
  90.9 5.7 %collective-permute-start.22 = (bf16[8,2688]{1,0:T(8,128)(2,1)}, bf16[8,2688]{1,0:T(8,128)(2,1)S(1)}, u32[]{:S(2)}, u32[]{:S(2)}) collective-permute-start(bf16[8,2688]{1,0:T(8,128)(2,1)} %get-tuple-element.135), channel_id=1, source_target_pairs={{0,4},{1,5},{2,6},{3,7},{4,0},{5,1},{6,2},{7,3},{8,12},{9,13},{10,... | collective-permute-start | bytes 129032 | tf_op jit(solution)/shard_map/ppermute | solution.py:668
  (8 other events, 69.1 us)

commit v4 on v3

--- a/solution.py
+++ b/solution.py
@@ -124,7 +124,7 @@
     )
     for copy in small:
         copy.start()
-    for copy in copies[:4]:
+    for copy in copies[:2]:
         copy.start()
     index = lax.axis_index("tensor")
     rows_copy = pltpu.make_async_copy(
@@ -146,6 +146,8 @@
         span = pl.ds(part * 128, 128)
         gain_row[:, span] = gain_flat[span].reshape(1, 128)
     copies[0].wait()
+    for copy in copies[2:4]:
+        copy.start()
 
     @pl.loop(0, half // LN_ROWS)
     def _(step):
@@ -475,7 +477,7 @@
         scratch_shapes=[pltpu.VMEM((RANK, WIDE), F32)],
         compiler_params=pltpu.CompilerParams(vmem_limit_bytes=16 * 2**20),
         cost_estimate=pl.CostEstimate(
-            flops=5 * 10**8, bytes_accessed=5 * 10**6, transcendentals=0
+            flops=10**6, bytes_accessed=10**5, transcendentals=0
         ),
     )(left, gain_rows, mats_out, mats_value)
 
@@ -577,62 +579,57 @@
 def finish_kernel(
     ours, theirs, left, mats_out, mats_value,
     err_out, err_value, share_out, share_value, ortho_out, ortho_value, gain_out,
-    sums, ortho_parts, right,
+    sums, ortho_parts, right, err_v, sems,
 ):
     chip, core = place()
-    step = pl.program_id(0)
-    lanes = pl.ds(pl.multiple_of(step * 1280, 1280), 1280)
-
-    @pl.when(step == 0)
-    def _():
-        for side, source in ((core, ours), (1 - core, theirs)):
-            wide = source[...].astype(F32)
-            for block in range(4):
-                offset = lax.rem(chip + block, 4) * 8
-                rows = pl.ds(pl.multiple_of(side * RANK + offset, 8), 8)
-                sums[rows, pl.ds(0, SENT)] = wide[block * 8 : block * 8 + 8, :SENT]
-            rows = pl.ds(pl.multiple_of(side * RANK, RANK), RANK)
-            sums[rows, pl.ds(SENT, 128)] = wide[:, SENT : SENT + 128] + wide[:, SENT + 128 :]
-        for part in range(D // 128):
-            row = sums[pl.ds(part // 3 * 8 + part % 3, 1), pl.ds(D, 128)]
-            gain_out[pl.ds(part * 128, 128)] = row.reshape(128)
-        for side, scaled in enumerate((ortho_out, ortho_value)):
-            span = pl.ds(side * RANK, RANK)
-            inverse = sums[span, pl.ds(SENT, 128)][:, :RANK]
-            ortho = dot_split(inverse, left[span, :])
-            scaled[...] = ortho * math.sqrt(HH)
-            high, low = split2(ortho)
-            parts = jnp.concatenate([high, low, high, jnp.zeros_like(high)], axis=0)
-            ortho_parts[side] = parts.T
-
-    for side, (mats, err) in enumerate(((mats_out, err_out), (mats_value, err_value))):
+    for side, source in ((core, ours), (1 - core, theirs)):
+        wide = source[...].astype(F32)
+        for block in range(4):
+            offset = lax.rem(chip + block, 4) * 8
+            rows = pl.ds(pl.multiple_of(side * RANK + offset, 8), 8)
+            sums[rows, pl.ds(0, SENT)] = wide[block * 8 : block * 8 + 8, :SENT]
+        rows = pl.ds(pl.multiple_of(side * RANK, RANK), RANK)
+        sums[rows, pl.ds(SENT, 128)] = wide[:, SENT : SENT + 128] + wide[:, SENT + 128 :]
+    copies = []
+    for side, (mats, err, scaled) in enumerate(
+        ((mats_out, err_out, ortho_out), (mats_value, err_value, ortho_value))
+    ):
         span = pl.ds(side * RANK, RANK)
         inverse = sums[span, pl.ds(SENT, 128)][:, :RANK]
-        rows = dot_split(inverse, sums[span, lanes]) * (1.0 / WORKERS)
-        right[span, lanes] = rows
-        high, low = split2(rows)
-        parts = jnp.concatenate([high, high, low, jnp.zeros_like(high)], axis=0)
-        err[0] = mats[...].astype(F32) - dot(ortho_parts[side], parts)
-
-    @pl.when(step == 1)
-    def _():
-        index = chip * 2 + core
-        window = right[:, pl.ds(pl.multiple_of(index * 5 // 2 * 128, 128), 512)]
-        window = jnp.where(lax.rem(index, 2) == 1, pltpu.roll(window, 512 - 64, 1), window)
-        share_out[...] = window[:RANK, : D // 8]
-        share_value[...] = window[RANK:, : D // 8]
+        ortho = dot_split(inverse, left[span, :])
+        scaled[...] = ortho * math.sqrt(HH)
+        high, low = split2(ortho)
+        parts = jnp.concatenate([high, low, high, jnp.zeros_like(high)], axis=0)
+        ortho_parts[side] = parts.T
+        for step in range(STEPS):
+            lanes = pl.ds(step * TILE, TILE)
+            rows = dot_split(inverse, sums[span, lanes]) * (1.0 / WORKERS)
+            right[span, lanes] = rows
+            high, low = split2(rows)
+            parts = jnp.concatenate([high, high, low, jnp.zeros_like(high)], axis=0)
+            err_v[side, :, lanes] = mats[:, lanes].astype(F32) - dot(ortho_parts[side], parts)
+            copy = pltpu.make_async_copy(
+                err_v.at[side, :, lanes], err.at[0, :, lanes], sems.at[side * STEPS + step]
+            )
+            copy.start()
+            copies.append(copy)
+    for part in range(D // 128):
+        row = sums[pl.ds(part // 3 * 8 + part % 3, 1), pl.ds(D, 128)]
+        gain_out[pl.ds(part * 128, 128)] = row.reshape(128)
+    index = chip * 2 + core
+    window = right[:, pl.ds(pl.multiple_of(index * 5 // 2 * 128, 128), 512)]
+    window = jnp.where(lax.rem(index, 2) == 1, pltpu.roll(window, 512 - 64, 1), window)
+    share_out[...] = window[:RANK, : D // 8]
+    share_value[...] = window[RANK:, : D // 8]
+    for copy in copies:
+        copy.wait()
 
 
 def finish(ours, theirs, left, mats_out, mats_value):
-    whole = pl.BlockSpec((RANK, WIDE), lambda n: (0, 0))
-    mats = pl.BlockSpec((COLS, 1280), lambda n: (0, n))
-    err = pl.BlockSpec((1, COLS, 1280), lambda n: (0, 0, n))
-    share = pl.BlockSpec((RANK, D // 8), lambda n: (0, 0))
-    ortho = pl.BlockSpec((RANK, COLS), lambda n: (0, 0))
+    vmem = pl.BlockSpec(memory_space=pltpu.VMEM)
     return pl.pallas_call(
         finish_kernel,
         name="finish",
-        grid=(2,),
         out_shape=(
             jax.ShapeDtypeStruct((1, COLS, D), F32),
             jax.ShapeDtypeStruct((1, COLS, D), F32),
@@ -642,18 +639,16 @@
             jax.ShapeDtypeStruct((RANK, COLS), F32),
             jax.ShapeDtypeStruct((D,), F32),
         ),
-        in_specs=[
-            whole, whole, pl.BlockSpec((2 * RANK, COLS), lambda n: (0, 0)), mats, mats,
-        ],
-        out_specs=(
-            err, err, share, share, ortho, ortho, pl.BlockSpec((D,), lambda n: (0,)),
-        ),
+        in_specs=[vmem] * 5,
+        out_specs=(ANY, ANY, vmem, vmem, vmem, vmem, vmem),
         scratch_shapes=[
             pltpu.VMEM((2 * RANK, WIDE), F32),
             pltpu.VMEM((2, COLS, 4 * RANK), BF16),
             pltpu.VMEM((2 * RANK, WIDE), F32),
+            pltpu.VMEM((2, COLS, D), F32),
+            pltpu.SemaphoreType.DMA((2 * STEPS,)),
         ],
-        compiler_params=pltpu.CompilerParams(vmem_limit_bytes=20 * 2**20),
+        compiler_params=pltpu.CompilerParams(vmem_limit_bytes=24 * 2**20),
         cost_estimate=pl.CostEstimate(
             flops=1 * 10**9, bytes_accessed=13 * 10**6, transcendentals=0
         ),
@@ -703,10 +698,13 @@
     here, after, before, far_after, far_before = branch(own_half, received_half, w_value, w_other)
     left, far_after, far_before = ring_sum(left_term, to_z, (far_after, far_before))
     far_after, far_before = to_x(far_after, 1), to_x(far_before, 3)
-    left, far_after, far_before = ring_sum(rounded(left), to_y, (far_after, far_before))
+    left = ring_sum(rounded(left), to_y)
 
     ours, theirs = right_terms(left, gain_rows, mats_out, mats_value)
-    own, to_opposite, to_after, to_before = merge(ours, to_core(theirs))
+    theirs, far_after, far_before = lax.optimization_barrier(
+        (to_core(theirs), far_after, far_before)
+    )
+    own, to_opposite, to_after, to_before = merge(ours, theirs)
     next_after, next_before = relay(after, before, far_after, far_before)
     parts = to_x(to_opposite, 2), to_x(to_after, 1), to_x(to_before, 3)
     parts, next_after, next_before = lax.optimization_barrier((parts, next_after, next_before))

time: 106 us -> 104 us (0.981)
  waiting for transfers between devices: 15.7 us -> 14.5 us
    ppermute x6, waiting for transfers between devices: 7.82 us -> 4.09 us  [to_y(): lax.ppermute(value, 'dp', [(i, (i // 4 + hops) % 4 * 4 + i % 4) for i in...]
    ppermute x10, waiting for transfers between devices: 2.49 us -> 5.04 us  [to_x(): lax.ppermute(value, 'tensor', [(i, (i // 2 + hops) % 4 * 2 + i % 2) for i...]
  transfers between devices with their start and end apart: 26 -> 26, of which waited for: 7 -> 9; matrix products, arithmetic and copies ran while one was open for 3% -> 3% of each run, Pallas kernels for 36% -> 38%
where the time goes in v4:
time: 104 us; the launch traced here: 102 us
  Pallas kernels  45.9 us (44%)
  starting transfers between devices  36.7 us (35%)
  waiting for transfers between devices  14.5 us (14%)
  other arithmetic  3.12 us (3%)
    pallas_call x1, Pallas kernels, front(): pl.pallas_call(front_kernel, name='front', out_shape=(jax.ShapeDtypeStruc...  25.1 us
    ppermute x10, starting transfers between devices, to_x(): lax.ppermute(value, 'tensor', [(i, (i // 2 + hops) % 4 * 2 + i % 2) for i...  15.6 us
    ppermute x6, starting transfers between devices, to_z(): lax.ppermute(value, 'dp', [(i, i // 4 * 4 + (i + hops) % 4) for i in rang...  10.9 us
    ppermute x6, starting transfers between devices, to_y(): lax.ppermute(value, 'dp', [(i, (i // 4 + hops) % 4 * 4 + i % 4) for i in...  9.29 us
    ppermute x10, waiting for transfers between devices, to_x(): lax.ppermute(value, 'tensor', [(i, (i // 2 + hops) % 4 * 2 + i % 2) for i...  5.04 us
    pallas_call x1, Pallas kernels, finish(): pl.pallas_call(finish_kernel, name='finish', out_shape=(jax.ShapeDtypeStr...  4.67 us
    pallas_call x1, Pallas kernels, branch(): pl.pallas_call(branch_kernel, name='branch', grid=(2,), out_shape=[jax.Sh...  4.13 us
    ppermute x6, waiting for transfers between devices, to_y(): lax.ppermute(value, 'dp', [(i, (i // 4 + hops) % 4 * 4 + i % 4) for i in...  4.09 us
  transfers between devices with their start and end apart: 26, of which 9 were waited for; matrix products, arithmetic and copies ran while one was open for 3% of the time, Pallas kernels for 38%

profile of v4, /device:TPU:0, one launch (start us, length us, event | category | flops | bytes accessed | tf_op | source)
XLA Modules:
  0.0 102.0 jit_solution(329344913030122344)
XLA Ops:
  0.7 25.1 %front.1 = (bf16[384,2560]{1,0:T(8,128)(2,1)S(1)}, bf16[384,2560]{1,0:T(8,128)(2,1)S(1)}, bf16[64,384]{1,0:T(8,128)(2,1)S(1)}, bf16[384,512]{1,0:T(8,128)(2,1)S(...) custom-call(s32[2]{0:T(128)} %codes.1, ...), custom_call_target="tpu_custom_call" | custom-call | flops 11000000512 | bytes 32000000 | tf_op jit(solution)/shard_map/front/pallas_call | solution.py:249
  26.4 4.1 %collective-permute-start.8 = (bf16[64,384]{1,0:T(8,128)(2,1)S(1)}, bf16[64,384]{1,0:T(8,128)(2,1)S(1)}, u32[]{:S(2)}, u32[]{:S(2)}) collective-permute-start(bf16[64,384]{1,0:T(8,128)(2,1)S(1)} %get-tuple-element.96), channel_id=1, source_target_pairs={{0,24},{8,0},{16,8},{24,16},{32,56},{40,32},{48,40},{56,48},{64,88... | collective-permute-start | bytes 147464 | tf_op jit(solution)/shard_map/ppermute | solution.py:667
  30.6 1.9 %collective-permute-start.6 = (bf16[64,384]{1,0:T(8,128)(2,1)S(1)}, bf16[64,384]{1,0:T(8,128)(2,1)S(1)}, u32[]{:S(2)}, u32[]{:S(2)}) collective-permute-start(bf16[64,384]{1,0:T(8,128)(2,1)S(1)} %get-tuple-element.96), channel_id=1, source_target_pairs={{0,16},{8,24},{16,0},{24,8},{32,48},{40,56},{48,32},{56,40},{64,80... | collective-permute-start | bytes 147464 | tf_op jit(solution)/shard_map/ppermute | solution.py:667
  32.4 4.1 %branch.1 = (bf16[128,2560]{1,0:T(8,128)(2,1)S(1)}, bf16[128,2560]{1,0:T(8,128)(2,1)S(1)}, bf16[128,2560]{1,0:T(8,128)(2,1)S(1)}, bf16[64,2560]{1,0:T(8,128)(2,1)S(1)}, bf16[64,2560]{1,0:T(8,128)(2,1)S(1)}) custom-call(bf16[384,512]{1,0:T(8,128)(2,1)S(1)} %get-tuple-element.97.own_half, bf16[384,512]{1,0:T(8,128)(2,1)S(1)} %collective-permute-done.9.other_half, ...), custom_call_target="tpu_custom_call" | custom-call | flops 2000000000 | bytes 7000000 | tf_op jit(solution)/shard_map/branch/pallas_call | solution.py:322
  36.7 3.1 %collective-permute-start.13 = (bf16[64,384]{1,0:T(8,128)(2,1)S(1)}, bf16[64,384]{1,0:T(8,128)(2,1)S(1)}, u32[]{:S(2)}, u32[]{:S(2)}) collective-permute-start(bf16[64,384]{1,0:T(8,128)(2,1)S(1)} %reduce-precision_convert_fusion.2), channel_id=1, source_target_pairs={{0,96},{8,104},{16,112},{24,120},{32,0},{40,8},{48,16},{56,24},{64... | collective-permute-start | bytes 147464 | tf_op jit(solution)/shard_map/ppermute | solution.py:671
  39.7 2.2 %collective-permute-start.11 = (bf16[64,384]{1,0:T(8,128)(2,1)S(1)}, bf16[64,384]{1,0:T(8,128)(2,1)S(1)}, u32[]{:S(2)}, u32[]{:S(2)}) collective-permute-start(bf16[64,384]{1,0:T(8,128)(2,1)S(1)} %reduce-precision_convert_fusion.2), channel_id=1, source_target_pairs={{0,64},{8,72},{16,80},{24,88},{32,96},{40,104},{48,112},{56,120},{... | collective-permute-start | bytes 147464 | tf_op jit(solution)/shard_map/ppermute | solution.py:671
  41.9 1.5 %collective-permute-start.15 = (bf16[64,2560]{1,0:T(8,128)(2,1)S(1)}, bf16[64,2560]{1,0:T(8,128)(2,1)S(1)}, u32[]{:S(2)}, u32[]{:S(2)}) collective-permute-start(bf16[64,2560]{1,0:T(8,128)(2,1)S(1)} %get-tuple-element.112), channel_id=1, source_target_pairs={{0,2},{1,3},{2,4},{3,5},{4,6},{5,7},{6,0},{7,1},{8,10},{9,11},{10,... | collective-permute-start | bytes 983048 | tf_op jit(solution)/shard_map/ppermute | solution.py:663
  43.5 1.7 %collective-permute-start.16 = (bf16[64,2560]{1,0:T(8,128)(2,1)S(1)}, bf16[64,2560]{1,0:T(8,128)(2,1)S(1)}, u32[]{:S(2)}, u32[]{:S(2)}) collective-permute-start(bf16[64,2560]{1,0:T(8,128)(2,1)S(1)} %get-tuple-element.113), channel_id=1, source_target_pairs={{0,6},{1,7},{2,0},{3,1},{4,2},{5,3},{6,4},{7,5},{8,14},{9,15},{10,... | collective-permute-start | bytes 983048 | tf_op jit(solution)/shard_map/ppermute | solution.py:663
  48.6 2.5 %collective-permute-done.15.far_after = bf16[64,2560]{1,0:T(8,128)(2,1)S(1)} collective-permute-done((bf16[64,2560]{1,0:T(8,128)(2,1)S(1)}, bf16[64,2560]{1,0:T(8,128)(2,1)S(1)}, u32[]{:S(2)}, u32[]{:S(2)}) %collective-permute-start.15) | collective-permute-done | bytes 327712 | tf_op jit(solution)/shard_map/ppermute | solution.py:663
  52.1 2.6 %collective-permute-start.17 = (bf16[8,2944]{1,0:T(8,128)(2,1)}, bf16[8,2944]{1,0:T(8,128)(2,1)S(1)}, u32[]{:S(2)}, u32[]{:S(2)}) collective-permute-start(bf16[8,2944]{1,0:T(8,128)(2,1)} %get-tuple-element.116), channel_id=1, source_target_pairs={{0,4},{1,5},{2,6},{3,7},{4,0},{5,1},{6,2},{7,3},{8,12},{9,13},{10,... | collective-permute-start | bytes 141320 | tf_op jit(solution)/shard_map/ppermute | solution.py:663
  55.8 2.2 %collective-permute-start.19 = (bf16[8,2944]{1,0:T(8,128)(2,1)}, bf16[8,2944]{1,0:T(8,128)(2,1)}, u32[]{:S(2)}, u32[]{:S(2)}) collective-permute-start(bf16[8,2944]{1,0:T(8,128)(2,1)} %get-tuple-element.118), channel_id=1, source_target_pairs={{0,6},{1,7},{2,0},{3,1},{4,2},{5,3},{6,4},{7,5},{8,14},{9,15},{10,... | collective-permute-start | bytes 141320 | tf_op jit(solution)/shard_map/ppermute | solution.py:663
  57.9 2.6 %relay.1 = (bf16[128,2560]{1,0:T(8,128)(2,1)}, bf16[128,2560]{1,0:T(8,128)(2,1)}) custom-call(bf16[128,2560]{1,0:T(8,128)(2,1)} %copy-done.2, bf16[128,2560]{1,0:T(8,128)(2,1)} %copy-done.3, bf16[64,2560]{1,0:T(8,128)(2,1)} %copy-done.4, bf16[64,2560]{1,0:T(8,128)(2,1)} %copy-done.5), custom_call_target="tpu_custom_call" | custom-call | flops 1000000 | bytes 4000000 | tf_op jit(solution)/shard_map/relay/pallas_call | solution.py:353
  62.1 3.2 %collective-permute-start.21 = (bf16[128,2560]{1,0:T(8,128)(2,1)}, bf16[128,2560]{1,0:T(8,128)(2,1)}, u32[]{:S(2)}, u32[]{:S(2)}) collective-permute-start(bf16[128,2560]{1,0:T(8,128)(2,1)} %get-tuple-element.136), channel_id=1, source_target_pairs={{0,6},{1,7},{2,0},{3,1},{4,2},{5,3},{6,4},{7,5},{8,14},{9,15},{10,... | collective-permute-start | bytes 1966088 | tf_op jit(solution)/shard_map/ppermute | solution.py:663
  65.3 20.5 %while.12 = (s32[]{:T(128)}, bf16[8,2688]{1,0:T(8,128)(2,1)}, bf16[32,256]{1,0:T(8,128)(2,1)S(1)}, s32[]{:T(128)}, s32[]{:T(128)}) while((s32[]{:T(128)}, bf16[8,2688]{1,0:T(8,128)(2,1)}, bf16[32,256]{1,0:T(8,128)(2,1)S(1)}, s32[]{:T(128)}, s32[]{:T(128)}) %tuple.42), condition=%wide.region_1.2_spmd, body=%wide.region_0.1_spmd.sunk | while | flops 5387074 | bytes 4495341 | solution.py:722
  65.3 2.0 %collective-permute-start = (bf16[8,2688]{1,0:T(8,128)(2,1)}, bf16[8,2688]{1,0:T(8,128)(2,1)S(1)}, u32[]{:S(2)}, u32[]{:S(2)}) collective-permute-start(bf16[8,2688]{1,0:T(8,128)(2,1)} %get-tuple-element.209), channel_id=1, source_target_pairs={{0,16},{8,24},{16,0},{24,8},{32,48},{40,56},{48,32},{56,40},{64,80... | collective-permute-start | bytes 129032 | tf_op jit(solution)/shard_map/while/body/ppermute | solution.py:667
  67.3 2.9 %collective-permute-start.2 = (bf16[8,2688]{1,0:T(8,128)(2,1)}, bf16[8,2688]{1,0:T(8,128)(2,1)S(1)}, u32[]{:S(2)}, u32[]{:S(2)}) collective-permute-start(bf16[8,2688]{1,0:T(8,128)(2,1)} %get-tuple-element.209), channel_id=1, source_target_pairs={{0,24},{8,0},{16,8},{24,16},{32,56},{40,32},{48,40},{56,48},{64,88... | collective-permute-start | bytes 129032 | tf_op jit(solution)/shard_map/while/body/ppermute | solution.py:667
  70.8 2.4 %factor.1 = bf16[32,256]{1,0:T(8,128)(2,1)S(1)} custom-call(bf16[32,256]{1,0:T(8,128)(2,1)} %copy.29.parts), custom_call_target="tpu_custom_call" | custom-call | flops 5000000 | bytes 3000000 | tf_op jit(solution)/shard_map/while/body/factor/pallas_call | solution.py:569
  73.2 2.5 %collective-permute-done.1 = bf16[8,2688]{1,0:T(8,128)(2,1)} collective-permute-done((bf16[8,2688]{1,0:T(8,128)(2,1)}, bf16[8,2688]{1,0:T(8,128)(2,1)}, u32[]{:S(2)}, u32[]{:S(2)}) %collective-permute-start.1) | collective-permute-done | bytes 43040 | tf_op jit(solution)/shard_map/while/body/ppermute | solution.py:667
  78.7 1.9 %collective-permute-start.3 = (bf16[8,2688]{1,0:T(8,128)(2,1)S(1)}, bf16[8,2688]{1,0:T(8,128)(2,1)}, u32[]{:S(2)}, u32[]{:S(2)}) collective-permute-start(bf16[8,2688]{1,0:T(8,128)(2,1)S(1)} %reduce-precision_convert_fusion.5), channel_id=1, source_target_pairs={{0,64},{8,72},{16,80},{24,88},{32,96},{40,104},{48,112},{56,120},{... | collective-permute-start | bytes 129032 | tf_op jit(solution)/shard_map/while/body/ppermute | solution.py:671
  80.7 2.5 %collective-permute-done.4 = bf16[8,2688]{1,0:T(8,128)(2,1)S(1)} collective-permute-done((bf16[8,2688]{1,0:T(8,128)(2,1)S(1)}, bf16[8,2688]{1,0:T(8,128)(2,1)S(1)}, u32[]{:S(2)}, u32[]{:S(2)}) %collective-permute-start.4) | collective-permute-done | bytes 43040 | tf_op jit(solution)/shard_map/while/body/ppermute | solution.py:671
  85.8 3.2 %collective-permute-start.23 = (bf16[8,2688]{1,0:T(8,128)(2,1)}, bf16[8,2688]{1,0:T(8,128)(2,1)S(1)}, u32[]{:S(2)}, u32[]{:S(2)}) collective-permute-start(bf16[8,2688]{1,0:T(8,128)(2,1)} %get-tuple-element.137), channel_id=1, source_target_pairs={{0,6},{1,7},{2,0},{3,1},{4,2},{5,3},{6,4},{7,5},{8,14},{9,15},{10,... | collective-permute-start | bytes 129032 | tf_op jit(solution)/shard_map/ppermute | solution.py:663
  89.1 3.3 %norm_back.1 = bf16[128,2560]{1,0:T(8,128)(2,1)} custom-call(bf16[128,2560]{1,0:T(8,128)(2,1)S(1)} %get-tuple-element.138.hidden, f32[1,2560]{1,0:T(1,128)S(1)} %get-tuple-element.139.gain, bf16[128,2560]{1,0:T(8,128)(2,1)S(1)} %get-tuple-element.140.here, bf16[128,2560]{1,0:T(8,128)(2,1)} %collective-permute-done.20.after, ...), custom_call_target="tpu_custom_call" | custom-call | flops 5000000 | bytes 1000000 | tf_op jit(solution)/shard_map/norm_back/pallas_call | solution.py:405
  92.3 2.5 %collective-permute-done.22 = bf16[8,2688]{1,0:T(8,128)(2,1)S(1)} collective-permute-done((bf16[8,2688]{1,0:T(8,128)(2,1)}, bf16[8,2688]{1,0:T(8,128)(2,1)S(1)}, u32[]{:S(2)}, u32[]{:S(2)}) %collective-permute-start.22) | collective-permute-done | bytes 43040 | tf_op jit(solution)/shard_map/ppermute | solution.py:663
  97.1 4.7 %finish.1 = (f32[1,384,2560]{2,1,0:T(8,128)}, f32[1,384,2560]{2,1,0:T(8,128)}, f32[32,320]{1,0:T(8,128)}, f32[32,320]{1,0:T(8,128)}, f32[32,384]{1,0:T(8,128)}, /*index=5*/f32[32,384]{1,0:T(8,128)}, f32[2560]{0:T(1024)}) custom-call(bf16[32,2944]{1,0:T(8,128)(2,1)S(1)} %pad_maximum_fusion.ours, bf16[32,2944]{1,0:T(8,128)(2,1)S(1)} %collective-permute-done.25.theirs, ...), custom_call_target="tpu_custom_call" | custom-call | flops 1000000000 | bytes 13000000 | tf_op jit(solution)/shard_map/finish/pallas_call | solution.py:630
  (56 shorter events, 16.1 us)
Async XLA Ops:
  0.6 31.8 %collective-permute-start.10 = (bf16[2560,384]{1,0:T(8,128)(2,1)}, bf16[2560,384]{1,0:T(8,128)(2,1)S(1)}, u32[]{:S(2)}, u32[]{:S(2)}) collective-permute-start(bf16[2560,384]{1,0:T(8,128)(2,1)} %w_own.1), channel_id=1, source_target_pairs={{0,1},{1,0},{2,3},{3,2},{4,5},{5,4},{6,7},{7,6},{8,9},{9,8},{10,11... | collective-permute-start | bytes 5898248 | tf_op jit(solution)/shard_map/ppermute | solution.py:659
  25.9 6.6 %collective-permute-start.9 = (bf16[384,512]{1,0:T(8,128)(2,1)S(1)}, bf16[384,512]{1,0:T(8,128)(2,1)S(1)}, u32[]{:S(2)}, u32[]{:S(2)}) collective-permute-start(bf16[384,512]{1,0:T(8,128)(2,1)S(1)} %get-tuple-element.98), channel_id=1, source_target_pairs={{0,1},{1,0},{2,3},{3,2},{4,5},{5,4},{6,7},{7,6},{8,9},{9,8},{10,11... | collective-permute-start | bytes 1179656 | tf_op jit(solution)/shard_map/ppermute | solution.py:659
  26.4 10.2 %collective-permute-start.8 = (bf16[64,384]{1,0:T(8,128)(2,1)S(1)}, bf16[64,384]{1,0:T(8,128)(2,1)S(1)}, u32[]{:S(2)}, u32[]{:S(2)}) collective-permute-start(bf16[64,384]{1,0:T(8,128)(2,1)S(1)} %get-tuple-element.96), channel_id=1, source_target_pairs={{0,24},{8,0},{16,8},{24,16},{32,56},{40,32},{48,40},{56,48},{64,88... | collective-permute-start | bytes 147464 | tf_op jit(solution)/shard_map/ppermute | solution.py:667
  30.6 6.1 %collective-permute-start.7 = (bf16[64,384]{1,0:T(8,128)(2,1)S(1)}, bf16[64,384]{1,0:T(8,128)(2,1)S(1)}, u32[]{:S(2)}, u32[]{:S(2)}) collective-permute-start(bf16[64,384]{1,0:T(8,128)(2,1)S(1)} %get-tuple-element.96), channel_id=1, source_target_pairs={{0,8},{8,16},{16,24},{24,0},{32,40},{40,48},{48,56},{56,32},{64,72... | collective-permute-start | bytes 147464 | tf_op jit(solution)/shard_map/ppermute | solution.py:667
  30.6 6.1 %collective-permute-start.6 = (bf16[64,384]{1,0:T(8,128)(2,1)S(1)}, bf16[64,384]{1,0:T(8,128)(2,1)S(1)}, u32[]{:S(2)}, u32[]{:S(2)}) collective-permute-start(bf16[64,384]{1,0:T(8,128)(2,1)S(1)} %get-tuple-element.96), channel_id=1, source_target_pairs={{0,16},{8,24},{16,0},{24,8},{32,48},{40,56},{48,32},{56,40},{64,80... | collective-permute-start | bytes 147464 | tf_op jit(solution)/shard_map/ppermute | solution.py:667
  36.7 8.5 %collective-permute-start.13 = (bf16[64,384]{1,0:T(8,128)(2,1)S(1)}, bf16[64,384]{1,0:T(8,128)(2,1)S(1)}, u32[]{:S(2)}, u32[]{:S(2)}) collective-permute-start(bf16[64,384]{1,0:T(8,128)(2,1)S(1)} %reduce-precision_convert_fusion.2), channel_id=1, source_target_pairs={{0,96},{8,104},{16,112},{24,120},{32,0},{40,8},{48,16},{56,24},{64... | collective-permute-start | bytes 147464 | tf_op jit(solution)/shard_map/ppermute | solution.py:671
  39.7 5.8 %collective-permute-start.12 = (bf16[64,384]{1,0:T(8,128)(2,1)S(1)}, bf16[64,384]{1,0:T(8,128)(2,1)S(1)}, u32[]{:S(2)}, u32[]{:S(2)}) collective-permute-start(bf16[64,384]{1,0:T(8,128)(2,1)S(1)} %reduce-precision_convert_fusion.2), channel_id=1, source_target_pairs={{0,32},{8,40},{16,48},{24,56},{32,64},{40,72},{48,80},{56,88},{64,... | collective-permute-start | bytes 147464 | tf_op jit(solution)/shard_map/ppermute | solution.py:671
  39.7 5.8 %collective-permute-start.11 = (bf16[64,384]{1,0:T(8,128)(2,1)S(1)}, bf16[64,384]{1,0:T(8,128)(2,1)S(1)}, u32[]{:S(2)}, u32[]{:S(2)}) collective-permute-start(bf16[64,384]{1,0:T(8,128)(2,1)S(1)} %reduce-precision_convert_fusion.2), channel_id=1, source_target_pairs={{0,64},{8,72},{16,80},{24,88},{32,96},{40,104},{48,112},{56,120},{... | collective-permute-start | bytes 147464 | tf_op jit(solution)/shard_map/ppermute | solution.py:671
  41.9 9.2 %collective-permute-start.15 = (bf16[64,2560]{1,0:T(8,128)(2,1)S(1)}, bf16[64,2560]{1,0:T(8,128)(2,1)S(1)}, u32[]{:S(2)}, u32[]{:S(2)}) collective-permute-start(bf16[64,2560]{1,0:T(8,128)(2,1)S(1)} %get-tuple-element.112), channel_id=1, source_target_pairs={{0,2},{1,3},{2,4},{3,5},{4,6},{5,7},{6,0},{7,1},{8,10},{9,11},{10,... | collective-permute-start | bytes 983048 | tf_op jit(solution)/shard_map/ppermute | solution.py:663
  43.5 7.7 %collective-permute-start.16 = (bf16[64,2560]{1,0:T(8,128)(2,1)S(1)}, bf16[64,2560]{1,0:T(8,128)(2,1)S(1)}, u32[]{:S(2)}, u32[]{:S(2)}) collective-permute-start(bf16[64,2560]{1,0:T(8,128)(2,1)S(1)} %get-tuple-element.113), channel_id=1, source_target_pairs={{0,6},{1,7},{2,0},{3,1},{4,2},{5,3},{6,4},{7,5},{8,14},{9,15},{10,... | collective-permute-start | bytes 983048 | tf_op jit(solution)/shard_map/ppermute | solution.py:663
  52.1 8.5 %collective-permute-start.17 = (bf16[8,2944]{1,0:T(8,128)(2,1)}, bf16[8,2944]{1,0:T(8,128)(2,1)S(1)}, u32[]{:S(2)}, u32[]{:S(2)}) collective-permute-start(bf16[8,2944]{1,0:T(8,128)(2,1)} %get-tuple-element.116), channel_id=1, source_target_pairs={{0,4},{1,5},{2,6},{3,7},{4,0},{5,1},{6,2},{7,3},{8,12},{9,13},{10,... | collective-permute-start | bytes 141320 | tf_op jit(solution)/shard_map/ppermute | solution.py:663
  54.7 5.9 %collective-permute-start.18 = (bf16[8,2944]{1,0:T(8,128)(2,1)}, bf16[8,2944]{1,0:T(8,128)(2,1)}, u32[]{:S(2)}, u32[]{:S(2)}) collective-permute-start(bf16[8,2944]{1,0:T(8,128)(2,1)} %get-tuple-element.117), channel_id=1, source_target_pairs={{0,2},{1,3},{2,4},{3,5},{4,6},{5,7},{6,0},{7,1},{8,10},{9,11},{10,... | collective-permute-start | bytes 141320 | tf_op jit(solution)/shard_map/ppermute | solution.py:663
  55.8 4.8 %collective-permute-start.19 = (bf16[8,2944]{1,0:T(8,128)(2,1)}, bf16[8,2944]{1,0:T(8,128)(2,1)}, u32[]{:S(2)}, u32[]{:S(2)}) collective-permute-start(bf16[8,2944]{1,0:T(8,128)(2,1)} %get-tuple-element.118), channel_id=1, source_target_pairs={{0,6},{1,7},{2,0},{3,1},{4,2},{5,3},{6,4},{7,5},{8,14},{9,15},{10,... | collective-permute-start | bytes 141320 | tf_op jit(solution)/shard_map/ppermute | solution.py:663
  62.1 23.7 %collective-permute-start.20 = (bf16[128,2560]{1,0:T(8,128)(2,1)}, bf16[128,2560]{1,0:T(8,128)(2,1)}, u32[]{:S(2)}, u32[]{:S(2)}) collective-permute-start(bf16[128,2560]{1,0:T(8,128)(2,1)} %get-tuple-element.135), channel_id=1, source_target_pairs={{0,2},{1,3},{2,4},{3,5},{4,6},{5,7},{6,0},{7,1},{8,10},{9,11},{10,... | collective-permute-start | bytes 1966088 | tf_op jit(solution)/shard_map/ppermute | solution.py:663
  62.1 23.7 %collective-permute-start.21 = (bf16[128,2560]{1,0:T(8,128)(2,1)}, bf16[128,2560]{1,0:T(8,128)(2,1)}, u32[]{:S(2)}, u32[]{:S(2)}) collective-permute-start(bf16[128,2560]{1,0:T(8,128)(2,1)} %get-tuple-element.136), channel_id=1, source_target_pairs={{0,6},{1,7},{2,0},{3,1},{4,2},{5,3},{6,4},{7,5},{8,14},{9,15},{10,... | collective-permute-start | bytes 1966088 | tf_op jit(solution)/shard_map/ppermute | solution.py:663
  65.3 7.9 %collective-permute-start = (bf16[8,2688]{1,0:T(8,128)(2,1)}, bf16[8,2688]{1,0:T(8,128)(2,1)S(1)}, u32[]{:S(2)}, u32[]{:S(2)}) collective-permute-start(bf16[8,2688]{1,0:T(8,128)(2,1)} %get-tuple-element.209), channel_id=1, source_target_pairs={{0,16},{8,24},{16,0},{24,8},{32,48},{40,56},{48,32},{56,40},{64,80... | collective-permute-start | bytes 129032 | tf_op jit(solution)/shard_map/while/body/ppermute | solution.py:667
  67.3 6.0 %collective-permute-start.2 = (bf16[8,2688]{1,0:T(8,128)(2,1)}, bf16[8,2688]{1,0:T(8,128)(2,1)S(1)}, u32[]{:S(2)}, u32[]{:S(2)}) collective-permute-start(bf16[8,2688]{1,0:T(8,128)(2,1)} %get-tuple-element.209), channel_id=1, source_target_pairs={{0,24},{8,0},{16,8},{24,16},{32,56},{40,32},{48,40},{56,48},{64,88... | collective-permute-start | bytes 129032 | tf_op jit(solution)/shard_map/while/body/ppermute | solution.py:667
  70.2 5.6 %collective-permute-start.1 = (bf16[8,2688]{1,0:T(8,128)(2,1)}, bf16[8,2688]{1,0:T(8,128)(2,1)}, u32[]{:S(2)}, u32[]{:S(2)}) collective-permute-start(bf16[8,2688]{1,0:T(8,128)(2,1)} %get-tuple-element.209), channel_id=1, source_target_pairs={{0,8},{8,16},{16,24},{24,0},{32,40},{40,48},{48,56},{56,32},{64,72... | collective-permute-start | bytes 129032 | tf_op jit(solution)/shard_map/while/body/ppermute | solution.py:667
  76.6 4.1 %collective-permute-start.5 = (bf16[8,2688]{1,0:T(8,128)(2,1)S(1)}, bf16[8,2688]{1,0:T(8,128)(2,1)S(1)}, u32[]{:S(2)}, u32[]{:S(2)}) collective-permute-start(bf16[8,2688]{1,0:T(8,128)(2,1)S(1)} %reduce-precision_convert_fusion.5), channel_id=1, source_target_pairs={{0,96},{8,104},{16,112},{24,120},{32,0},{40,8},{48,16},{56,24},{64... | collective-permute-start | bytes 129032 | tf_op jit(solution)/shard_map/while/body/ppermute | solution.py:671
  78.0 5.2 %collective-permute-start.4 = (bf16[8,2688]{1,0:T(8,128)(2,1)S(1)}, bf16[8,2688]{1,0:T(8,128)(2,1)S(1)}, u32[]{:S(2)}, u32[]{:S(2)}) collective-permute-start(bf16[8,2688]{1,0:T(8,128)(2,1)S(1)} %reduce-precision_convert_fusion.5), channel_id=1, source_target_pairs={{0,32},{8,40},{16,48},{24,56},{32,64},{40,72},{48,80},{56,88},{64,... | collective-permute-start | bytes 129032 | tf_op jit(solution)/shard_map/while/body/ppermute | solution.py:671
  78.7 5.6 %collective-permute-start.3 = (bf16[8,2688]{1,0:T(8,128)(2,1)S(1)}, bf16[8,2688]{1,0:T(8,128)(2,1)}, u32[]{:S(2)}, u32[]{:S(2)}) collective-permute-start(bf16[8,2688]{1,0:T(8,128)(2,1)S(1)} %reduce-precision_convert_fusion.5), channel_id=1, source_target_pairs={{0,64},{8,72},{16,80},{24,88},{32,96},{40,104},{48,112},{56,120},{... | collective-permute-start | bytes 129032 | tf_op jit(solution)/shard_map/while/body/ppermute | solution.py:671
  85.8 6.6 %collective-permute-start.24 = (bf16[8,2688]{1,0:T(8,128)(2,1)}, bf16[8,2688]{1,0:T(8,128)(2,1)S(1)}, u32[]{:S(2)}, u32[]{:S(2)}) collective-permute-start(bf16[8,2688]{1,0:T(8,128)(2,1)} %get-tuple-element.137), channel_id=1, source_target_pairs={{0,2},{1,3},{2,4},{3,5},{4,6},{5,7},{6,0},{7,1},{8,10},{9,11},{10,... | collective-permute-start | bytes 129032 | tf_op jit(solution)/shard_map/ppermute | solution.py:663
  85.8 6.5 %collective-permute-start.23 = (bf16[8,2688]{1,0:T(8,128)(2,1)}, bf16[8,2688]{1,0:T(8,128)(2,1)S(1)}, u32[]{:S(2)}, u32[]{:S(2)}) collective-permute-start(bf16[8,2688]{1,0:T(8,128)(2,1)} %get-tuple-element.137), channel_id=1, source_target_pairs={{0,6},{1,7},{2,0},{3,1},{4,2},{5,3},{6,4},{7,5},{8,14},{9,15},{10,... | collective-permute-start | bytes 129032 | tf_op jit(solution)/shard_map/ppermute | solution.py:663
  89.1 5.7 %collective-permute-start.22 = (bf16[8,2688]{1,0:T(8,128)(2,1)}, bf16[8,2688]{1,0:T(8,128)(2,1)S(1)}, u32[]{:S(2)}, u32[]{:S(2)}) collective-permute-start(bf16[8,2688]{1,0:T(8,128)(2,1)} %get-tuple-element.137), channel_id=1, source_target_pairs={{0,4},{1,5},{2,6},{3,7},{4,0},{5,1},{6,2},{7,3},{8,12},{9,13},{10,... | collective-permute-start | bytes 129032 | tf_op jit(solution)/shard_map/ppermute | solution.py:663
  (8 other events, 56.8 us)
